TPU v7x, 32 devices: a whole 2x2x4 slice. The times are simulated.
32 devices in a mesh: rep: 4 (over y, core), shard: 8 (over z, x).
Axes of the slice: x: 2, y: 2, z: 4, core: 2. Of those that a mesh axis runs over, the one named last changes fastest.
Arguments:
- tokens: bfloat16 [32768, 1024], P(('rep', 'shard')), may hold values from -6 to 6
- norm_gain_one: bfloat16 [1024], P('shard'), may hold values from 0.099609375 to 1.8984375
- in_weight: bfloat16 [1024, 3072], P('shard'), may hold values from -0.1875 to 0.1875
- conv_weight: bfloat16 [3, 1024], P(None, 'shard'), may hold values from -3.5 to 3.5
- out_weight: bfloat16 [1024, 1024], P(None, 'shard'), may hold values from -0.1875 to 0.1875
- norm_gain_two: bfloat16 [1024], P('shard'), may hold values from 0.099609375 to 1.8984375
- gate_weight: bfloat16 [1024, 4608], P('shard'), may hold values from -0.1875 to 0.1875
- up_weight: bfloat16 [1024, 4608], P('shard'), may hold values from -0.1875 to 0.1875
- down_weight: bfloat16 [4608, 1024], P(None, 'shard'), may hold values from -0.1875 to 0.1875
- cotangent: bfloat16 [32768, 1024], P(('rep', 'shard')), may hold values from -6 to 6
Outputs:
- block_out: bfloat16 [32768, 1024], P(('rep', 'shard'))
- tokens_grad: bfloat16 [32768, 1024], P(('rep', 'shard'))
- gain_one_grad: float32 [1024], P('shard')
- in_grad: float32 [1024, 3072], P('shard')
- conv_grad: float32 [3, 1024], P(None, 'shard')
- out_grad: float32 [1024, 1024], P(None, 'shard')
- gain_two_grad: float32 [1024], P('shard')
- gate_grad: float32 [1024, 4608], P('shard')
- up_grad: float32 [1024, 4608], P('shard')
- down_grad: float32 [4608, 1024], P(None, 'shard')
All inputs are finite; a program needn't handle non-finite values.
Results may differ from a plain program's by a relative error of at most 0.018.
Values may be sent and summed in bfloat16 or wider, within the bound.
No kernel may reach another device: no remote copies, remote signals or barrier semaphores. Data moves between devices by JAX's collectives and lax.ppermute only.
A program may use at most 256 MiB of HBM per device.

v0:
```python
import jax
import jax.numpy as jnp
from jax import lax
from jax.sharding import PartitionSpec as P

SEQ = 512


EPSILON = 1e-05


def plain_dot(left, right):
    return jnp.dot(left, right, preferred_element_type=jnp.float32)


def rows_dot(left, right):
    return lax.dot_general(
        left, right, (((1,), (1,)), ((), ())), preferred_element_type=jnp.float32
    )


def cols_dot(left, right):
    return lax.dot_general(
        left, right, (((0,), (0,)), ((), ())), preferred_element_type=jnp.float32
    )


def shift_back(values, steps):
    return jnp.pad(values[:, : values.shape[1] - steps], ((0, 0), (steps, 0), (0, 0)))


def shift_ahead(values, steps):
    return jnp.pad(values[:, steps:], ((0, 0), (0, steps), (0, 0)))


def norm_back(grad_norm, values, inv_rms, gain):
    scaled = grad_norm * gain
    grad_values = inv_rms * (
        scaled - values * inv_rms * inv_rms * jnp.mean(scaled * values, -1, keepdims=True)
    )
    grad_gain = jnp.sum(grad_norm * values * inv_rms, 0)
    return (grad_values, grad_gain)


def shards(
    tokens,
    norm_gain_one,
    in_weight,
    conv_weight,
    out_weight,
    norm_gain_two,
    gate_weight,
    up_weight,
    down_weight,
    cotangent,
):
    model_width = tokens.shape[1]
    gathered = (
        lax.all_gather(norm_gain_one, "shard", axis=0, tiled=True),
        lax.all_gather(in_weight, "shard", axis=0, tiled=True),
        lax.all_gather(conv_weight, "shard", axis=1, tiled=True),
        lax.all_gather(out_weight, "shard", axis=1, tiled=True),
        lax.all_gather(norm_gain_two, "shard", axis=0, tiled=True),
        lax.all_gather(gate_weight, "shard", axis=0, tiled=True),
        lax.all_gather(up_weight, "shard", axis=0, tiled=True),
        lax.all_gather(down_weight, "shard", axis=1, tiled=True),
    )
    gain_one, weight_in, weight_conv, weight_out, gain_two, weight_gate, weight_up, weight_down = (
        gathered
    )
    taps = weight_conv.astype(jnp.float32)
    gain_one_f = gain_one.astype(jnp.float32)
    gain_two_f = gain_two.astype(jnp.float32)
    tokens_f = tokens.astype(jnp.float32)
    inv_one = lax.rsqrt(jnp.mean(tokens_f * tokens_f, -1, keepdims=True) + EPSILON)
    normed_one = (tokens_f * inv_one * gain_one_f).astype(jnp.bfloat16)
    projected = plain_dot(normed_one, weight_in)
    b_part = projected[:, :model_width]
    c_part = projected[:, model_width : 2 * model_width]
    x_part = projected[:, 2 * model_width :]
    mixed_in = (b_part * x_part).reshape(-1, SEQ, model_width)
    conv_out = (
        taps[0] * shift_back(mixed_in, 2) + taps[1] * shift_back(mixed_in, 1) + taps[2] * mixed_in
    ).reshape(-1, model_width)
    gated = (c_part * conv_out).astype(jnp.bfloat16)
    middle = tokens_f + plain_dot(gated, weight_out)
    inv_two = lax.rsqrt(jnp.mean(middle * middle, -1, keepdims=True) + EPSILON)
    normed_two = (middle * inv_two * gain_two_f).astype(jnp.bfloat16)
    gate_pre = plain_dot(normed_two, weight_gate)
    up_proj = plain_dot(normed_two, weight_up)
    sigma_gate = jax.nn.sigmoid(gate_pre)
    silu_gate = gate_pre * sigma_gate
    hidden = (silu_gate * up_proj).astype(jnp.bfloat16)
    block_out = (middle + plain_dot(hidden, weight_down)).astype(jnp.bfloat16)
    regathered = (
        lax.all_gather(norm_gain_one, "shard", axis=0, tiled=True),
        lax.all_gather(in_weight, "shard", axis=0, tiled=True),
        lax.all_gather(conv_weight, "shard", axis=1, tiled=True),
        lax.all_gather(out_weight, "shard", axis=1, tiled=True),
        lax.all_gather(norm_gain_two, "shard", axis=0, tiled=True),
        lax.all_gather(gate_weight, "shard", axis=0, tiled=True),
        lax.all_gather(up_weight, "shard", axis=0, tiled=True),
        lax.all_gather(down_weight, "shard", axis=1, tiled=True),
    )
    back_in, back_out, back_gate, back_up, back_down = (
        regathered[1],
        regathered[3],
        regathered[5],
        regathered[6],
        regathered[7],
    )
    cot_f = cotangent.astype(jnp.float32)
    down_local = cols_dot(hidden, cotangent)
    hidden_grad = rows_dot(cotangent, back_down)
    gate_back = (hidden_grad * up_proj * sigma_gate * (1.0 + gate_pre * (1.0 - sigma_gate))).astype(
        jnp.bfloat16
    )
    up_back = (hidden_grad * silu_gate).astype(jnp.bfloat16)
    gate_local = cols_dot(normed_two, gate_back)
    up_local = cols_dot(normed_two, up_back)
    normed_two_grad = rows_dot(gate_back, back_gate) + rows_dot(up_back, back_up)
    middle_norm_grad, gain_two_local = norm_back(normed_two_grad, middle, inv_two, gain_two_f)
    middle_grad = cot_f + middle_norm_grad
    branch_back = middle_grad.astype(jnp.bfloat16)
    out_local = cols_dot(gated, branch_back)
    gated_grad = rows_dot(branch_back, back_out)
    c_grad = gated_grad * conv_out
    conv_grad_in = (gated_grad * c_part).reshape(-1, SEQ, model_width)
    conv_local = jnp.stack(
        [
            jnp.sum(conv_grad_in * shift_back(mixed_in, 2), (0, 1)),
            jnp.sum(conv_grad_in * shift_back(mixed_in, 1), (0, 1)),
            jnp.sum(conv_grad_in * mixed_in, (0, 1)),
        ],
        0,
    )
    mixed_grad = (
        taps[2] * conv_grad_in
        + taps[1] * shift_ahead(conv_grad_in, 1)
        + taps[0] * shift_ahead(conv_grad_in, 2)
    ).reshape(-1, model_width)
    projected_back = jnp.concatenate([mixed_grad * x_part, c_grad, mixed_grad * b_part], 1).astype(
        jnp.bfloat16
    )
    in_local = cols_dot(normed_one, projected_back)
    normed_one_grad = rows_dot(projected_back, back_in)
    tokens_norm_grad, gain_one_local = norm_back(normed_one_grad, tokens_f, inv_one, gain_one_f)
    tokens_grad = (middle_grad + tokens_norm_grad).astype(jnp.bfloat16)
    group_sums = None
    totals = None
    group_sums = (
        lax.psum_scatter(
            gain_one_local.astype(jnp.bfloat16), "shard", scatter_dimension=0, tiled=True
        ).astype(jnp.float32),
        lax.psum_scatter(
            in_local.astype(jnp.bfloat16), "shard", scatter_dimension=0, tiled=True
        ).astype(jnp.float32),
        lax.psum_scatter(
            conv_local.astype(jnp.bfloat16), "shard", scatter_dimension=1, tiled=True
        ).astype(jnp.float32),
        lax.psum_scatter(
            out_local.astype(jnp.bfloat16), "shard", scatter_dimension=1, tiled=True
        ).astype(jnp.float32),
        lax.psum_scatter(
            gain_two_local.astype(jnp.bfloat16), "shard", scatter_dimension=0, tiled=True
        ).astype(jnp.float32),
        lax.psum_scatter(
            gate_local.astype(jnp.bfloat16), "shard", scatter_dimension=0, tiled=True
        ).astype(jnp.float32),
        lax.psum_scatter(
            up_local.astype(jnp.bfloat16), "shard", scatter_dimension=0, tiled=True
        ).astype(jnp.float32),
        lax.psum_scatter(
            down_local.astype(jnp.bfloat16), "shard", scatter_dimension=1, tiled=True
        ).astype(jnp.float32),
    )
    totals = (
        lax.psum(group_sums[0].astype(jnp.bfloat16), "rep").astype(jnp.float32),
        lax.psum(group_sums[1].astype(jnp.bfloat16), "rep").astype(jnp.float32),
        lax.psum(group_sums[2].astype(jnp.bfloat16), "rep").astype(jnp.float32),
        lax.psum(group_sums[3].astype(jnp.bfloat16), "rep").astype(jnp.float32),
        lax.psum(group_sums[4].astype(jnp.bfloat16), "rep").astype(jnp.float32),
        lax.psum(group_sums[5].astype(jnp.bfloat16), "rep").astype(jnp.float32),
        lax.psum(group_sums[6].astype(jnp.bfloat16), "rep").astype(jnp.float32),
        lax.psum(group_sums[7].astype(jnp.bfloat16), "rep").astype(jnp.float32),
    )
    return (
        block_out,
        tokens_grad,
        totals[0],
        totals[1],
        totals[2],
        totals[3],
        totals[4],
        totals[5],
        totals[6],
        totals[7],
    )


def solution(mesh):
    in_specs = (
        P(("rep", "shard"), None),
        P("shard"),
        P("shard", None),
        P(None, "shard"),
        P(None, "shard"),
        P("shard"),
        P("shard", None),
        P("shard", None),
        P(None, "shard"),
        P(("rep", "shard"), None),
    )
    out_specs = (
        P(("rep", "shard"), None),
        P(("rep", "shard"), None),
        P("shard"),
        P("shard", None),
        P(None, "shard"),
        P(None, "shard"),
        P("shard"),
        P("shard", None),
        P("shard", None),
        P(None, "shard"),
    )
    return jax.shard_map(shards, mesh=mesh, in_specs=in_specs, out_specs=out_specs, check_vma=False)
```

profile of v0, /device:TPU:0, one launch (start us, length us, event | category | flops | bytes accessed | tf_op | source)
XLA Modules:
  0.0 1512.0 jit_solution(7165202146490991137)
XLA Ops:
  13.5 22.4 %all-gather = bf16[8,1,128]{2,1,0:T(2,128)(2,1)S(1)} all-gather(bf16[1,1,128]{2,1,0:T(2,128)(2,1)S(1)} %bitcast.87), channel_id=1, replica_groups=mesh['rep'=4,'shard'=8] {'shard'}, dimensions={0}, use_global_device_ids=true | all-gather | bytes 2304 | tf_op jit(solution)/shard_map/all_gather | solution.py:59
  35.9 16.5 %all-gather.1 = bf16[8,1,128]{2,1,0:T(2,128)(2,1)S(1)} all-gather(bf16[1,1,128]{2,1,0:T(2,128)(2,1)S(1)} %bitcast.88), channel_id=1, replica_groups=mesh['rep'=4,'shard'=8] {'shard'}, dimensions={0}, use_global_device_ids=true | all-gather | bytes 2304 | tf_op jit(solution)/shard_map/all_gather | solution.py:63
  56.3 18.5 %all_gather.31 = bf16[3,1024]{1,0:T(4,128)(2,1)S(1)} all-gather(bf16[3,128]{1,0:T(4,128)(2,1)S(1)} %copy-done.31), channel_id=1, replica_groups=mesh['rep'=4,'shard'=8] {'shard'}, dimensions={1}, use_global_device_ids=true | all-gather | bytes 6912 | tf_op jit(solution)/shard_map/all_gather | solution.py:61
  75.4 36.7 %all-gather.8.cloned.1.call-done = bf16[1024,3072]{1,0:T(8,128)(2,1)} async-done(((bf16[128,3072]{1,0:T(8,128)(2,1)}), bf16[1024,3072]{1,0:T(8,128)(2,1)}) %all-gather.8.cloned.1.call-update) | async-done | bytes 6291472 | tf_op jit(solution)/shard_map/all_gather | solution.py:60
  132.1 31.4 %all-gather.10.cloned.1.call-done = bf16[1024,1024]{1,0:T(8,128)(2,1)} async-done(((bf16[1024,128]{1,0:T(8,128)(2,1)}), bf16[1024,1024]{1,0:T(8,128)(2,1)}) %all-gather.10.cloned.1.call-update) | async-done | bytes 2097168 | tf_op jit(solution)/shard_map/all_gather | solution.py:62
  171.3 130.6 %all-gather.12.cloned.1.call-done = bf16[1024,4608]{1,0:T(8,128)(2,1)} async-done(((bf16[128,4608]{1,0:T(8,128)(2,1)}), bf16[1024,4608]{1,0:T(8,128)(2,1)}) %all-gather.12.cloned.1.call-update) | async-done | bytes 9437200 | tf_op jit(solution)/shard_map/all_gather | solution.py:64
  301.9 16.5 %fusion.27 = f32[1024,4608]{1,0:T(8,128)} fusion(bf16[1024,1024]{0,1:T(8,128)(2,1)S(1)} %multiply_convert_fusion.3, bf16[1024,4608]{1,0:T(8,128)(2,1)} %all-gather.12.cloned.1.call-done), kind=kOutput, calls=%fused_computation.63 | convolution fusion | flops 9663676416 | bytes 30408704 | tf_op jit(solution)/shard_map/dot_general | solution.py:13
  318.4 121.8 %all-gather.14.cloned.1.call-done = bf16[1024,4608]{1,0:T(8,128)(2,1)} async-done(((bf16[128,4608]{1,0:T(8,128)(2,1)}), bf16[1024,4608]{1,0:T(8,128)(2,1)}) %all-gather.14.cloned.1.call-update) | async-done | bytes 9437200 | tf_op jit(solution)/shard_map/all_gather | solution.py:65
  440.2 17.0 %fusion.28 = f32[1024,4608]{1,0:T(8,128)} fusion(bf16[1024,1024]{0,1:T(8,128)(2,1)} %copy-done.15, bf16[1024,4608]{1,0:T(8,128)(2,1)} %all-gather.14.cloned.1.call-done), kind=kOutput, calls=%fused_computation.64 | convolution fusion | flops 9663676416 | bytes 30408704 | tf_op jit(solution)/shard_map/dot_general | solution.py:13
  457.2 121.3 %all-gather.16.cloned.1.call-done = bf16[4608,1024]{1,0:T(8,128)(2,1)} async-done(((bf16[4608,128]{1,0:T(8,128)(2,1)}), bf16[4608,1024]{1,0:T(8,128)(2,1)}) %all-gather.16.cloned.1.call-update) | async-done | bytes 9437200 | tf_op jit(solution)/shard_map/all_gather | solution.py:66
  578.5 30.8 %multiply_convert_fusion = (bf16[1024,4608]{1,0:T(8,128)(2,1)}, bf16[1024,4608]{1,0:T(8,128)(2,1)}, bf16[1024,4608]{1,0:T(8,128)(2,1)}) fusion(f32[1024,4608]{1,0:T(8,128)} %fusion.27, f32[1024,4608]{1,0:T(8,128)} %fusion.28, bf16[1024,1024]{1,0:T(8,128)(2,1)S(1)} %copy-done.14, bf16[4608,1024]{1,0:T(8,128)(2,1)} %all-gather.16.cloned.1.call-done), kind=kOutput, calls=%fused_computation | convolution fusion | flops 9734455296 | bytes 77594624 | tf_op jit(solution)/shard_map/dot_general | solution.py:17
  609.4 14.2 fusion.29
  623.6 17.0 %multiply_reduce_fusion = (bf16[1024]{0:T(1024)(128)(2,1)}, f32[1024]{0:T(1024)S(1)}, f32[1024,1024]{0,1:T(8,128)S(1)}) fusion(f32[1024,1024]{0,1:T(8,128)S(1)} %copy-done.9, f32[1024]{0:T(1024)S(1)} %add_rsqrt_fusion, f32[1024]{0:T(1024)S(1)} %bitcast.80, f32[1024,1024]{0,1:T(8,128)S(1)} %fusion.29, bf16[1024,4608]{1,0:T(8,128)(2,1)} %get-tuple-element.47, ...), kind=kOutput, calls=%fused_computation.35 | convolution fusion | flops 9671014400 | bytes 31471616 | tf_op jit(solution)/shard_map/dot_general | solution.py:17
  651.6 16.0 %convolution_convert_fusion.2 = bf16[4608,1024]{1,0:T(8,128)(2,1)} fusion(bf16[1024,4608]{1,0:T(8,128)(2,1)} %get-tuple-element.49, bf16[1024,1024]{1,0:T(8,128)(2,1)S(1)} %copy-done.14), kind=kOutput, calls=%fused_computation.7 | convolution fusion | flops 9668395008 | bytes 20971520 | tf_op jit(solution)/shard_map/dot_general | solution.py:23
  725.2 17.3 %convolution_convert_fusion.1 = bf16[1024,4608]{1,0:T(8,128)(2,1)} fusion(bf16[1024,1024]{0,1:T(8,128)(2,1)} %copy-done.15, bf16[1024,4608]{1,0:T(8,128)(2,1)} %get-tuple-element.48), kind=kOutput, calls=%fused_computation.6 | convolution fusion | flops 9668395008 | bytes 20971520 | tf_op jit(solution)/shard_map/dot_general | solution.py:23
  742.5 16.4 %convolution_convert_fusion = bf16[1024,4608]{1,0:T(8,128)(2,1)} fusion(bf16[1024,1024]{0,1:T(8,128)(2,1)} %copy-done.15, bf16[1024,4608]{1,0:T(8,128)(2,1)} %get-tuple-element.47), kind=kOutput, calls=%fused_computation.5 | convolution fusion | flops 9668395008 | bytes 20971520 | tf_op jit(solution)/shard_map/dot_general | solution.py:23
  786.4 20.2 %all-reduce.6 = (bf16[1024]{0:T(1024)(128)(2,1)S(1)}, bf16[1024]{0:T(1024)(128)(2,1)S(1)}) all-reduce(bf16[1024]{0:T(1024)(128)(2,1)S(1)} %get-tuple-element.32, bf16[1024]{0:T(1024)(128)(2,1)S(1)} %copy-done.30), channel_id=2, replica_groups=mesh['rep'=4,'shard'=8] {'shard'}, use_global_device_ids=true, to_apply=%region_5.6.clone | all-reduce | flops 2048 | bytes 8192
  812.4 71.3 %reduce-scatter.23.cloned.1.call-done = bf16[128,4608]{1,0:T(8,128)(2,1)} async-done(((bf16[1024,4608]{1,0:T(8,128)(2,1)}), bf16[128,4608]{1,0:T(8,128)(2,1)}) %reduce-scatter.23.cloned.1.call-update) | async-done | bytes 1179664
  886.1 118.3 %reduce-scatter.13.cloned.1.call-done = bf16[128,3072]{1,0:T(8,128)(2,1)} async-done(((bf16[1024,3072]{1,0:T(8,128)(2,1)}), bf16[128,3072]{1,0:T(8,128)(2,1)}) %reduce-scatter.13.cloned.1.call-update) | async-done | bytes 786448 | tf_op jit(solution)/shard_map/reduce_scatter | solution.py:155
  1004.4 166.2 %reduce-scatter.15.cloned.1.call-done = bf16[128,4608]{1,0:T(8,128)(2,1)} async-done(((bf16[1024,4608]{1,0:T(8,128)(2,1)}), bf16[128,4608]{1,0:T(8,128)(2,1)}) %reduce-scatter.15.cloned.1.call-update) | async-done | bytes 1179664 | tf_op jit(solution)/shard_map/reduce_scatter | solution.py:167
  1170.6 166.0 %reduce-scatter.17.cloned.1.call-done = bf16[128,4608]{1,0:T(8,128)(2,1)} async-done(((bf16[1024,4608]{1,0:T(8,128)(2,1)}), bf16[128,4608]{1,0:T(8,128)(2,1)}) %reduce-scatter.17.cloned.1.call-update) | async-done | bytes 1179664 | tf_op jit(solution)/shard_map/reduce_scatter | solution.py:170
  1336.7 15.9 %add_convert_fusion = bf16[1024,1024]{0,1:T(8,128)(2,1)S(1)} fusion(f32[1024,1024]{0,1:T(8,128)} %copy-done.8, bf16[1024,4608]{1,0:T(8,128)(2,1)} %get-tuple-element.49, bf16[4608,1024]{1,0:T(8,128)(2,1)} %all-gather.16.cloned.1.call-done), kind=kOutput, calls=%fused_computation.42 | convolution fusion | flops 9665773568 | bytes 25165824 | tf_op jit(solution)/shard_map/dot_general | solution.py:13
  1355.2 45.8 %reduce-scatter.19.cloned.1.call-done = bf16[128,3]{1,0:T(8,128)(2,1)} async-done(((bf16[1024,3]{1,0:T(8,128)(2,1)}), bf16[128,3]{1,0:T(8,128)(2,1)}) %reduce-scatter.19.cloned.1.call-update) | async-done | bytes 784
  1409.0 87.3 %all-reduce.11.cloned.1.call-done = (bf16[128,3072]{1,0:T(8,128)(2,1)}, bf16[1024,128]{1,0:T(8,128)(2,1)}, bf16[128,4608]{1,0:T(8,128)(2,1)}, bf16[128,4608]{1,0:T(8,128)(2,1)}, bf16[4608,128]{1,0:T(8,128)(2,1)}) async-done(((bf16[128,3072]{1,0:T(8,128)(2,1)}, bf16[1024,128]{1,0:T(8,128)(2,1)}, bf16[128,4608]{1,0:T(8,128)(2,1)}, bf16[128,4608]{1,0:T(8,128)(2,1)}, bf16[4608,128]{1,0:T(8,128)(2,1)}), ...) | async-done | bytes 4587536 | tf_op jit(solution)/shard_map/psum | solution.py:179
  (154 shorter events, 160.9 us)
Async XLA Ops:
  7.2 104.9 %all-gather.8.cloned.1.call-start = ((), (), s32[]{:S(2)}) async-start(), calls=%async_computation.6 | async-start | bytes 7077888 | tf_op jit(solution)/shard_map/all_gather | solution.py:60
  7.9 28.0 %copy-start.33 = (bf16[128]{0:T(256)(128)(2,1)S(1)}, bf16[128]{0:T(256)(128)(2,1)}, u32[]{:S(2)}) copy-start(bf16[128]{0:T(256)(128)(2,1)} %param.15) | copy-start | bytes 772
  7.9 155.5 %all-gather.10.cloned.1.call-start = ((), (), s32[]{:S(2)}) async-start(), calls=%async_computation.7 | async-start | bytes 2359296 | tf_op jit(solution)/shard_map/all_gather | solution.py:62
  8.7 293.2 %all-gather.12.cloned.1.call-start = ((), (), s32[]{:S(2)}) async-start(), calls=%async_computation.8 | async-start | bytes 10616832 | tf_op jit(solution)/shard_map/all_gather | solution.py:64
  9.4 430.8 %all-gather.14.cloned.1.call-start = ((), (), s32[]{:S(2)}) async-start(), calls=%async_computation.9 | async-start | bytes 10616832 | tf_op jit(solution)/shard_map/all_gather | solution.py:65
  10.0 568.5 %all-gather.16.cloned.1.call-start = ((), (), s32[]{:S(2)}) async-start(), calls=%async_computation.10 | async-start | bytes 10616832 | tf_op jit(solution)/shard_map/all_gather | solution.py:66
  10.6 45.8 %copy-start.31 = (bf16[3,128]{1,0:T(4,128)(2,1)S(1)}, bf16[3,128]{1,0:T(4,128)(2,1)}, u32[]{:S(2)}) copy-start(bf16[3,128]{1,0:T(4,128)(2,1)} %param.13) | copy-start | bytes 2308
  10.6 800.0 %reduce-scatter.21.cloned.1.call-start = ((), (), s32[]{:S(2)}) async-start(), calls=%async_computation.15 | async-start | bytes 2359296
  13.5 107.9 %copy-start.6 = (bf16[1024,1024]{0,1:T(8,128)(2,1)}, bf16[1024,1024]{0,1:T(8,128)(2,1)S(1)}, u32[]{:S(2)}) copy-start(bf16[1024,1024]{0,1:T(8,128)(2,1)S(1)} %copy.29) | copy-start | bytes 6291460
  35.9 85.5 %copy-start.26 = (f32[8,1,128]{2,1,0:T(1,128)}, f32[8,1,128]{2,1,0:T(1,128)S(1)}, u32[]{:S(2)}) copy-start(f32[8,1,128]{2,1,0:T(1,128)S(1)} %convert_element_type.144) | copy-start | bytes 12292
  75.3 46.1 %copy-start.28 = (f32[1024]{0:T(1024)}, f32[1024]{0:T(1024)S(1)}, u32[]{:S(2)}) copy-start(f32[1024]{0:T(1024)S(1)} %add_rsqrt_fusion.1) | copy-start | bytes 12292
  75.3 47.5 %copy-start.20 = (f32[1,1024]{1,0:T(1,128)}, f32[1,1024]{1,0:T(1,128)S(1)}, u32[]{:S(2)}) copy-start(f32[1,1024]{1,0:T(1,128)S(1)} %get-tuple-element.52) | copy-start | bytes 12292
  75.4 47.5 %copy-start.22 = (f32[1,1024]{1,0:T(1,128)}, f32[1,1024]{1,0:T(1,128)S(1)}, u32[]{:S(2)}) copy-start(f32[1,1024]{1,0:T(1,128)S(1)} %get-tuple-element.53) | copy-start | bytes 12292
  75.4 47.5 %copy-start.24 = (f32[1,1024]{1,0:T(1,128)}, f32[1,1024]{1,0:T(1,128)S(1)}, u32[]{:S(2)}) copy-start(f32[1,1024]{1,0:T(1,128)S(1)} %get-tuple-element.54) | copy-start | bytes 12292
  171.3 130.6 %copy-start.15 = (bf16[1024,1024]{0,1:T(8,128)(2,1)}, bf16[1024,1024]{0,1:T(8,128)(2,1)S(1)}, u32[]{:S(2)}) copy-start(bf16[1024,1024]{0,1:T(8,128)(2,1)S(1)} %multiply_convert_fusion.3) | copy-start | bytes 6291460
  318.4 260.1 %copy-start.14 = (bf16[1024,1024]{1,0:T(8,128)(2,1)S(1)}, bf16[1024,1024]{1,0:T(8,128)(2,1)}, u32[]{:S(2)}) copy-start(bf16[1024,1024]{1,0:T(8,128)(2,1)} %param.19) | copy-start | bytes 6291460
  609.4 14.2 copy-start.9
  623.6 17.1 %copy-start.10 = (bf16[1024,1024]{0,1:T(8,128)(2,1)S(1)}, bf16[1024,1024]{0,1:T(8,128)(2,1)}, u32[]{:S(2)}) copy-start(bf16[1024,1024]{0,1:T(8,128)(2,1)} %copy.31) | copy-start | bytes 6291460
  651.5 232.2 %reduce-scatter.23.cloned.1.call-start = ((), (), s32[]{:S(2)}) async-start(), calls=%async_computation.16 | async-start | bytes 10616832
  680.3 324.1 %reduce-scatter.13.cloned.1.call-start = ((), (), s32[]{:S(2)}) async-start(), calls=%async_computation.11 | async-start | bytes 7077888 | tf_op jit(solution)/shard_map/reduce_scatter | solution.py:155
  725.1 445.5 %reduce-scatter.15.cloned.1.call-start = ((), (), s32[]{:S(2)}) async-start(), calls=%async_computation.12 | async-start | bytes 10616832 | tf_op jit(solution)/shard_map/reduce_scatter | solution.py:167
  742.5 594.1 %reduce-scatter.17.cloned.1.call-start = ((), (), s32[]{:S(2)}) async-start(), calls=%async_computation.13 | async-start | bytes 10616832 | tf_op jit(solution)/shard_map/reduce_scatter | solution.py:170
  758.9 642.0 %reduce-scatter.19.cloned.1.call-start = ((), (), s32[]{:S(2)}) async-start(), calls=%async_computation.14 | async-start | bytes 294912
  780.3 716.0 %all-reduce.11.cloned.1.call-start = ((), (), s32[]{:S(2)}) async-start(), calls=%async_computation.17 | async-start | bytes 9175040 | tf_op jit(solution)/shard_map/psum | solution.py:179
  (26 other events, 123.0 us)
Sparse Core Ops, SparseCore 0:
  10.2 101.8 all-gather.7
  114.2 49.2 all-gather.9
  165.6 136.2 all-gather.11
  303.9 136.2 all-gather.13
  442.1 136.3 all-gather.15
  651.6 65.8 reduce-scatter.20
  721.1 162.5 reduce-scatter.22
  887.3 117.0 reduce-scatter.12
  1008.0 162.5 reduce-scatter.14
  1174.0 162.5 reduce-scatter.16
  1340.5 60.3 reduce-scatter.18
  1404.6 91.6 all-reduce.10
where the time goes:
time: 1520 us; the launch traced here: 1510 us
  waiting for transfers between devices  1100 us (72%)
  matrix products  212 us (14%)
  blocking collectives  83.2 us (5%)
  local copies, waits for them, and re-layouts  52.8 us (3%)
  other arithmetic  47.7 us (3%)
  between operations  15.7 us (1%)
    reduce_scatter x1, waiting for transfers between devices, shards(): lax.psum_scatter(gate_local.astype(jnp.bfloat16), 'shard', scatter_dimens...  166 us
    reduce_scatter x1, waiting for transfers between devices, shards(): lax.psum_scatter(up_local.astype(jnp.bfloat16), 'shard', scatter_dimensio...  166 us
    all_gather x1, waiting for transfers between devices, shards(): lax.all_gather(gate_weight, 'shard', axis=0, tiled=True)  131 us
    all_gather x1, waiting for transfers between devices, shards(): lax.all_gather(up_weight, 'shard', axis=0, tiled=True)  122 us
    all_gather x1, waiting for transfers between devices, shards(): lax.all_gather(down_weight, 'shard', axis=1, tiled=True)  121 us
    unnamed x15, waiting for transfers between devices  120 us
    reduce_scatter x1, waiting for transfers between devices, shards(): lax.psum_scatter(in_local.astype(jnp.bfloat16), 'shard', scatter_dimensio...  118 us
    psum x1, waiting for transfers between devices, shards(): lax.psum(group_sums[1].astype(jnp.bfloat16), 'rep').astype(jnp.float32)  87.3 us
  transfers between devices with their start and end apart: 12, of which 11 were waited for; matrix products, arithmetic and copies ran while one was open for 15% of the time, Pallas kernels for 0%

commit v1 on v0

v1 whole, which is shorter than its diff:
```python
import functools

import jax
import jax.numpy as jnp
from jax import lax
from jax.sharding import PartitionSpec as P

SEQ = 512


EPSILON = 1e-05

AXES = ("rep", "shard")
PACK = 16


def plain_dot(left, right, kind=jnp.float32):
    return jnp.dot(left, right, preferred_element_type=jnp.float32).astype(kind)


def rows_dot(left, right):
    return lax.dot_general(
        left, right, (((1,), (1,)), ((), ())), preferred_element_type=jnp.float32
    )


def cols_dot(left, right):
    return lax.dot_general(
        left, right, (((0,), (0,)), ((), ())), preferred_element_type=jnp.float32
    ).astype(jnp.bfloat16)


def shift_back(values, steps):
    return jnp.pad(values[:, : values.shape[1] - steps], ((0, 0), (steps, 0), (0, 0)))


def shift_ahead(values, steps):
    return jnp.pad(values[:, steps:], ((0, 0), (0, steps), (0, 0)))


def norm_back(grad_norm, values, inv_rms, gain):
    scaled = grad_norm * gain
    grad_values = inv_rms * (
        scaled - values * inv_rms * inv_rms * jnp.mean(scaled * values, -1, keepdims=True)
    )
    grad_gain = jnp.sum(grad_norm * values * inv_rms, 0)
    return (grad_values, grad_gain)


def cycle_of(size):
    wide = size // 4
    walk = [(0, 0)]
    for row in range(4):
        cols = range(1, wide)
        walk += [(row, col) for col in (cols if row % 2 == 0 else reversed(cols))]
    walk += [(row, 0) for row in (3, 2, 1)]
    return [row * wide + col for row, col in walk]


def shards(
    reps,
    size,
    tokens,
    norm_gain_one,
    in_weight,
    conv_weight,
    out_weight,
    norm_gain_two,
    gate_weight,
    up_weight,
    down_weight,
    cotangent,
):
    bf16, f32 = jnp.bfloat16, jnp.float32
    width = tokens.shape[1]
    hidden_width = gate_weight.shape[1]
    block = width // size
    fq, dq = hidden_width // 4, width // 4
    ring = cycle_of(size)
    place = [ring.index(s) for s in range(size)]

    def pairs(move):
        return [
            (r * size + s, move(r, s)[0] * size + move(r, s)[1])
            for r in range(reps)
            for s in range(size)
        ]

    cw = pairs(lambda r, s: (r, ring[(place[s] + 1) % size]))
    ccw = pairs(lambda r, s: (r, ring[(place[s] - 1) % size]))
    to_core = pairs(lambda r, s: (r ^ 1, s))
    to_y = pairs(lambda r, s: (r ^ 2, s))

    def send(value, perm):
        return lax.ppermute(value, AXES, perm)

    rep = lax.axis_index("rep")
    core, ybit = rep % 2, (rep // 2) % 2
    at = jnp.asarray(place)[lax.axis_index("shard")]

    order = [0]
    for step in range(1, size // 2):
        order += [step, size - step]
    order += [size // 2]
    natural_block = jnp.asarray(ring)[(at - jnp.asarray(order)) % size]
    natural = (natural_block[:, None] * block + jnp.arange(block)[None, :]).reshape(-1)
    to_rel = (jnp.arange(width)[:, None] == natural[None, :]).astype(bf16)

    def quarter(i, j):
        return (core ^ i) * 2 + (ybit ^ j)

    quarters = ((0, 0), (0, 1), (1, 0), (1, 1))
    natural_feature = (
        jnp.stack([quarter(i, j) for i, j in quarters])[:, None] * dq + jnp.arange(dq)[None, :]
    ).reshape(-1)

    def ring_gather(piece, flip):
        got = {0: piece}
        n_cw = size // 2 - (1 if flip else 0)
        up = down = piece
        for step in range(1, size // 2 + 1):
            if step <= n_cw:
                up = got[step] = send(up, cw)
            if step <= size - 1 - n_cw:
                down = got[size - step] = send(down, ccw)
        return got

    def paired(got):
        return [[got[s], got[size - s]] for s in range(1, size // 2)] + [[got[size // 2]]]

    def ring_scatter(blocks, flip):
        n_cw = size // 2 - (1 if flip else 0)
        n_ccw = size - 1 - n_cw
        up = down = None
        for step in range(size // 2, 0, -1):
            if step <= n_cw:
                own = blocks[size - step]
                up = send(own if up is None else up + own, cw)
            if step <= n_ccw:
                own = blocks[step]
                down = send(own if down is None else down + own, ccw)
        return (blocks[0].astype(f32) + up.astype(f32) + down.astype(f32)).astype(bf16)

    def add(left, right):
        return (left.astype(f32) + right.astype(f32)).astype(bf16)

    def high_reps(value):
        step = 4
        while step < reps:
            value = add(value, send(value, pairs(lambda r, s: (r ^ step, s))))
            step *= 2
        return value

    def part(value, axis, i, j, extent):
        return lax.dynamic_slice_in_dim(value, quarter(i, j) * extent, extent, axis)

    def in_part(i, j):
        return part(in_weight.reshape(block, 3, width), 2, i, j, dq).reshape(block, 3 * dq)

    def gu_part(i, j):
        return jnp.concatenate(
            [part(gate_weight, 1, i, j, fq), part(up_weight, 1, i, j, fq)], 1
        )

    small = jnp.concatenate([norm_gain_one, norm_gain_two, conv_weight.reshape(-1)])
    pack = jnp.pad(small[None, :], ((0, PACK - 1), (0, 3 * dq - small.shape[0])))

    in_got = ring_gather(jnp.concatenate([in_part(0, 0), pack], 0), False)
    gu_got = ring_gather(gu_part(0, 0), True)
    out_own = jnp.concatenate([part(out_weight, 0, 0, 0, dq), part(out_weight, 0, 0, 1, dq)], 0)
    out_got = ring_gather(out_own, True)
    down_own = jnp.concatenate([part(down_weight, 0, 0, 0, fq), part(down_weight, 0, 0, 1, fq)], 0)
    down_got = ring_gather(down_own, False)

    def quarters_of(got, mine):
        groups = [jnp.concatenate(g, 0) for g in paired(got)]
        q00 = jnp.concatenate([got[0]] + groups, 0)
        q01 = jnp.concatenate([mine] + [send(g, to_y) for g in groups], 0)
        return q00, q01, send(q00, to_core), send(q01, to_core)

    in_rows = {b: v[:block] for b, v in in_got.items()}
    packs = jnp.stack([in_got[b][block, : 5 * block] for b in order], 0).reshape(size, 5, block)
    in_q = quarters_of(in_rows, in_part(0, 1))
    gu_q = quarters_of(gu_got, gu_part(0, 1))
    out_half = jnp.concatenate([out_got[b] for b in order], 1)
    out_full = jnp.concatenate([out_half, send(out_half, to_core)], 0)
    down_half = jnp.concatenate([down_got[b] for b in order], 1)
    down_h = (down_half, send(down_half, to_core))

    gain_one_f = packs[:, 0].reshape(-1).astype(f32)
    gain_two_f = packs[:, 1].reshape(-1).astype(f32)
    to_feature = (natural[:, None] == natural_feature[None, :]).astype(bf16)
    taps = plain_dot(packs[:, 2:].transpose(1, 0, 2).reshape(3, width), to_feature)

    tokens_f = plain_dot(tokens, to_rel)
    cot = plain_dot(cotangent, to_rel, bf16)
    inv_one = lax.rsqrt(jnp.mean(tokens_f * tokens_f, -1, keepdims=True) + EPSILON)
    normed_one = (tokens_f * inv_one * gain_one_f).astype(bf16)
    projected = [plain_dot(normed_one, w) for w in in_q]
    b_part = jnp.concatenate([p[:, :dq] for p in projected], 1)
    c_part = jnp.concatenate([p[:, dq : 2 * dq] for p in projected], 1)
    x_part = jnp.concatenate([p[:, 2 * dq :] for p in projected], 1)
    mixed_in = (b_part * x_part).reshape(-1, SEQ, width)
    conv_out = (
        taps[0] * shift_back(mixed_in, 2) + taps[1] * shift_back(mixed_in, 1) + taps[2] * mixed_in
    ).reshape(-1, width)
    gated = (c_part * conv_out).astype(bf16)
    middle = tokens_f + plain_dot(gated, out_full)
    inv_two = lax.rsqrt(jnp.mean(middle * middle, -1, keepdims=True) + EPSILON)
    normed_two = (middle * inv_two * gain_two_f).astype(bf16)
    pre = [plain_dot(normed_two, w) for w in gu_q]
    gate_pre = [p[:, :fq] for p in pre]
    up_proj = [p[:, fq:] for p in pre]
    sigma = [jax.nn.sigmoid(g) for g in gate_pre]
    silu = [g * s for g, s in zip(gate_pre, sigma)]
    hidden = [(s * u).astype(bf16) for s, u in zip(silu, up_proj)]
    hidden_h = [jnp.concatenate(hidden[2 * i : 2 * i + 2], 1) for i in range(2)]
    block_out = (
        middle + plain_dot(hidden_h[0], down_h[0]) + plain_dot(hidden_h[1], down_h[1])
    ).astype(bf16)

    def cut(value, axis, at_block, count=1):
        start = at_block * block
        return lax.slice_in_dim(value, start, start + count * block, axis=axis)

    def blocks_of(value, axis):
        return {b: cut(value, axis, n) for n, b in enumerate(order)}

    down_local = [cols_dot(h, cot) for h in hidden_h]
    down_sum = add(down_local[0], send(down_local[1], to_core))
    down_slice = ring_scatter(blocks_of(down_sum, 1), True)

    cot_f = cot.astype(f32)
    hidden_grad_h = [rows_dot(cot, w) for w in down_h]
    hidden_grad = [h[:, j * fq : (j + 1) * fq] for h in hidden_grad_h for j in range(2)]
    gu_back = [
        jnp.concatenate(
            [
                (hg * u * s * (1.0 + g * (1.0 - s))).astype(bf16),
                (hg * sl).astype(bf16),
            ],
            1,
        )
        for hg, u, s, g, sl in zip(hidden_grad, up_proj, sigma, gate_pre, silu)
    ]
    gu_local = [cols_dot(normed_two, b) for b in gu_back]
    gu_sum = [add(gu_local[j], send(gu_local[2 + j], to_core)) for j in range(2)]
    cuts = [(size - 3, 3), (3, size - 6), (0, 3)]
    gu_rows = {}
    for start, count in cuts:
        away = send(cut(gu_sum[1], 0, start, count), to_y)
        both = add(cut(gu_sum[0], 0, start, count), away)
        for n in range(count):
            gu_rows[order[start + n]] = cut(both, 0, n)

    normed_two_grad = sum(rows_dot(b, w) for b, w in zip(gu_back, gu_q))
    middle_norm_grad, gain_two_local = norm_back(normed_two_grad, middle, inv_two, gain_two_f)
    middle_grad = cot_f + middle_norm_grad
    branch_back = middle_grad.astype(bf16)
    out_local = cols_dot(gated, branch_back)
    half = out_local.shape[0] // 2
    out_sum = add(out_local[:half], send(out_local[half:], to_core))
    out_slice = ring_scatter(blocks_of(out_sum, 1), True)
    gated_grad = rows_dot(branch_back, out_full)
    c_grad = gated_grad * conv_out
    conv_grad_in = (gated_grad * c_part).reshape(-1, SEQ, width)
    conv_local = jnp.stack(
        [
            jnp.sum(conv_grad_in * shift_back(mixed_in, 2), (0, 1)),
            jnp.sum(conv_grad_in * shift_back(mixed_in, 1), (0, 1)),
            jnp.sum(conv_grad_in * mixed_in, (0, 1)),
        ],
        0,
    )
    mixed_grad = (
        taps[2] * conv_grad_in
        + taps[1] * shift_ahead(conv_grad_in, 1)
        + taps[0] * shift_ahead(conv_grad_in, 2)
    ).reshape(-1, width)
    b_back = (mixed_grad * x_part).astype(bf16)
    c_back = c_grad.astype(bf16)
    x_back = (mixed_grad * b_part).astype(bf16)

    def of_quarter(value, n):
        return value[:, n * dq : (n + 1) * dq]

    projected_back = [
        jnp.concatenate([of_quarter(v, n) for v in (b_back, c_back, x_back)], 1) for n in range(4)
    ]
    in_back_h = [jnp.concatenate(projected_back[2 * i : 2 * i + 2], 1) for i in range(2)]
    in_local = [cols_dot(normed_one, b) for b in in_back_h]
    normed_one_grad = sum(rows_dot(b, w) for b, w in zip(projected_back, in_q))
    tokens_norm_grad, gain_one_local = norm_back(normed_one_grad, tokens_f, inv_one, gain_one_f)
    tokens_grad = (middle_grad + tokens_norm_grad).astype(bf16)

    conv_rel = lax.dot_general(
        conv_local.astype(bf16), to_feature, (((1,), (1,)), ((), ())), preferred_element_type=f32
    ).astype(bf16)
    small_grad = jnp.concatenate(
        [gain_one_local.astype(bf16)[None], gain_two_local.astype(bf16)[None], conv_rel], 0
    )
    small_rows = small_grad.reshape(5, size, block).transpose(1, 0, 2).reshape(size, 5 * block)
    small_rows = jnp.pad(small_rows, ((0, 0), (0, 6 * dq - 5 * block)))
    small_sum = jnp.pad(small_rows[:, None], ((0, 0), (0, PACK - 1), (0, 0)))

    def with_small(value):
        rows = value.reshape(size, block, 6 * dq)
        return jnp.concatenate([rows, small_sum], 1)

    in_mine = with_small(in_local[0])
    in_sum = add(in_mine, send(with_small(in_local[1]), to_core))
    in_slice = ring_scatter({b: in_sum[n] for n, b in enumerate(order)}, False)
    gu_slice = ring_scatter(gu_rows, False)

    def over_y(value):
        return high_reps(add(value, send(value, to_y)))

    def swap(flag, first, second, axis):
        return jnp.where(
            flag == 0,
            jnp.concatenate([first, second], axis),
            jnp.concatenate([second, first], axis),
        )

    def y_ordered(value, axis):
        n = value.shape[axis] // 2
        return swap(
            ybit,
            lax.slice_in_dim(value, 0, n, axis=axis),
            lax.slice_in_dim(value, n, 2 * n, axis=axis),
            axis,
        )

    def whole(value):
        total = over_y(y_ordered(value, 0))
        return swap(core, total, send(total, to_core), 0).astype(f32)

    down_grad = whole(down_slice)
    out_grad = whole(out_slice)
    in_total = over_y(
        jnp.concatenate([y_ordered(in_slice[:block], 1), in_slice[block:]], 0)
    )
    in_mine_total = in_total[:block].reshape(block, 2, 3, dq)
    in_other_total = send(in_total[:block], to_core).reshape(block, 2, 3, dq)
    in_grad = (
        swap(core, in_mine_total, in_other_total, 1)
        .transpose(0, 2, 1, 3)
        .reshape(block, 3 * width)
        .astype(f32)
    )
    small_total = in_total[block, : 5 * block].astype(f32).reshape(5, block)
    gu_total = high_reps(gu_slice)
    gu_other = send(gu_total, to_y)
    gu_both = jnp.stack([gu_total, gu_other], 0)
    gu_far = send(gu_both, to_core)

    def gu_out(start):
        own = swap(ybit, gu_both[0][:, start : start + fq], gu_both[1][:, start : start + fq], 1)
        far = swap(ybit, gu_far[0][:, start : start + fq], gu_far[1][:, start : start + fq], 1)
        return swap(core, own, far, 1).astype(f32)

    gate_grad, up_grad = gu_out(0), gu_out(fq)

    def to_natural(value):
        return rows_dot(value, to_rel).astype(bf16)

    return (
        to_natural(block_out),
        to_natural(tokens_grad),
        small_total[0],
        in_grad,
        small_total[2:],
        out_grad,
        small_total[1],
        gate_grad,
        up_grad,
        down_grad,
    )


def solution(mesh):
    in_specs = (
        P(("rep", "shard"), None),
        P("shard"),
        P("shard", None),
        P(None, "shard"),
        P(None, "shard"),
        P("shard"),
        P("shard", None),
        P("shard", None),
        P(None, "shard"),
        P(("rep", "shard"), None),
    )
    out_specs = (
        P(("rep", "shard"), None),
        P(("rep", "shard"), None),
        P("shard"),
        P("shard", None),
        P(None, "shard"),
        P(None, "shard"),
        P("shard"),
        P("shard", None),
        P("shard", None),
        P(None, "shard"),
    )
    body = functools.partial(shards, mesh.shape["rep"], mesh.shape["shard"])
    return jax.shard_map(body, mesh=mesh, in_specs=in_specs, out_specs=out_specs, check_vma=False)
```

time: 1520 us -> 747 us (0.49)
  waiting for transfers between devices: 1100 us -> 274 us
  blocking collectives: 83.2 us -> 0 us
  starting transfers between devices: 0.48 us -> 82.5 us
  other arithmetic: 47.7 us -> 83.2 us
  matrix products: 212 us -> 232 us
    reduce_scatter x3 -> x0, waiting for transfers between devices: 451 us -> none  [the longest x1 166 us: shards(): lax.psum_scatter(gate_local.astype(jnp.bfloat16), 'shard', scatter_dimens...]
    all_gather x5 -> x0, waiting for transfers between devices: 442 us -> none  [the longest x1 131 us: shards(): lax.all_gather(gate_weight, 'shard', axis=0, tiled=True)]
    ppermute x0 -> x86, waiting for transfers between devices: none -> 274 us  [send(): return lax.ppermute(value, AXES, perm)]
    unnamed x15 -> x0, waiting for transfers between devices: 120 us -> none
    psum x1 -> x0, waiting for transfers between devices: 87.3 us -> none  [shards(): lax.psum(group_sums[1].astype(jnp.bfloat16), 'rep').astype(jnp.float32)]
    ppermute x0 -> x86, starting transfers between devices: none -> 82.5 us  [send(): return lax.ppermute(value, AXES, perm)]
    all_gather x3 -> x0, blocking collectives: 57.3 us -> none  [the longest x1 22.4 us: shards(): lax.all_gather(norm_gain_one, 'shard', axis=0, tiled=True)]
    convert_element_type x13 -> x24, other arithmetic: 18.8 us -> 52 us  [the longest x2 28.3 us: shards(): (hg * u * s * (1.0 + g * (1.0 - s))).astype(bf16)]
  transfers between devices with their start and end apart: 12 -> 86, of which waited for: 11 -> 32; matrix products, arithmetic and copies ran while one was open for 15% -> 38% of each run, Pallas kernels for 0% -> 0%
where the time goes in v1:
time: 747 us; the launch traced here: 739 us
  waiting for transfers between devices  274 us (37%)
  matrix products  232 us (31%)
  other arithmetic  83.2 us (11%)
  starting transfers between devices  82.5 us (11%)
  local copies, waits for them, and re-layouts  64.8 us (9%)
    ppermute x86, waiting for transfers between devices, send(): return lax.ppermute(value, AXES, perm)  274 us
    dot_general x13, matrix products, rows_dot(): lax.dot_general(left, right, (((1,), (1,)), ((), ())), preferred_element_...  102 us
    ppermute x86, starting transfers between devices, send(): return lax.ppermute(value, AXES, perm)  82.5 us
    dot_general x13, matrix products, plain_dot(): return jnp.dot(left, right, preferred_element_type=jnp.float32).astype(kind)  71.3 us
    dot_general x9, matrix products, cols_dot(): lax.dot_general(left, right, (((0,), (0,)), ((), ())), preferred_element_...  57.9 us
    unnamed x217, local copies, waits for them, and re-layouts  39.9 us
    convert_element_type x2, other arithmetic, shards(): (hg * u * s * (1.0 + g * (1.0 - s))).astype(bf16)  28.3 us
  transfers between devices with their start and end apart: 86, of which 32 were waited for; matrix products, arithmetic and copies ran while one was open for 38% of the time, Pallas kernels for 0%

profile of v1, /device:TPU:0, one launch (start us, length us, event | category | flops | bytes accessed | tf_op | source)
XLA Modules:
  0.0 738.9 jit_solution(4273377654977269600)
XLA Ops:
  67.2 13.6 %collective-permute-done.3 = bf16[144,768]{0,1:T(8,128)(2,1)S(1)} collective-permute-done((bf16[144,768]{0,1:T(8,128)(2,1)}, bf16[144,768]{0,1:T(8,128)(2,1)S(1)}, u32[]{:S(2)}, u32[]{:S(2)}) %collective-permute-start.3) | collective-permute-done | bytes 221216 | tf_op jit(solution)/shard_map/ppermute | solution.py:95
  106.0 14.7 %collective-permute-done.6 = bf16[144,768]{0,1:T(8,128)(2,1)S(1)} collective-permute-done((bf16[144,768]{0,1:T(8,128)(2,1)S(1)}, bf16[144,768]{0,1:T(8,128)(2,1)S(1)}, u32[]{:S(2)}, u32[]{:S(2)}) %collective-permute-start.6) | collective-permute-done | bytes 221216 | tf_op jit(solution)/shard_map/ppermute | solution.py:95
  205.3 10.0 %fusion.145 = f32[1024,2304]{1,0:T(8,128)} fusion(bf16[1024,1024]{1,0:T(8,128)(2,1)S(1)} %copy-done.49, bf16[2304,1024]{1,0:T(8,128)(2,1)} %constant_dynamic-update-slice_fusion.41), kind=kOutput, calls=%fused_computation.368 | convolution fusion | flops 4831838208 | bytes 16252928 | tf_op jit(solution)/shard_map/dot_general | solution.py:22
  231.5 11.6 %fusion.141 = f32[1024,2304]{1,0:T(8,128)} fusion(bf16[1024,1024]{0,1:T(8,128)(2,1)S(1)} %multiply_convert_fusion.12, bf16[1024,2304]{1,0:T(8,128)(2,1)} %constant_dynamic-update-slice_fusion.29), kind=kOutput, calls=%fused_computation.364 | convolution fusion | flops 4831838208 | bytes 16252928 | tf_op jit(solution)/shard_map/dot_general | solution.py:18
  247.6 10.0 %fusion.142 = f32[1024,2304]{1,0:T(8,128)} fusion(bf16[1024,1024]{0,1:T(8,128)(2,1)S(1)} %multiply_convert_fusion.12, bf16[1024,2304]{1,0:T(8,128)(2,1)} %constant_dynamic-update-slice_fusion.37), kind=kOutput, calls=%fused_computation.365 | convolution fusion | flops 4831838208 | bytes 16252928 | tf_op jit(solution)/shard_map/dot_general | solution.py:18
  257.6 14.3 %multiply_convert_fusion.5 = (bf16[1024,1152]{1,0:T(8,128)(2,1)}, bf16[1024,1152]{1,0:T(8,128)(2,1)}, bf16[1024,1152]{1,0:T(8,128)(2,1)}, bf16[1024,1152]{1,0:T(...) fusion(f32[1024,2304]{1,0:T(8,128)S(1)} %bitcast.206, f32[1024,2304]{1,0:T(8,128)} %fusion.142, ...), kind=kLoop, calls=%fused_computation.28 | loop fusion | flops 35389440 | bytes 42467328 | tf_op jit(solution)/shard_map/convert_element_type | solution.py:239
  272.0 10.3 %fusion.25 = f32[1024,1024]{0,1:T(8,128)} fusion(bf16[1024,2304]{1,0:T(8,128)(2,1)} %constant_dynamic-update-slice_fusion.29, bf16[1024,1152]{1,0:T(8,128)(2,1)S(1)} %get-tuple-element.56, bf16[1024,1152]{1,0:T(8,128)(2,1)} %get-tuple-element.57), kind=kOutput, calls=%fused_computation.92 | convolution fusion | flops 4841275392 | bytes 13631488 | tf_op jit(solution)/shard_map/dot_general | solution.py:22
  290.0 9.9 %fusion.146 = f32[1024,2304]{1,0:T(8,128)} fusion(bf16[1024,1024]{1,0:T(8,128)(2,1)S(1)} %copy-done.50, bf16[2304,1024]{1,0:T(8,128)(2,1)} %collective-permute-done.41), kind=kOutput, calls=%fused_computation.369 | convolution fusion | flops 4831838208 | bytes 16252928 | tf_op jit(solution)/shard_map/dot_general | solution.py:22
  299.9 10.3 %fusion.144 = f32[1024,2304]{1,0:T(8,128)} fusion(bf16[1024,1024]{0,1:T(8,128)(2,1)S(1)} %copy-done.47, bf16[1024,2304]{1,0:T(8,128)(2,1)} %collective-permute-done.40), kind=kOutput, calls=%fused_computation.367 | convolution fusion | flops 4831838208 | bytes 16252928 | tf_op jit(solution)/shard_map/dot_general | solution.py:18
  310.1 13.9 %multiply_convert_fusion.3 = (bf16[1024,1152]{1,0:T(8,128)(2,1)}, bf16[1024,1152]{1,0:T(8,128)(2,1)}, bf16[1024,1152]{1,0:T(8,128)(2,1)}, bf16[1024,1152]{1,0:T(...) fusion(f32[1024,2304]{1,0:T(8,128)} %fusion.146, f32[1024,2304]{1,0:T(8,128)S(1)} %fusion.143, ...), kind=kLoop, calls=%fused_computation.26 | loop fusion | flops 35389440 | bytes 42467328 | tf_op jit(solution)/shard_map/convert_element_type | solution.py:239
  324.1 10.2 %fusion.22 = f32[1024,1024]{0,1:T(8,128)} fusion(bf16[1024,2304]{1,0:T(8,128)(2,1)} %collective-permute-done.40, bf16[1024,1152]{1,0:T(8,128)(2,1)S(1)} %get-tuple-element.60, bf16[1024,1152]{1,0:T(8,128)(2,1)} %get-tuple-element.61), kind=kOutput, calls=%fused_computation.89 | convolution fusion | flops 4841275392 | bytes 13631488 | tf_op jit(solution)/shard_map/dot_general | solution.py:22
  334.3 9.2 %fusion.23 = f32[1024,1024]{0,1:T(8,128)} fusion(bf16[1024,2304]{1,0:T(8,128)(2,1)} %collective-permute-done.39, bf16[1024,1152]{1,0:T(8,128)(2,1)S(1)} %copy-done.40, bf16[1024,1152]{1,0:T(8,128)(2,1)S(1)} %copy-done.39), kind=kOutput, calls=%fused_computation.90 | convolution fusion | flops 4841275392 | bytes 13631488 | tf_op jit(solution)/shard_map/dot_general | solution.py:22
  343.5 15.3 %multiply_reduce_fusion.3 = (bf16[1024]{0:T(1024)(128)(2,1)S(1)}, f32[1024]{0:T(1024)S(1)}, f32[1024,1024]{0,1:T(8,128)}) fusion(f32[1024,1024]{0,1:T(8,128)S(1)} %get-tuple-element.180, f32[1024]{0:T(1024)S(1)} %add_rsqrt_fusion, f32[1024]{0:T(1024)S(1)} %bitcast.236, f32[1024,1024]{0,1:T(8,128)} %fusion.22, f32[1024,1024]{0,1:T(8,128)} %fusion.23, ...), kind=kOutput, calls=%fused_computation.68 | convolution fusion | flops 4850710528 | bytes 30423040 | tf_op jit(solution)/shard_map/dot_general | solution.py:22
  368.7 8.6 %multiply_reduce_fusion.2 = (bf16[1024]{0:T(1024)(128)(2,1)S(1)}, bf16[1024]{0:T(1024)(128)(2,1)S(1)}, f32[1024,1024]{1,0:T(8,128)S(1)}, f32[1024,1024]{1,0:T(8,128)}) fusion(f32[2,510,1024]{2,1,0:T(8,128)S(1)} %bitcast.201, f32[2,511,1024]{2,1,0:T(8,128)S(1)} %bitcast.200, f32[1024,256]{1,0:T(8,128)} %copy-done.11, f32[1024,256]{1,0:T(8,128)} %copy-done.10, ...), kind=kOutput, calls=%fused_computation.67 | convolution fusion | flops 2161113088 | bytes 27242496 | tf_op jit(solution)/shard_map/dot_general | solution.py:22
  411.2 9.0 %fusion.26 = f32[1024,1024]{0,1:T(8,128)} fusion(bf16[2304,1024]{1,0:T(8,128)(2,1)} %collective-permute-done.41, bf16[1024,1152]{1,0:T(8,128)(2,1)S(1)} %copy-done.34, bf16[1024,1152]{1,0:T(8,128)(2,1)S(1)} %copy-done.32), kind=kOutput, calls=%fused_computation.93 | convolution fusion | flops 4841275392 | bytes 13631488 | tf_op jit(solution)/shard_map/dot_general | solution.py:18
  420.2 13.3 %fusion.47 = bf16[1024,1024]{1,0:T(8,128)(2,1)} fusion(s32[1024]{0:T(1024)S(1)} %copy-done.69, f32[1024,1024]{0,1:T(8,128)} %fusion.26, f32[1024,1024]{0,1:T(8,128)} %copy-done.6, bf16[2304,1024]{1,0:T(8,128)(2,1)} %constant_dynamic-update-slice_fusion.41, bf16[1024,1152]{1,0:T(8,128)(2,1)} %get-tuple-element.55, bf16[1024,1152]{1,0:T(8,128)(2,1)} %get-tuple-element.58), kind=kOutput, calls=%fused_computation.113 | convolution fusion | flops 6994001920 | bytes 19927040 | tf_op jit(solution)/shard_map/dot_general | solution.py:22
  436.0 9.6 %convolution_convert_fusion.4 = bf16[1024,2304]{1,0:T(8,128)(2,1)} fusion(bf16[1024,1024]{0,1:T(8,128)(2,1)} %copy-done.46, bf16[1024,1152]{1,0:T(8,128)(2,1)} %get-tuple-element.52, bf16[1024,1152]{1,0:T(8,128)(2,1)} %get-tuple-element.51), kind=kOutput, calls=%fused_computation.11 | convolution fusion | flops 4843634688 | bytes 11534336 | tf_op jit(solution)/shard_map/dot_general | solution.py:28
  477.7 8.4 %collective-permute-done.43 = bf16[144,1536]{1,0:T(8,128)(2,1)S(1)} collective-permute-done((bf16[144,1536]{1,0:T(8,128)(2,1)S(1)}, bf16[144,1536]{1,0:T(8,128)(2,1)S(1)}, u32[]{:S(2)}, u32[]{:S(2)}) %collective-permute-start.43) | collective-permute-done | bytes 442400 | tf_op jit(solution)/shard_map/ppermute | solution.py:95
  523.5 8.3 %add_convert_fusion.2 = bf16[1024,2304]{1,0:T(8,128)(2,1)} fusion(bf16[1024,2304]{1,0:T(8,128)(2,1)} %collective-permute-done.62, bf16[1024,1024]{0,1:T(8,128)(2,1)S(1)} %copy-done.48, bf16[1024,1152]{1,0:T(8,128)(2,1)S(1)} %copy-done.26, bf16[1024,1152]{1,0:T(8,128)(2,1)S(1)} %copy-done.27), kind=kOutput, calls=%fused_computation.3 | convolution fusion | flops 4853071872 | bytes 16252928 | tf_op jit(solution)/shard_map/dot_general | solution.py:28
  537.0 89.8 %collective-permute-done.50 = bf16[144,1536]{1,0:T(8,128)(2,1)S(1)} collective-permute-done((bf16[144,1536]{1,0:T(8,128)(2,1)S(1)}, bf16[144,1536]{1,0:T(8,128)(2,1)S(1)}, u32[]{:S(2)}, u32[]{:S(2)}) %collective-permute-start.50) | collective-permute-done | bytes 442400 | tf_op jit(solution)/shard_map/ppermute | solution.py:95
  628.6 9.8 %collective-permute-done.81 = bf16[2304,128]{1,0:T(8,128)(2,1)S(1)} collective-permute-done((bf16[2304,128]{1,0:T(8,128)(2,1)S(1)}, bf16[2304,128]{1,0:T(8,128)(2,1)S(1)}, u32[]{:S(2)}, u32[]{:S(2)}) %collective-permute-start.81) | collective-permute-done | bytes 589856 | tf_op jit(solution)/shard_map/ppermute | solution.py:95
  660.9 10.7 %collective-permute-done.66 = bf16[128,2304]{1,0:T(8,128)(2,1)S(1)} collective-permute-done((bf16[128,2304]{1,0:T(8,128)(2,1)S(1)}, bf16[128,2304]{1,0:T(8,128)(2,1)S(1)}, u32[]{:S(2)}, u32[]{:S(2)}) %collective-permute-start.66) | collective-permute-done | bytes 589856 | tf_op jit(solution)/shard_map/ppermute | solution.py:95
  673.8 10.4 %collective-permute-done.79 = bf16[2304,128]{1,0:T(8,128)(2,1)S(1)} collective-permute-done((bf16[2304,128]{1,0:T(8,128)(2,1)S(1)}, bf16[2304,128]{1,0:T(8,128)(2,1)S(1)}, u32[]{:S(2)}, u32[]{:S(2)}) %collective-permute-start.79) | collective-permute-done | bytes 589856 | tf_op jit(solution)/shard_map/ppermute | solution.py:95
  696.9 11.2 %collective-permute-done.69 = bf16[128,2304]{1,0:T(8,128)(2,1)S(1)} collective-permute-done((bf16[128,2304]{1,0:T(8,128)(2,1)S(1)}, bf16[128,2304]{1,0:T(8,128)(2,1)S(1)}, u32[]{:S(2)}, u32[]{:S(2)}) %collective-permute-start.69) | collective-permute-done | bytes 589856 | tf_op jit(solution)/shard_map/ppermute | solution.py:95
  (533 shorter events, 393.5 us)
Async XLA Ops:
  4.8 35.9 %collective-permute-start.1 = (bf16[144,768]{0,1:T(8,128)(2,1)}, bf16[144,768]{0,1:T(8,128)(2,1)}, u32[]{:S(2)}, u32[]{:S(2)}) collective-permute-start(bf16[144,768]{0,1:T(8,128)(2,1)} %fusion.92), channel_id=1, source_target_pairs={{0,2},{1,0},{2,4},{3,1},{4,6},{5,3},{6,7},{7,5},{8,10},{9,8},{10,1... | collective-permute-start | bytes 663560 | tf_op jit(solution)/shard_map/ppermute | solution.py:95
  14.6 74.5 %collective-permute-start.21 = (bf16[128,2304]{1,0:T(8,128)(2,1)}, bf16[128,2304]{1,0:T(8,128)(2,1)S(1)}, u32[]{:S(2)}, u32[]{:S(2)}) collective-permute-start(bf16[128,2304]{1,0:T(8,128)(2,1)} %get-tuple-element.145), channel_id=1, source_target_pairs={{0,1},{1,3},{2,0},{3,5},{4,2},{5,7},{6,4},{7,6},{8,9},{9,11},{10,8... | collective-permute-start | bytes 1769480 | tf_op jit(solution)/shard_map/ppermute | solution.py:95
  32.8 56.7 %collective-permute-start.22 = (bf16[128,2304]{1,0:T(8,128)(2,1)}, bf16[128,2304]{1,0:T(8,128)(2,1)S(1)}, u32[]{:S(2)}, u32[]{:S(2)}) collective-permute-start(bf16[128,2304]{1,0:T(8,128)(2,1)} %get-tuple-element.145), channel_id=1, source_target_pairs={{0,2},{1,0},{2,4},{3,1},{4,6},{5,3},{6,7},{7,5},{8,10},{9,8},{10,1... | collective-permute-start | bytes 1769480 | tf_op jit(solution)/shard_map/ppermute | solution.py:95
  34.6 57.0 %collective-permute-start.32 = (bf16[2304,128]{1,0:T(8,128)(2,1)S(1)}, bf16[2304,128]{1,0:T(8,128)(2,1)S(1)}, u32[]{:S(2)}, u32[]{:S(2)}) collective-permute-start(bf16[2304,128]{1,0:T(8,128)(2,1)S(1)} %get-tuple-element.146), channel_id=1, source_target_pairs={{0,1},{1,3},{2,0},{3,5},{4,2},{5,7},{6,4},{7,6},{8,9},{9,11},{10,8... | collective-permute-start | bytes 1769480 | tf_op jit(solution)/shard_map/ppermute | solution.py:95
  59.9 34.5 %collective-permute-start.33 = (bf16[2304,128]{1,0:T(8,128)(2,1)S(1)}, bf16[2304,128]{1,0:T(8,128)(2,1)S(1)}, u32[]{:S(2)}, u32[]{:S(2)}) collective-permute-start(bf16[2304,128]{1,0:T(8,128)(2,1)S(1)} %get-tuple-element.146), channel_id=1, source_target_pairs={{0,2},{1,0},{2,4},{3,1},{4,6},{5,3},{6,7},{7,5},{8,10},{9,8},{10,1... | collective-permute-start | bytes 1769480 | tf_op jit(solution)/shard_map/ppermute | solution.py:95
  94.4 131.9 %collective-permute-start.20 = (bf16[512,1024]{1,0:T(8,128)(2,1)}, bf16[512,1024]{1,0:T(8,128)(2,1)}, u32[]{:S(2)}, u32[]{:S(2)}) collective-permute-start(bf16[512,1024]{1,0:T(8,128)(2,1)} %constant_dynamic-update-slice_fusion.21), channel_id=1, source_target_pairs={{0,8},{1,9},{2,10},{3,11},{4,12},{5,13},{6,14},{7,15},{8,0},{9,1},... | collective-permute-start | bytes 3145736 | tf_op jit(solution)/shard_map/ppermute | solution.py:95
  95.3 80.2 %collective-permute-start.28 = (bf16[256,2304]{1,0:T(8,128)(2,1)S(1)}, bf16[256,2304]{1,0:T(8,128)(2,1)S(1)}, u32[]{:S(2)}, u32[]{:S(2)}) collective-permute-start(bf16[256,2304]{1,0:T(8,128)(2,1)S(1)} %pad_maximum_fusion.26), channel_id=1, source_target_pairs={{0,16},{1,17},{2,18},{3,19},{4,20},{5,21},{6,22},{7,23},{8,24},{9,... | collective-permute-start | bytes 3538952 | tf_op jit(solution)/shard_map/ppermute | solution.py:95
  99.4 42.1 %collective-permute-start.23 = (bf16[128,2304]{1,0:T(8,128)(2,1)S(1)}, bf16[128,2304]{1,0:T(8,128)(2,1)S(1)}, u32[]{:S(2)}, u32[]{:S(2)}) collective-permute-start(bf16[128,2304]{1,0:T(8,128)(2,1)S(1)} %collective-permute-done.21), channel_id=1, source_target_pairs={{0,1},{1,3},{2,0},{3,5},{4,2},{5,7},{6,4},{7,6},{8,9},{9,11},{10,8... | collective-permute-start | bytes 1769480 | tf_op jit(solution)/shard_map/ppermute | solution.py:95
  150.3 65.0 %collective-permute-start.11 = (bf16[1024,768]{0,1:T(8,128)(2,1)S(1)}, bf16[1024,768]{0,1:T(8,128)(2,1)S(1)}, u32[]{:S(2)}, u32[]{:S(2)}) collective-permute-start(bf16[1024,768]{0,1:T(8,128)(2,1)S(1)} %copy-done.55), channel_id=1, source_target_pairs={{0,8},{1,9},{2,10},{3,11},{4,12},{5,13},{6,14},{7,15},{8,0},{9,1},... | collective-permute-start | bytes 4718600 | tf_op jit(solution)/shard_map/ppermute | solution.py:95
  167.0 37.0 %collective-permute-start.29 = (bf16[256,2304]{1,0:T(8,128)(2,1)S(1)}, bf16[256,2304]{1,0:T(8,128)(2,1)S(1)}, u32[]{:S(2)}, u32[]{:S(2)}) collective-permute-start(bf16[256,2304]{1,0:T(8,128)(2,1)S(1)} %pad_maximum_fusion.27), channel_id=1, source_target_pairs={{0,16},{1,17},{2,18},{3,19},{4,20},{5,21},{6,22},{7,23},{8,24},{9,... | collective-permute-start | bytes 3538952 | tf_op jit(solution)/shard_map/ppermute | solution.py:95
  201.6 41.5 %collective-permute-start.30 = (bf16[256,2304]{1,0:T(8,128)(2,1)}, bf16[256,2304]{1,0:T(8,128)(2,1)}, u32[]{:S(2)}, u32[]{:S(2)}) collective-permute-start(bf16[256,2304]{1,0:T(8,128)(2,1)} %pad_maximum_fusion.28), channel_id=1, source_target_pairs={{0,16},{1,17},{2,18},{3,19},{4,20},{5,21},{6,22},{7,23},{8,24},{9,... | collective-permute-start | bytes 3538952 | tf_op jit(solution)/shard_map/ppermute | solution.py:95
  204.0 85.9 %collective-permute-start.41 = (bf16[2304,1024]{1,0:T(8,128)(2,1)}, bf16[2304,1024]{1,0:T(8,128)(2,1)}, u32[]{:S(2)}, u32[]{:S(2)}) collective-permute-start(bf16[2304,1024]{1,0:T(8,128)(2,1)} %constant_dynamic-update-slice_fusion.41), channel_id=1, source_target_pairs={{0,8},{1,9},{2,10},{3,11},{4,12},{5,13},{6,14},{7,15},{8,0},{9,1},... | collective-permute-start | bytes 14155784 | tf_op jit(solution)/shard_map/ppermute | solution.py:95
  215.4 66.9 %collective-permute-start.39 = (bf16[1024,2304]{1,0:T(8,128)(2,1)}, bf16[1024,2304]{1,0:T(8,128)(2,1)}, u32[]{:S(2)}, u32[]{:S(2)}) collective-permute-start(bf16[1024,2304]{1,0:T(8,128)(2,1)} %constant_dynamic-update-slice_fusion.29), channel_id=1, source_target_pairs={{0,8},{1,9},{2,10},{3,11},{4,12},{5,13},{6,14},{7,15},{8,0},{9,1},... | collective-permute-start | bytes 14155784 | tf_op jit(solution)/shard_map/ppermute | solution.py:95
  247.6 52.3 %collective-permute-start.40 = (bf16[1024,2304]{1,0:T(8,128)(2,1)}, bf16[1024,2304]{1,0:T(8,128)(2,1)}, u32[]{:S(2)}, u32[]{:S(2)}) collective-permute-start(bf16[1024,2304]{1,0:T(8,128)(2,1)} %constant_dynamic-update-slice_fusion.37), channel_id=1, source_target_pairs={{0,8},{1,9},{2,10},{3,11},{4,12},{5,13},{6,14},{7,15},{8,0},{9,1},... | collective-permute-start | bytes 14155784 | tf_op jit(solution)/shard_map/ppermute | solution.py:95
  382.7 50.9 %collective-permute-start.52 = (bf16[512,1024]{1,0:T(8,128)(2,1)}, bf16[512,1024]{1,0:T(8,128)(2,1)}, u32[]{:S(2)}, u32[]{:S(2)}) collective-permute-start(bf16[512,1024]{1,0:T(8,128)(2,1)} %slice.603), channel_id=1, source_target_pairs={{0,8},{1,9},{2,10},{3,11},{4,12},{5,13},{6,14},{7,15},{8,0},{9,1},... | collective-permute-start | bytes 3145736 | tf_op jit(solution)/shard_map/ppermute | solution.py:95
  409.8 63.0 %collective-permute-start.42 = (bf16[8,144,1536]{2,1,0:T(8,128)(2,1)}, bf16[8,144,1536]{2,1,0:T(8,128)(2,1)}, u32[]{:S(2)}, u32[]{:S(2)}) collective-permute-start(bf16[8,144,1536]{2,1,0:T(8,128)(2,1)} %fusion.21), channel_id=1, source_target_pairs={{0,8},{1,9},{2,10},{3,11},{4,12},{5,13},{6,14},{7,15},{8,0},{9,1},... | collective-permute-start | bytes 10616840 | tf_op jit(solution)/shard_map/ppermute | solution.py:95
  463.5 44.1 %collective-permute-start.63 = (bf16[1024,2304]{1,0:T(8,128)(2,1)}, bf16[1024,2304]{1,0:T(8,128)(2,1)}, u32[]{:S(2)}, u32[]{:S(2)}) collective-permute-start(bf16[1024,2304]{1,0:T(8,128)(2,1)} %convolution_convert_fusion.2), channel_id=1, source_target_pairs={{0,8},{1,9},{2,10},{3,11},{4,12},{5,13},{6,14},{7,15},{8,0},{9,1},... | collective-permute-start | bytes 14155784 | tf_op jit(solution)/shard_map/ppermute | solution.py:95
  463.5 35.5 %collective-permute-start.76 = (bf16[2304,1024]{1,0:T(8,128)(2,1)}, bf16[2304,1024]{1,0:T(8,128)(2,1)}, u32[]{:S(2)}, u32[]{:S(2)}) collective-permute-start(bf16[2304,1024]{1,0:T(8,128)(2,1)} %convolution_convert_fusion), channel_id=1, source_target_pairs={{0,8},{1,9},{2,10},{3,11},{4,12},{5,13},{6,14},{7,15},{8,0},{9,1},... | collective-permute-start | bytes 14155784 | tf_op jit(solution)/shard_map/ppermute | solution.py:95
  492.4 30.7 %collective-permute-start.62 = (bf16[1024,2304]{1,0:T(8,128)(2,1)}, bf16[1024,2304]{1,0:T(8,128)(2,1)}, u32[]{:S(2)}, u32[]{:S(2)}) collective-permute-start(bf16[1024,2304]{1,0:T(8,128)(2,1)} %convolution_convert_fusion.4), channel_id=1, source_target_pairs={{0,8},{1,9},{2,10},{3,11},{4,12},{5,13},{6,14},{7,15},{8,0},{9,1},... | collective-permute-start | bytes 14155784 | tf_op jit(solution)/shard_map/ppermute | solution.py:95
  516.0 126.6 %collective-permute-start.68 = (bf16[256,2304]{1,0:T(8,128)(2,1)}, bf16[256,2304]{1,0:T(8,128)(2,1)}, u32[]{:S(2)}, u32[]{:S(2)}) collective-permute-start(bf16[256,2304]{1,0:T(8,128)(2,1)} %slice.623), channel_id=1, source_target_pairs={{0,16},{1,17},{2,18},{3,19},{4,20},{5,21},{6,22},{7,23},{8,24},{9,... | collective-permute-start | bytes 3538952 | tf_op jit(solution)/shard_map/ppermute | solution.py:95
  518.6 132.8 %collective-permute-start.64 = (bf16[384,2304]{1,0:T(8,128)(2,1)}, bf16[384,2304]{1,0:T(8,128)(2,1)}, u32[]{:S(2)}, u32[]{:S(2)}) collective-permute-start(bf16[384,2304]{1,0:T(8,128)(2,1)} %get-tuple-element.71), channel_id=1, source_target_pairs={{0,16},{1,17},{2,18},{3,19},{4,20},{5,21},{6,22},{7,23},{8,24},{9,... | collective-permute-start | bytes 5308424 | tf_op jit(solution)/shard_map/ppermute | solution.py:95
  531.9 119.5 %collective-permute-start.65 = (bf16[384,2304]{1,0:T(8,128)(2,1)}, bf16[384,2304]{1,0:T(8,128)(2,1)}, u32[]{:S(2)}, u32[]{:S(2)}) collective-permute-start(bf16[384,2304]{1,0:T(8,128)(2,1)} %get-tuple-element.72), channel_id=1, source_target_pairs={{0,16},{1,17},{2,18},{3,19},{4,20},{5,21},{6,22},{7,23},{8,24},{9,... | collective-permute-start | bytes 5308424 | tf_op jit(solution)/shard_map/ppermute | solution.py:95
  532.8 93.9 %collective-permute-start.50 = (bf16[144,1536]{1,0:T(8,128)(2,1)S(1)}, bf16[144,1536]{1,0:T(8,128)(2,1)S(1)}, u32[]{:S(2)}, u32[]{:S(2)}) collective-permute-start(bf16[144,1536]{1,0:T(8,128)(2,1)S(1)} %pad_maximum_fusion.36), channel_id=1, source_target_pairs={{0,16},{1,17},{2,18},{3,19},{4,20},{5,21},{6,22},{7,23},{8,24},{9,... | collective-permute-start | bytes 1327112 | tf_op jit(solution)/shard_map/ppermute | solution.py:95
  535.4 93.2 %collective-permute-start.77 = (bf16[2304,128]{1,0:T(8,128)(2,1)}, bf16[2304,128]{1,0:T(8,128)(2,1)S(1)}, u32[]{:S(2)}, u32[]{:S(2)}) collective-permute-start(bf16[2304,128]{1,0:T(8,128)(2,1)} %get-tuple-element.67), channel_id=1, source_target_pairs={{0,1},{1,3},{2,0},{3,5},{4,2},{5,7},{6,4},{7,6},{8,9},{9,11},{10,8... | collective-permute-start | bytes 1769480 | tf_op jit(solution)/shard_map/ppermute | solution.py:95
  (146 other events, 2385.2 us)

commit v2 on v1

v2 whole, which is shorter than its diff:
```python
import functools

import jax
import jax.numpy as jnp
from jax import lax
from jax.sharding import PartitionSpec as P

SEQ = 512


EPSILON = 1e-05

AXES = ("rep", "shard")
PACK = 16


def plain_dot(left, right, kind=jnp.float32):
    return jnp.dot(left, right, preferred_element_type=jnp.float32).astype(kind)


def rows_dot(left, right):
    return lax.dot_general(
        left, right, (((1,), (1,)), ((), ())), preferred_element_type=jnp.float32
    )


def cols_dot(left, right):
    return lax.dot_general(
        left, right, (((0,), (0,)), ((), ())), preferred_element_type=jnp.float32
    ).astype(jnp.bfloat16)


def shift_back(values, steps):
    return jnp.pad(values[:, : values.shape[1] - steps], ((0, 0), (steps, 0), (0, 0)))


def shift_ahead(values, steps):
    return jnp.pad(values[:, steps:], ((0, 0), (0, steps), (0, 0)))


def norm_back(grad_norm, values, inv_rms, gain):
    scaled = grad_norm * gain
    grad_values = inv_rms * (
        scaled - values * inv_rms * inv_rms * jnp.mean(scaled * values, -1, keepdims=True)
    )
    grad_gain = jnp.sum(grad_norm * values * inv_rms, 0)
    return (grad_values, grad_gain)


def cycle_of(size):
    wide = size // 4
    walk = [(0, 0)]
    for row in range(4):
        cols = range(1, wide)
        walk += [(row, col) for col in (cols if row % 2 == 0 else reversed(cols))]
    walk += [(row, 0) for row in (3, 2, 1)]
    return [row * wide + col for row, col in walk]


def shards(
    reps,
    size,
    tokens,
    norm_gain_one,
    in_weight,
    conv_weight,
    out_weight,
    norm_gain_two,
    gate_weight,
    up_weight,
    down_weight,
    cotangent,
):
    bf16, f32 = jnp.bfloat16, jnp.float32
    width = tokens.shape[1]
    hidden_width = gate_weight.shape[1]
    block = width // size
    fq, dq = hidden_width // 4, width // 4
    ring = cycle_of(size)
    place = [ring.index(s) for s in range(size)]

    def pairs(move):
        return [
            (r * size + s, move(r, s)[0] * size + move(r, s)[1])
            for r in range(reps)
            for s in range(size)
        ]

    cw = pairs(lambda r, s: (r, ring[(place[s] + 1) % size]))
    ccw = pairs(lambda r, s: (r, ring[(place[s] - 1) % size]))
    to_core = pairs(lambda r, s: (r ^ 1, s))
    to_y = pairs(lambda r, s: (r ^ 2, s))

    def send(value, perm):
        return lax.ppermute(value, AXES, perm)

    rep = lax.axis_index("rep")
    core, ybit = rep % 2, (rep // 2) % 2
    at = jnp.asarray(place)[lax.axis_index("shard")]

    order = [0]
    for step in range(1, size // 2):
        order += [step, size - step]
    order += [size // 2]
    natural_block = jnp.asarray(ring)[(at - jnp.asarray(order)) % size]
    natural = (natural_block[:, None] * block + jnp.arange(block)[None, :]).reshape(-1)
    to_rel = (jnp.arange(width)[:, None] == natural[None, :]).astype(bf16)

    def quarter(i, j):
        return (core ^ i) * 2 + (ybit ^ j)

    quarters = ((0, 0), (0, 1), (1, 0), (1, 1))
    natural_feature = (
        jnp.stack([quarter(i, j) for i, j in quarters])[:, None] * dq + jnp.arange(dq)[None, :]
    ).reshape(-1)

    last = []

    def ordered_round(sends, work=None, args=()):
        leaves, tree = jax.tree.flatten(([v for v, _ in sends], tuple(args)))
        held = lax.optimization_barrier(tuple(leaves) + tuple(last))
        values, args = jax.tree.unflatten(tree, held[: len(leaves)])
        got = [send(v, perm) for v, (_, perm) in zip(values, sends)]
        made = work(*args) if work is not None else None
        last[:] = got + jax.tree.leaves(made)
        return got, made

    class Gather:
        def __init__(self, piece, flip):
            self.got = {0: piece}
            self.n_cw = size // 2 - (1 if flip else 0)
            self.n_ccw = size - 1 - self.n_cw
            self.step = 0

        def sends(self):
            self.step += 1
            self.to = []
            out = []
            if self.step <= self.n_cw:
                out.append((self.got[self.step - 1], cw))
                self.to.append(self.step)
            if self.step <= self.n_ccw:
                out.append((self.got[(size - self.step + 1) % size], ccw))
                self.to.append(size - self.step)
            return out

        def take(self, got):
            for b in self.to:
                self.got[b] = got.pop(0)

        def done(self):
            return self.step == size // 2

        def rows(self):
            return jnp.concatenate([self.got[b] for b in order], 0)

        def cols(self):
            return jnp.concatenate([self.got[b] for b in order], 1)

    class Scatter:
        def __init__(self, own, flip):
            self.own = own
            self.n_cw = size // 2 - (1 if flip else 0)
            self.n_ccw = size - 1 - self.n_cw
            self.step = size // 2 + 1
            self.up = self.down = None

        def sends(self):
            self.step -= 1
            out = []
            if self.step <= self.n_cw:
                out.append((total(*self.own(size - self.step), self.up), cw))
            if self.step <= self.n_ccw:
                out.append((total(*self.own(self.step), self.down), ccw))
            return out

        def take(self, got):
            if self.step <= self.n_cw:
                self.up = got.pop(0)
            if self.step <= self.n_ccw:
                self.down = got.pop(0)

        def done(self):
            return self.step == 1

        def result(self):
            return total(*self.own(0), self.up, self.down)

    def total(*values):
        values = [v for v in values if v is not None]
        if len(values) == 1:
            return values[0]
        return sum(v.astype(f32) for v in values).astype(bf16)

    def add(left, right):
        return total(left, right)

    def both_rounds(rings, others=(), work=None, args=()):
        sends = []
        counts = []
        for r in rings:
            mine = r.sends()
            counts.append(len(mine))
            sends += mine
        got, made = ordered_round(sends + list(others), work, args)
        for r, n in zip(rings, counts):
            r.take(got[:n])
            got = got[n:]
        return got, made

    def finish(*rings):
        while rings := [r for r in rings if not r.done()]:
            both_rounds(rings)

    def high_reps(value):
        step = 4
        while step < reps:
            value = add(value, send(value, pairs(lambda r, s: (r ^ step, s))))
            step *= 2
        return value

    def part(value, axis, i, j, extent):
        return lax.dynamic_slice_in_dim(value, quarter(i, j) * extent, extent, axis)

    def in_part(i, j):
        return part(in_weight.reshape(block, 3, width), 2, i, j, dq).reshape(block, 3 * dq)

    def gu_part(i, j):
        return jnp.concatenate(
            [part(gate_weight, 1, i, j, fq), part(up_weight, 1, i, j, fq)], 1
        )

    def half_part(value, extent):
        return jnp.concatenate([part(value, 0, 0, j, extent) for j in range(2)], 0)

    small = jnp.concatenate([norm_gain_one, norm_gain_two, conv_weight.reshape(-1)])
    pack = jnp.pad(small[None, :], ((0, PACK - 1), (0, 6 * dq - small.shape[0])))
    in_ring = Gather(
        jnp.concatenate([jnp.concatenate([in_part(0, 0), in_part(0, 1)], 1), pack], 0), False
    )
    out_ring = Gather(half_part(out_weight, dq), True)
    gu_ring = Gather(gu_part(0, 0), True)
    down_ring = Gather(half_part(down_weight, fq), False)
    far_pieces = {0: gu_part(0, 1)}
    far_order = [b for b in order if b != 0]

    def far_send():
        b = far_order[len(far_pieces) - 1]
        return (gu_ring.got[b], to_y)

    def far_take(value):
        far_pieces[far_order[len(far_pieces) - 1]] = value

    def prepare(tokens, cotangent):
        tokens_f = plain_dot(tokens, to_rel)
        inv_one = lax.rsqrt(jnp.mean(tokens_f * tokens_f, -1, keepdims=True) + EPSILON)
        return tokens_f, plain_dot(cotangent, to_rel, bf16), inv_one

    _, (tokens_f, cot, inv_one) = both_rounds([in_ring], (), prepare, (tokens, cotangent))
    both_rounds([in_ring, out_ring])
    both_rounds([in_ring, out_ring])
    both_rounds([in_ring, out_ring])
    finish(in_ring)
    in_half = jnp.concatenate([in_ring.got[b][:block] for b in order], 0)
    packs = jnp.stack([in_ring.got[b][block, : 5 * block] for b in order], 0).reshape(
        size, 5, block
    )
    gain_one_f = packs[:, 0].reshape(-1).astype(f32)
    gain_two_f = packs[:, 1].reshape(-1).astype(f32)
    to_feature = (natural[:, None] == natural_feature[None, :]).astype(bf16)
    taps = plain_dot(packs[:, 2:].transpose(1, 0, 2).reshape(3, width), to_feature)

    def project_first(tokens_f, inv_one, gain, weight):
        normed_one = (tokens_f * inv_one * gain).astype(bf16)
        return normed_one, plain_dot(normed_one, weight)

    (in_far,), (normed_one, projected_0) = both_rounds(
        [gu_ring, out_ring],
        [(in_half, to_core)],
        project_first,
        (tokens_f, inv_one, gain_one_f, in_half),
    )
    in_h = (in_half, in_far)
    finish(out_ring)
    out_half = out_ring.cols()
    (far, out_far), projected_1 = both_rounds(
        [gu_ring], [far_send(), (out_half, to_core)], plain_dot, (normed_one, in_far)
    )
    far_take(far)
    out_full = jnp.concatenate([out_half, out_far], 0)

    def convolve(p0, p1):
        projected = [p[:, 3 * dq * j : 3 * dq * (j + 1)] for p in (p0, p1) for j in range(2)]
        b_part = jnp.concatenate([p[:, :dq] for p in projected], 1)
        c_part = jnp.concatenate([p[:, dq : 2 * dq] for p in projected], 1)
        x_part = jnp.concatenate([p[:, 2 * dq :] for p in projected], 1)
        mixed_in = (b_part * x_part).reshape(-1, SEQ, width)
        conv_out = (
            taps[0] * shift_back(mixed_in, 2)
            + taps[1] * shift_back(mixed_in, 1)
            + taps[2] * mixed_in
        ).reshape(-1, width)
        gated = (c_part * conv_out).astype(bf16)
        return b_part, c_part, x_part, mixed_in, conv_out, gated

    (far,), (b_part, c_part, x_part, mixed_in, conv_out, gated) = both_rounds(
        [gu_ring], [far_send()], convolve, (projected_0, projected_1)
    )
    far_take(far)

    def mid(tokens_f, gated, weight):
        middle = tokens_f + plain_dot(gated, weight)
        inv_two = lax.rsqrt(jnp.mean(middle * middle, -1, keepdims=True) + EPSILON)
        return middle, inv_two, (middle * inv_two * gain_two_f).astype(bf16)

    (far,), (middle, inv_two, normed_two) = both_rounds(
        [gu_ring], [far_send()], mid, (tokens_f, gated, out_full)
    )
    far_take(far)

    def feed(normed, weight):
        pre = plain_dot(normed, weight)
        gate_pre, up_proj = pre[:, :fq], pre[:, fq:]
        return gate_pre, up_proj, (jax.nn.silu(gate_pre) * up_proj).astype(bf16)

    gu_q = [None] * 4
    fed = [None] * 4
    finish(gu_ring)
    gu_q[0] = gu_ring.rows()
    (far, gu_q[2]), fed[0] = both_rounds(
        [down_ring], [far_send(), (gu_q[0], to_core)], feed, (normed_two, gu_q[0])
    )
    far_take(far)
    (far,), fed[2] = both_rounds([down_ring], [far_send()], feed, (normed_two, gu_q[2]))
    far_take(far)

    def down_parts(cot, *hidden):
        return [cols_dot(h, cot) for h in hidden]

    (far,), (down_00, down_10) = both_rounds(
        [down_ring], [far_send()], down_parts, (cot, fed[0][2], fed[2][2])
    )
    far_take(far)
    (far, down_far), _ = both_rounds([down_ring], [far_send(), (down_10, to_core)])
    far_take(far)

    def column(value, b):
        n = order.index(b)
        return value[:, n * block : (n + 1) * block]

    def row(value, b):
        n = order.index(b)
        return value[n * block : (n + 1) * block]

    def col_scatter(mine, other, flip):
        return Scatter(lambda b: (column(mine, b), column(other, b)), flip)

    finish(down_ring)
    while len(far_pieces) < size:
        (far,), _ = ordered_round([far_send()])
        far_take(far)
    down_half = down_ring.cols()
    gu_q[1] = jnp.concatenate([far_pieces[b] for b in order], 0)
    down_s0 = col_scatter(down_00, down_far, True)
    (down_other, gu_q[3]), grad_h0 = both_rounds(
        [down_s0], [(down_half, to_core), (gu_q[1], to_core)], rows_dot, (cot, down_half)
    )
    down_h = (down_half, down_other)
    _, fed[1] = both_rounds([down_s0], (), feed, (normed_two, gu_q[1]))
    _, fed[3] = both_rounds([down_s0], (), feed, (normed_two, gu_q[3]))
    _, grad_h1 = both_rounds([down_s0], (), rows_dot, (cot, down_other))
    hidden_grad = [h[:, j * fq : (j + 1) * fq] for h in (grad_h0, grad_h1) for j in range(2)]

    def feed_back(grad, gate_pre, up_proj, normed):
        s = jax.nn.sigmoid(gate_pre)
        back = jnp.concatenate(
            [
                (grad * up_proj * s * (1.0 + gate_pre * (1.0 - s))).astype(bf16),
                (grad * gate_pre * s).astype(bf16),
            ],
            1,
        )
        return back, cols_dot(normed, back)

    def back_args(n):
        return (hidden_grad[n], fed[n][0], fed[n][1], normed_two)

    _, (back_3, local_3) = ordered_round([], feed_back, back_args(3))
    (gu_far_1,), (back_1, local_1) = ordered_round([(local_3, to_core)], feed_back, back_args(1))
    y_order = [size // 2]
    for step in range(size // 2 - 1, 0, -1):
        y_order += [size - step, step]
    y_order += [0]
    y_got = {}

    def y_send():
        b = y_order[len(y_got)]
        return (total(row(local_1, b), row(gu_far_1, b)), to_y)

    def y_take(value):
        y_got[y_order[len(y_got)]] = value

    (away,), (down_01, down_11) = ordered_round(
        [y_send()], down_parts, (cot, fed[1][2], fed[3][2])
    )
    y_take(away)
    (away, down_far_1), (back_2, local_2) = ordered_round(
        [y_send(), (down_11, to_core)], feed_back, back_args(2)
    )
    y_take(away)
    down_s1 = col_scatter(down_01, down_far_1, False)
    (away, gu_far_0), (back_0, local_0) = both_rounds(
        [down_s1], [y_send(), (local_2, to_core)], feed_back, back_args(0)
    )
    y_take(away)
    gu_s = Scatter(lambda b: (row(local_0, b), row(gu_far_0, b), y_got[b]), False)

    def through(b0, w0, b1, w1):
        return rows_dot(b0, w0) + rows_dot(b1, w1)

    (away,), grad_a = both_rounds(
        [down_s1, gu_s], [y_send()], through, (back_1, gu_q[1], back_3, gu_q[3])
    )
    y_take(away)

    def mid_back(grad_a, b0, w0, b1, w1, middle, inv_two, cot):
        grad = grad_a + rows_dot(b0, w0) + rows_dot(b1, w1)
        values, gain = norm_back(grad, middle, inv_two, gain_two_f)
        middle_grad = cot.astype(f32) + values
        return middle_grad, middle_grad.astype(bf16), gain

    (away,), (middle_grad, branch_back, gain_two_local) = both_rounds(
        [down_s1],
        [y_send()],
        mid_back,
        (grad_a, back_0, gu_q[0], back_2, gu_q[2], middle, inv_two, cot),
    )
    y_take(away)

    def gate_conv(branch_back, weight, gated):
        return cols_dot(gated, branch_back), rows_dot(branch_back, weight)

    (away,), (out_local, gated_grad) = both_rounds(
        [down_s1, gu_s], [y_send()], gate_conv, (branch_back, out_full, gated)
    )
    y_take(away)

    def conv_back(gated_grad, conv_out, c_part, b_part, x_part, mixed_in):
        c_grad = gated_grad * conv_out
        conv_grad_in = (gated_grad * c_part).reshape(-1, SEQ, width)
        conv_local = jnp.stack(
            [
                jnp.sum(conv_grad_in * shift_back(mixed_in, 2), (0, 1)),
                jnp.sum(conv_grad_in * shift_back(mixed_in, 1), (0, 1)),
                jnp.sum(conv_grad_in * mixed_in, (0, 1)),
            ],
            0,
        )
        mixed_grad = (
            taps[2] * conv_grad_in
            + taps[1] * shift_ahead(conv_grad_in, 1)
            + taps[0] * shift_ahead(conv_grad_in, 2)
        ).reshape(-1, width)
        b_back = (mixed_grad * x_part).astype(bf16)
        c_back = c_grad.astype(bf16)
        x_back = (mixed_grad * b_part).astype(bf16)

        def of_half(i):
            return jnp.concatenate(
                [
                    v[:, n * dq : (n + 1) * dq]
                    for n in (2 * i, 2 * i + 1)
                    for v in (b_back, c_back, x_back)
                ],
                1,
            )

        return conv_local, of_half(0), of_half(1)

    half = out_local.shape[0] // 2
    (away, out_got), (conv_local, in_back_0, in_back_1) = ordered_round(
        [y_send(), (out_local[half:], to_core)],
        conv_back,
        (gated_grad, conv_out, c_part, b_part, x_part, mixed_in),
    )
    y_take(away)
    out_s = col_scatter(out_local[:half], out_got, True)

    def in_parts(normed_one, back_0, back_1):
        return cols_dot(normed_one, back_0), cols_dot(normed_one, back_1)

    (away,), (in_local_0, in_local_1) = both_rounds(
        [gu_s, out_s], [y_send()], in_parts, (normed_one, in_back_0, in_back_1)
    )
    y_take(away)

    def first_back(b0, w0, b1, w1, tokens_f, inv_one, middle_grad):
        grad = through(b0, w0, b1, w1)
        values, gain = norm_back(grad, tokens_f, inv_one, gain_one_f)
        return (middle_grad + values).astype(bf16), gain

    (in_far_0,), (tokens_grad, gain_one_local) = both_rounds(
        [gu_s, out_s],
        [(in_local_1, to_core)],
        first_back,
        (in_back_0, in_h[0], in_back_1, in_h[1], tokens_f, inv_one, middle_grad),
    )

    conv_rel = lax.dot_general(
        conv_local.astype(bf16), to_feature, (((1,), (1,)), ((), ())), preferred_element_type=f32
    ).astype(bf16)
    small_grad = jnp.concatenate(
        [gain_one_local.astype(bf16)[None], gain_two_local.astype(bf16)[None], conv_rel], 0
    )
    small_rows = small_grad.reshape(5, size, block).transpose(1, 0, 2).reshape(size, 5 * block)
    small_rows = jnp.pad(small_rows, ((0, PACK - size), (0, 6 * dq - 5 * block)))

    def in_block(b):
        n = order.index(b)
        small = jnp.pad(small_rows[n : n + 1], ((0, PACK - 1), (0, 0)))
        far = jnp.pad(small_far[n : n + 1], ((0, PACK - 1), (0, 0)))
        return (
            jnp.concatenate([row(in_local_0, b), small], 0),
            jnp.concatenate([row(in_far_0, b), far], 0),
        )

    small_far = send(small_rows, to_core)
    in_s = Scatter(in_block, False)
    while len(y_got) < size:
        (away,), _ = ordered_round([y_send()])
        y_take(away)
    finish(gu_s)
    gu_slice = gu_s.result()

    def block_sum(middle, h0, h1, h2, h3, w0, w1):
        return (
            middle
            + plain_dot(jnp.concatenate([h0, h1], 1), w0)
            + plain_dot(jnp.concatenate([h2, h3], 1), w1)
        ).astype(bf16)

    (gu_other,), block_out = both_rounds(
        [in_s, out_s],
        [(gu_slice, to_y)],
        block_sum,
        (middle, *[f[2] for f in fed], *down_h),
    )
    both_rounds([in_s, out_s])
    both_rounds([in_s])
    both_rounds([in_s])
    finish(in_s, out_s, down_s0, down_s1)
    down_slice = jnp.concatenate([down_s0.result(), down_s1.result()], 0)
    out_slice = out_s.result()
    in_slice = in_s.result()

    def over_y(value):
        return high_reps(add(value, send(value, to_y)))

    def swap(flag, first, second, axis):
        return jnp.where(
            flag == 0,
            jnp.concatenate([first, second], axis),
            jnp.concatenate([second, first], axis),
        )

    def y_ordered(value, axis):
        n = value.shape[axis] // 2
        return swap(
            ybit,
            lax.slice_in_dim(value, 0, n, axis=axis),
            lax.slice_in_dim(value, n, 2 * n, axis=axis),
            axis,
        )

    def whole(value):
        total = over_y(y_ordered(value, 0))
        return swap(core, total, send(total, to_core), 0).astype(f32)

    down_grad = whole(down_slice)
    out_grad = whole(out_slice)
    in_total = over_y(
        jnp.concatenate([y_ordered(in_slice[:block], 1), in_slice[block:]], 0)
    )
    in_mine_total = in_total[:block].reshape(block, 2, 3, dq)
    in_other_total = send(in_total[:block], to_core).reshape(block, 2, 3, dq)
    in_grad = (
        swap(core, in_mine_total, in_other_total, 1)
        .transpose(0, 2, 1, 3)
        .reshape(block, 3 * width)
        .astype(f32)
    )
    small_total = in_total[block, : 5 * block].astype(f32).reshape(5, block)
    gu_total = high_reps(gu_slice)
    gu_other = high_reps(gu_other)
    gu_both = jnp.stack([gu_total, gu_other], 0)
    gu_far = send(gu_both, to_core)

    def gu_out(start):
        own = swap(ybit, gu_both[0][:, start : start + fq], gu_both[1][:, start : start + fq], 1)
        far = swap(ybit, gu_far[0][:, start : start + fq], gu_far[1][:, start : start + fq], 1)
        return swap(core, own, far, 1).astype(f32)

    gate_grad, up_grad = gu_out(0), gu_out(fq)

    def to_natural(value):
        return rows_dot(value, to_rel).astype(bf16)

    return (
        to_natural(block_out),
        to_natural(tokens_grad),
        small_total[0],
        in_grad,
        small_total[2:],
        out_grad,
        small_total[1],
        gate_grad,
        up_grad,
        down_grad,
    )


def solution(mesh):
    in_specs = (
        P(("rep", "shard"), None),
        P("shard"),
        P("shard", None),
        P(None, "shard"),
        P(None, "shard"),
        P("shard"),
        P("shard", None),
        P("shard", None),
        P(None, "shard"),
        P(("rep", "shard"), None),
    )
    out_specs = (
        P(("rep", "shard"), None),
        P(("rep", "shard"), None),
        P("shard"),
        P("shard", None),
        P(None, "shard"),
        P(None, "shard"),
        P("shard"),
        P("shard", None),
        P("shard", None),
        P(None, "shard"),
    )
    body = functools.partial(shards, mesh.shape["rep"], mesh.shape["shard"])
    return jax.shard_map(body, mesh=mesh, in_specs=in_specs, out_specs=out_specs, check_vma=False)
```

time: 747 us -> 654 us (0.88)
  waiting for transfers between devices: 274 us -> 133 us
  other arithmetic: 83.2 us -> 131 us
  matrix products: 232 us -> 197 us
  local copies, waits for them, and re-layouts: 64.8 us -> 92.1 us
    ppermute x86 -> x98, waiting for transfers between devices: 274 us -> 133 us  [send(): return lax.ppermute(value, AXES, perm)]
    convert_element_type x17 -> x45, other arithmetic: 44.8 us -> 82.4 us  [the longest x32 35.4 us: total(): return sum((v.astype(f32) for v in values)).astype(bf16)]
    dot_general x13 -> x11, matrix products: 102 us -> 79.1 us  [rows_dot(): lax.dot_general(left, right, (((1,), (1,)), ((), ())), preferred_element_...]
    slice x17 -> x24, local copies, waits for them, and re-layouts: 8.41 us -> 27 us  [the longest x2 14.4 us: shards(): h[:, j * fq:(j + 1) * fq]]
    concatenate x10 -> x9, other arithmetic: 5.94 us -> 16.6 us  [the longest x4 7.84 us: feed_back(): jnp.concatenate([(grad * up_proj * s * (1.0 + gate_pre * (1.0 - s))).asty...]
    dot_general x13 -> x12, matrix products: 71.3 us -> 64.3 us  [plain_dot(): return jnp.dot(left, right, preferred_element_type=jnp.float32).astype(kind)]
    unnamed x217 -> x332, local copies, waits for them, and re-layouts: 39.9 us -> 46.2 us
    ppermute x86 -> x98, starting transfers between devices: 82.5 us -> 88 us  [send(): return lax.ppermute(value, AXES, perm)]
  transfers between devices with their start and end apart: 86 -> 98, of which waited for: 32 -> 38; matrix products, arithmetic and copies ran while one was open for 38% -> 58% of each run, Pallas kernels for 0% -> 0%
where the time goes in v2:
time: 654 us; the launch traced here: 645 us
  matrix products  197 us (30%)
  waiting for transfers between devices  133 us (20%)
  other arithmetic  131 us (20%)
  local copies, waits for them, and re-layouts  92.1 us (14%)
  starting transfers between devices  88 us (13%)
    ppermute x98, waiting for transfers between devices, send(): return lax.ppermute(value, AXES, perm)  133 us
    ppermute x98, starting transfers between devices, send(): return lax.ppermute(value, AXES, perm)  88 us
    dot_general x11, matrix products, rows_dot(): lax.dot_general(left, right, (((1,), (1,)), ((), ())), preferred_element_...  79.1 us
    dot_general x12, matrix products, plain_dot(): return jnp.dot(left, right, preferred_element_type=jnp.float32).astype(kind)  64.3 us
    dot_general x11, matrix products, cols_dot(): lax.dot_general(left, right, (((0,), (0,)), ((), ())), preferred_element_...  52.5 us
    unnamed x332, local copies, waits for them, and re-layouts  46.2 us
    convert_element_type x32, other arithmetic, total(): return sum((v.astype(f32) for v in values)).astype(bf16)  35.4 us
    convert_element_type x4, other arithmetic, feed_back(): (grad * up_proj * s * (1.0 + gate_pre * (1.0 - s))).astype(bf16)  19.1 us
  transfers between devices with their start and end apart: 98, of which 38 were waited for; matrix products, arithmetic and copies ran while one was open for 58% of the time, Pallas kernels for 0%

profile of v2, /device:TPU:0, one launch (start us, length us, event | category | flops | bytes accessed | tf_op | source)
XLA Modules:
  0.0 644.7 jit_solution(1590708580339293138)
XLA Ops:
  37.9 7.5 %collective-permute-done.2 = bf16[144,1536]{1,0:T(8,128)(2,1)S(1)} collective-permute-done((bf16[144,1536]{1,0:T(8,128)(2,1)}, bf16[144,1536]{1,0:T(8,128)(2,1)S(1)}, u32[]{:S(2)}, u32[]{:S(2)}) %collective-permute-start.2) | collective-permute-done | bytes 442400 | tf_op jit(solution)/shard_map/ppermute | solution.py:95
  52.8 7.5 %collective-permute-done.6 = bf16[144,1536]{1,0:T(8,128)(2,1)S(1)} collective-permute-done((bf16[144,1536]{1,0:T(8,128)(2,1)S(1)}, bf16[144,1536]{1,0:T(8,128)(2,1)S(1)}, u32[]{:S(2)}, u32[]{:S(2)}) %collective-permute-start.6) | collective-permute-done | bytes 442400 | tf_op jit(solution)/shard_map/ppermute | solution.py:95
  69.8 6.5 %collective-permute-done.11 = bf16[144,1536]{1,0:T(8,128)(2,1)S(1)} collective-permute-done((bf16[144,1536]{1,0:T(8,128)(2,1)}, bf16[144,1536]{1,0:T(8,128)(2,1)S(1)}, u32[]{:S(2)}, u32[]{:S(2)}) %collective-permute-start.11) | collective-permute-done | bytes 442400 | tf_op jit(solution)/shard_map/ppermute | solution.py:95
  110.4 9.1 %collective-permute-done.18 = bf16[128,2304]{1,0:T(8,128)(2,1)} collective-permute-done((bf16[128,2304]{1,0:T(8,128)(2,1)S(1)}, bf16[128,2304]{1,0:T(8,128)(2,1)}, u32[]{:S(2)}, u32[]{:S(2)}) %collective-permute-start.18) | collective-permute-done | bytes 589856 | tf_op jit(solution)/shard_map/ppermute | solution.py:95
  212.6 12.0 %collective-permute-done.37 = bf16[2304,128]{1,0:T(8,128)(2,1)S(1)} collective-permute-done((bf16[2304,128]{1,0:T(8,128)(2,1)S(1)}, bf16[2304,128]{1,0:T(8,128)(2,1)S(1)}, u32[]{:S(2)}, u32[]{:S(2)}) %collective-permute-start.37) | collective-permute-done | bytes 589856 | tf_op jit(solution)/shard_map/ppermute | solution.py:95
  228.8 9.9 %fusion.97 = f32[1024,2304]{1,0:T(8,128)} fusion(bf16[1024,1024]{0,1:T(8,128)(2,1)S(1)} %copy-done.32, bf16[2304,1024]{1,0:T(8,128)(2,1)} %constant_dynamic-update-slice_fusion.31), kind=kOutput, calls=%fused_computation.337 | convolution fusion | flops 4831838208 | bytes 16252928 | tf_op jit(solution)/shard_map/dot_general | solution.py:22
  248.6 8.3 %fusion.98 = f32[1024,2304]{1,0:T(8,128)S(1)} fusion(bf16[1024,1024]{0,1:T(8,128)(2,1)} %copy-done.40, bf16[1024,2304]{1,0:T(8,128)(2,1)} %constant_dynamic-update-slice_fusion.39), kind=kOutput, calls=%fused_computation.338 | convolution fusion | flops 4831838208 | bytes 16252928 | tf_op jit(solution)/shard_map/dot_general | solution.py:18
  264.8 7.6 %fusion.99 = f32[1024,2304]{1,0:T(8,128)S(1)} fusion(bf16[1024,1024]{0,1:T(8,128)(2,1)S(1)} %copy-done.41, bf16[1024,2304]{1,0:T(8,128)(2,1)} %collective-permute-done.41), kind=kOutput, calls=%fused_computation.339 | convolution fusion | flops 4831838208 | bytes 16252928 | tf_op jit(solution)/shard_map/dot_general | solution.py:18
  279.6 9.9 %fusion.100 = f32[1024,2304]{1,0:T(8,128)} fusion(bf16[1024,1024]{0,1:T(8,128)(2,1)S(1)} %copy-done.32, bf16[2304,1024]{1,0:T(8,128)(2,1)} %collective-permute-done.40), kind=kOutput, calls=%fused_computation.340 | convolution fusion | flops 4831838208 | bytes 16252928 | tf_op jit(solution)/shard_map/dot_general | solution.py:22
  289.5 8.0 %fusion.78 = (f32[1024,1152]{1,0:T(8,128)}, f32[1024,1152]{1,0:T(8,128)}) fusion(f32[1024,2304]{1,0:T(8,128)} %fusion.100), kind=kLoop, calls=%fused_computation.318 | loop fusion | bytes 18874368 | tf_op jit(solution)/shard_map/slice | solution.py:372
  307.7 9.2 %convolution_convert_fusion.3 = bf16[1024,2304]{1,0:T(8,128)(2,1)} fusion(bf16[1024,1024]{0,1:T(8,128)(2,1)} %copy-done.40, bf16[1024,1152]{1,0:T(8,128)(2,1)S(1)} %get-tuple-element.418, bf16[1024,1152]{1,0:T(8,128)(2,1)S(1)} %get-tuple-element.417), kind=kOutput, calls=%fused_computation.4 | convolution fusion | flops 4843634688 | bytes 11534336 | tf_op jit(solution)/shard_map/dot_general | solution.py:28
  323.6 7.3 %convolution_convert_fusion.2 = bf16[1024,2304]{1,0:T(8,128)(2,1)S(1)} fusion(bf16[1024,1024]{0,1:T(8,128)(2,1)} %copy-done.40, bf16[1024,1152]{1,0:T(8,128)(2,1)S(1)} %get-tuple-element.416, bf16[1024,1152]{1,0:T(8,128)(2,1)S(1)} %get-tuple-element.415), kind=kOutput, calls=%fused_computation.3 | convolution fusion | flops 4843634688 | bytes 11534336 | tf_op jit(solution)/shard_map/dot_general | solution.py:28
  342.7 8.0 %collective-permute-done.49 = bf16[128,2304]{1,0:T(8,128)(2,1)S(1)} collective-permute-done((bf16[128,2304]{1,0:T(8,128)(2,1)S(1)}, bf16[128,2304]{1,0:T(8,128)(2,1)S(1)}, u32[]{:S(2)}, u32[]{:S(2)}) %collective-permute-start.49) | collective-permute-done | bytes 589856 | tf_op jit(solution)/shard_map/ppermute | solution.py:95
  353.7 6.7 %convolution_convert_fusion.1 = bf16[1024,2304]{1,0:T(8,128)(2,1)} fusion(bf16[1024,1024]{0,1:T(8,128)(2,1)S(1)} %copy-done.42, bf16[1024,1152]{1,0:T(8,128)(2,1)S(1)} %get-tuple-element.412, bf16[1024,1152]{1,0:T(8,128)(2,1)S(1)} %get-tuple-element.411), kind=kOutput, calls=%fused_computation.2 | convolution fusion | flops 4843634688 | bytes 11534336 | tf_op jit(solution)/shard_map/dot_general | solution.py:28
  389.7 7.1 %fusion.101 = f32[1024,1024]{0,1:T(8,128)S(1)} fusion(bf16[1024,2304]{1,0:T(8,128)(2,1)S(1)} %bitcast.183, bf16[1024,2304]{1,0:T(8,128)(2,1)} %collective-permute-done.41), kind=kOutput, calls=%fused_computation.341 | convolution fusion | flops 4831838208 | bytes 13631488 | tf_op jit(solution)/shard_map/dot_general | solution.py:22
  396.8 9.2 %convolution_add_fusion = f32[1024,1024]{0,1:T(8,128)} fusion(f32[1024,1024]{0,1:T(8,128)S(1)} %fusion.101, bf16[1024,2304]{1,0:T(8,128)(2,1)S(1)} %bitcast.185, bf16[1024,2304]{1,0:T(8,128)(2,1)} %constant_dynamic-update-slice_fusion.39), kind=kOutput, calls=%fused_computation.84 | convolution fusion | flops 4832886784 | bytes 17825792 | tf_op jit(solution)/shard_map/dot_general | solution.py:22
  410.8 9.0 %fusion.102 = f32[1024,1024]{0,1:T(8,128)} fusion(bf16[1024,2304]{1,0:T(8,128)(2,1)S(1)} %pad_maximum_fusion.3, bf16[1024,2304]{1,0:T(8,128)(2,1)} %copy-done.88), kind=kOutput, calls=%fused_computation.342 | convolution fusion | flops 4831838208 | bytes 13631488 | tf_op jit(solution)/shard_map/dot_general | solution.py:22
  419.8 9.9 %multiply_reduce_fusion.5 = (bf16[1024]{0:T(1024)(128)(2,1)S(1)}, f32[1024]{0:T(1024)S(1)}, f32[1024,1024]{0,1:T(8,128)S(1)}) fusion(f32[1024,1024]{0,1:T(8,128)S(1)} %copy-done.10, f32[1024]{0:T(1024)S(1)} %copy-done.91, f32[1024]{0:T(1024)S(1)} %bitcast.205, f32[1024,1024]{0,1:T(8,128)} %convolution_add_fusion, f32[1024,1024]{0,1:T(8,128)} %fusion.102, ...), kind=kOutput, calls=%fused_computation.54 | convolution fusion | flops 4840224768 | bytes 26228736 | tf_op jit(solution)/shard_map/dot_general | solution.py:22
  468.9 7.2 %multiply_add_fusion = f32[2,512,1024]{2,1,0:T(8,128)} fusion(f32[2,510,1024]{2,1,0:T(8,128)} %slice.929, f32[2,511,1024]{2,1,0:T(8,128)} %slice.928, f32[2,512,1024]{2,1,0:T(8,128)S(1)} %bitcast.166, f32[1024]{0:T(1024)S(1)} %bitcast.201, f32[1024]{0:T(1024)S(1)} %bitcast.203, f32[1024]{0:T(1024)S(1)} %bitcast.199), kind=kLoop, calls=%fused_computation.53 | loop fusion | flops 5242880 | bytes 16764928 | tf_op jit(solution)/shard_map/add | solution.py:460
  521.8 9.0 %multiply_reduce_fusion = (f32[1024]{0:T(1024)S(1)}, bf16[1024]{0:T(1024)(128)(2,1)S(1)}, f32[1024,1024]{0,1:T(8,128)S(1)}) fusion(f32[1024,1024]{0,1:T(8,128)S(1)} %copy-done.8, f32[1024]{0:T(1024)S(1)} %bitcast.208, f32[1024]{0:T(1024)S(1)} %copy-done.101, f32[1024,1024]{0,1:T(8,128)} %fusion.104, bf16[1024,1536]{1,0:T(8,128)(2,1)} %copy-done.87, ...), kind=kOutput, calls=%fused_computation.47 | convolution fusion | flops 3228563456 | bytes 18888704 | tf_op jit(solution)/shard_map/dot_general | solution.py:22
  542.5 10.3 %collective-permute-done.78 = bf16[128,2304]{1,0:T(8,128)(2,1)S(1)} collective-permute-done((bf16[128,2304]{1,0:T(8,128)(2,1)S(1)}, bf16[128,2304]{1,0:T(8,128)(2,1)S(1)}, u32[]{:S(2)}, u32[]{:S(2)}) %collective-permute-start.78) | collective-permute-done | bytes 589856 | tf_op jit(solution)/shard_map/ppermute | solution.py:95
  561.9 9.2 %fusion.4 = f32[1024,1024]{0,1:T(8,128)} fusion(bf16[2304,1024]{1,0:T(8,128)(2,1)} %constant_dynamic-update-slice_fusion.31, bf16[1024,1152]{1,0:T(8,128)(2,1)S(1)} %copy-done.22, bf16[1024,1152]{1,0:T(8,128)(2,1)S(1)} %copy-done.18), kind=kOutput, calls=%fused_computation.13 | convolution fusion | flops 4841275392 | bytes 13631488 | tf_op jit(solution)/shard_map/dot_general | solution.py:18
  571.1 8.5 %add_convert_fusion = bf16[1024,1024]{0,1:T(8,128)(2,1)S(1)} fusion(f32[1024,1024]{0,1:T(8,128)S(1)} %copy-done.10, f32[1024,1024]{0,1:T(8,128)} %fusion.4, bf16[2304,1024]{1,0:T(8,128)(2,1)} %collective-permute-done.40, bf16[1024,1152]{1,0:T(8,128)(2,1)S(1)} %copy-done.24, bf16[1024,1152]{1,0:T(8,128)(2,1)S(1)} %copy-done.20), kind=kOutput, calls=%fused_computation.45 | convolution fusion | flops 4844421120 | bytes 19922944 | tf_op jit(solution)/shard_map/dot_general | solution.py:18
  605.2 8.4 %collective-permute-done.87 = bf16[144,1536]{1,0:T(8,128)(2,1)S(1)} collective-permute-done((bf16[144,1536]{1,0:T(8,128)(2,1)S(1)}, bf16[144,1536]{1,0:T(8,128)(2,1)S(1)}, u32[]{:S(2)}, u32[]{:S(2)}) %collective-permute-start.87) | collective-permute-done | bytes 442400 | tf_op jit(solution)/shard_map/ppermute | solution.py:95
  (697 shorter events, 435.8 us)
Async XLA Ops:
  4.5 23.7 %collective-permute-start.1 = (bf16[144,1536]{1,0:T(8,128)(2,1)}, bf16[144,1536]{1,0:T(8,128)(2,1)}, u32[]{:S(2)}, u32[]{:S(2)}) collective-permute-start(bf16[144,1536]{1,0:T(8,128)(2,1)} %copy.63), channel_id=1, source_target_pairs={{0,2},{1,0},{2,4},{3,1},{4,6},{5,3},{6,7},{7,5},{8,10},{9,8},{10,1... | collective-permute-start | bytes 1327112 | tf_op jit(solution)/shard_map/ppermute | solution.py:95
  8.5 20.9 %collective-permute-start = (bf16[144,1536]{1,0:T(8,128)(2,1)}, bf16[144,1536]{1,0:T(8,128)(2,1)}, u32[]{:S(2)}, u32[]{:S(2)}) collective-permute-start(bf16[144,1536]{1,0:T(8,128)(2,1)} %copy.62), channel_id=1, source_target_pairs={{0,1},{1,3},{2,0},{3,5},{4,2},{5,7},{6,4},{7,6},{8,9},{9,11},{10,8... | collective-permute-start | bytes 1327112 | tf_op jit(solution)/shard_map/ppermute | solution.py:95
  77.5 25.8 %collective-permute-start.16 = (bf16[1024,1536]{0,1:T(8,128)(2,1)}, bf16[1024,1536]{0,1:T(8,128)(2,1)S(1)}, u32[]{:S(2)}, u32[]{:S(2)}) collective-permute-start(bf16[1024,1536]{0,1:T(8,128)(2,1)} %constant_dynamic-update-slice_fusion), channel_id=1, source_target_pairs={{0,8},{1,9},{2,10},{3,11},{4,12},{5,13},{6,14},{7,15},{8,0},{9,1},... | collective-permute-start | bytes 9437192 | tf_op jit(solution)/shard_map/ppermute | solution.py:95
  153.9 22.3 %collective-permute-start.28 = (bf16[1024,2304]{1,0:T(8,128)(2,1)S(1)}, bf16[1024,2304]{1,0:T(8,128)(2,1)S(1)}, u32[]{:S(2)}, u32[]{:S(2)}) collective-permute-start(bf16[1024,2304]{1,0:T(8,128)(2,1)S(1)} %constant_dynamic-update-slice_fusion.23), channel_id=1, source_target_pairs={{0,8},{1,9},{2,10},{3,11},{4,12},{5,13},{6,14},{7,15},{8,0},{9,1},... | collective-permute-start | bytes 14155784 | tf_op jit(solution)/shard_map/ppermute | solution.py:95
  226.7 19.8 %collective-permute-start.40 = (bf16[2304,1024]{1,0:T(8,128)(2,1)}, bf16[2304,1024]{1,0:T(8,128)(2,1)}, u32[]{:S(2)}, u32[]{:S(2)}) collective-permute-start(bf16[2304,1024]{1,0:T(8,128)(2,1)} %constant_dynamic-update-slice_fusion.31), channel_id=1, source_target_pairs={{0,8},{1,9},{2,10},{3,11},{4,12},{5,13},{6,14},{7,15},{8,0},{9,1},... | collective-permute-start | bytes 14155784 | tf_op jit(solution)/shard_map/ppermute | solution.py:95
  226.8 19.7 %collective-permute-start.41 = (bf16[1024,2304]{1,0:T(8,128)(2,1)}, bf16[1024,2304]{1,0:T(8,128)(2,1)}, u32[]{:S(2)}, u32[]{:S(2)}) collective-permute-start(bf16[1024,2304]{1,0:T(8,128)(2,1)} %constant_dynamic-update-slice_fusion.39), channel_id=1, source_target_pairs={{0,8},{1,9},{2,10},{3,11},{4,12},{5,13},{6,14},{7,15},{8,0},{9,1},... | collective-permute-start | bytes 14155784 | tf_op jit(solution)/shard_map/ppermute | solution.py:95
  277.4 20.1 %collective-permute-start.46 = (bf16[1152,128]{1,0:T(8,128)(2,1)S(1)}, bf16[1152,128]{1,0:T(8,128)(2,1)S(1)}, u32[]{:S(2)}, u32[]{:S(2)}) collective-permute-start(bf16[1152,128]{1,0:T(8,128)(2,1)S(1)} %get-tuple-element.259), channel_id=1, source_target_pairs={{0,1},{1,3},{2,0},{3,5},{4,2},{5,7},{6,4},{7,6},{8,9},{9,11},{10,8... | collective-permute-start | bytes 884744 | tf_op jit(solution)/shard_map/ppermute | solution.py:95
  385.8 20.3 %collective-permute-start.56 = (bf16[1152,128]{1,0:T(8,128)(2,1)S(1)}, bf16[1152,128]{1,0:T(8,128)(2,1)S(1)}, u32[]{:S(2)}, u32[]{:S(2)}) collective-permute-start(bf16[1152,128]{1,0:T(8,128)(2,1)S(1)} %get-tuple-element.288), channel_id=1, source_target_pairs={{0,1},{1,3},{2,0},{3,5},{4,2},{5,7},{6,4},{7,6},{8,9},{9,11},{10,8... | collective-permute-start | bytes 884744 | tf_op jit(solution)/shard_map/ppermute | solution.py:95
  386.3 19.8 %collective-permute-start.57 = (bf16[1152,128]{1,0:T(8,128)(2,1)S(1)}, bf16[1152,128]{1,0:T(8,128)(2,1)S(1)}, u32[]{:S(2)}, u32[]{:S(2)}) collective-permute-start(bf16[1152,128]{1,0:T(8,128)(2,1)S(1)} %get-tuple-element.289), channel_id=1, source_target_pairs={{0,2},{1,0},{2,4},{3,1},{4,6},{5,3},{6,7},{7,5},{8,10},{9,8},{10,1... | collective-permute-start | bytes 884744 | tf_op jit(solution)/shard_map/ppermute | solution.py:95
  408.0 28.2 %collective-permute-start.59 = (bf16[1152,128]{1,0:T(8,128)(2,1)}, bf16[1152,128]{1,0:T(8,128)(2,1)}, u32[]{:S(2)}, u32[]{:S(2)}) collective-permute-start(bf16[1152,128]{1,0:T(8,128)(2,1)} %get-tuple-element.295), channel_id=1, source_target_pairs={{0,1},{1,3},{2,0},{3,5},{4,2},{5,7},{6,4},{7,6},{8,9},{9,11},{10,8... | collective-permute-start | bytes 884744 | tf_op jit(solution)/shard_map/ppermute | solution.py:95
  408.3 27.9 %collective-permute-start.60 = (bf16[1152,128]{1,0:T(8,128)(2,1)}, bf16[1152,128]{1,0:T(8,128)(2,1)}, u32[]{:S(2)}, u32[]{:S(2)}) collective-permute-start(bf16[1152,128]{1,0:T(8,128)(2,1)} %get-tuple-element.296), channel_id=1, source_target_pairs={{0,2},{1,0},{2,4},{3,1},{4,6},{5,3},{6,7},{7,5},{8,10},{9,8},{10,1... | collective-permute-start | bytes 884744 | tf_op jit(solution)/shard_map/ppermute | solution.py:95
  410.1 27.5 %collective-permute-start.61 = (bf16[128,2304]{1,0:T(8,128)(2,1)S(1)}, bf16[128,2304]{1,0:T(8,128)(2,1)}, u32[]{:S(2)}, u32[]{:S(2)}) collective-permute-start(bf16[128,2304]{1,0:T(8,128)(2,1)S(1)} %get-tuple-element.305), channel_id=1, source_target_pairs={{0,16},{1,17},{2,18},{3,19},{4,20},{5,21},{6,22},{7,23},{8,24},{9,... | collective-permute-start | bytes 1769480 | tf_op jit(solution)/shard_map/ppermute | solution.py:95
  450.5 35.6 %collective-permute-start.96 = (bf16[2304,128]{1,0:T(8,128)(2,1)S(1)}, bf16[2304,128]{1,0:T(8,128)(2,1)}, u32[]{:S(2)}, u32[]{:S(2)}) collective-permute-start(bf16[2304,128]{1,0:T(8,128)(2,1)S(1)} %maximum_select_fusion.8), channel_id=1, source_target_pairs={{0,16},{1,17},{2,18},{3,19},{4,20},{5,21},{6,22},{7,23},{8,24},{9,... | collective-permute-start | bytes 1769480 | tf_op jit(solution)/shard_map/ppermute | solution.py:95
  466.5 26.0 %collective-permute-start.68 = (bf16[128,2304]{1,0:T(8,128)(2,1)}, bf16[128,2304]{1,0:T(8,128)(2,1)}, u32[]{:S(2)}, u32[]{:S(2)}) collective-permute-start(bf16[128,2304]{1,0:T(8,128)(2,1)} %get-tuple-element.320), channel_id=1, source_target_pairs={{0,16},{1,17},{2,18},{3,19},{4,20},{5,21},{6,22},{7,23},{8,24},{9,... | collective-permute-start | bytes 1769480 | tf_op jit(solution)/shard_map/ppermute | solution.py:95
  467.8 23.4 %collective-permute-start.67 = (bf16[512,1024]{1,0:T(8,128)(2,1)}, bf16[512,1024]{1,0:T(8,128)(2,1)}, u32[]{:S(2)}, u32[]{:S(2)}) collective-permute-start(bf16[512,1024]{1,0:T(8,128)(2,1)} %slice.924), channel_id=1, source_target_pairs={{0,8},{1,9},{2,10},{3,11},{4,12},{5,13},{6,14},{7,15},{8,0},{9,1},... | collective-permute-start | bytes 3145736 | tf_op jit(solution)/shard_map/ppermute | solution.py:95
  514.1 26.5 %collective-permute-start.75 = (bf16[512,128]{1,0:T(8,128)(2,1)}, bf16[512,128]{1,0:T(8,128)(2,1)}, u32[]{:S(2)}, u32[]{:S(2)}) collective-permute-start(bf16[512,128]{1,0:T(8,128)(2,1)} %get-tuple-element.336), channel_id=1, source_target_pairs={{0,1},{1,3},{2,0},{3,5},{4,2},{5,7},{6,4},{7,6},{8,9},{9,11},{10,8... | collective-permute-start | bytes 393224 | tf_op jit(solution)/shard_map/ppermute | solution.py:95
  514.6 26.0 %collective-permute-start.76 = (bf16[512,128]{1,0:T(8,128)(2,1)}, bf16[512,128]{1,0:T(8,128)(2,1)}, u32[]{:S(2)}, u32[]{:S(2)}) collective-permute-start(bf16[512,128]{1,0:T(8,128)(2,1)} %get-tuple-element.337), channel_id=1, source_target_pairs={{0,2},{1,0},{2,4},{3,1},{4,6},{5,3},{6,7},{7,5},{8,10},{9,8},{10,1... | collective-permute-start | bytes 393224 | tf_op jit(solution)/shard_map/ppermute | solution.py:95
  516.2 26.4 %collective-permute-start.77 = (bf16[128,2304]{1,0:T(8,128)(2,1)}, bf16[128,2304]{1,0:T(8,128)(2,1)}, u32[]{:S(2)}, u32[]{:S(2)}) collective-permute-start(bf16[128,2304]{1,0:T(8,128)(2,1)} %get-tuple-element.338), channel_id=1, source_target_pairs={{0,1},{1,3},{2,0},{3,5},{4,2},{5,7},{6,4},{7,6},{8,9},{9,11},{10,8... | collective-permute-start | bytes 1769480 | tf_op jit(solution)/shard_map/ppermute | solution.py:95
  516.6 39.0 %collective-permute-start.73 = (bf16[1024,1536]{1,0:T(8,128)(2,1)}, bf16[1024,1536]{1,0:T(8,128)(2,1)S(1)}, u32[]{:S(2)}, u32[]{:S(2)}) collective-permute-start(bf16[1024,1536]{1,0:T(8,128)(2,1)} %convolution_convert_fusion.8), channel_id=1, source_target_pairs={{0,8},{1,9},{2,10},{3,11},{4,12},{5,13},{6,14},{7,15},{8,0},{9,1},... | collective-permute-start | bytes 9437192 | tf_op jit(solution)/shard_map/ppermute | solution.py:95
  557.3 26.2 %collective-permute-start.80 = (bf16[512,128]{1,0:T(8,128)(2,1)}, bf16[512,128]{1,0:T(8,128)(2,1)S(1)}, u32[]{:S(2)}, u32[]{:S(2)}) collective-permute-start(bf16[512,128]{1,0:T(8,128)(2,1)} %get-tuple-element.349), channel_id=1, source_target_pairs={{0,1},{1,3},{2,0},{3,5},{4,2},{5,7},{6,4},{7,6},{8,9},{9,11},{10,8... | collective-permute-start | bytes 393224 | tf_op jit(solution)/shard_map/ppermute | solution.py:95
  558.9 24.7 %collective-permute-start.81 = (bf16[512,128]{1,0:T(8,128)(2,1)S(1)}, bf16[512,128]{1,0:T(8,128)(2,1)S(1)}, u32[]{:S(2)}, u32[]{:S(2)}) collective-permute-start(bf16[512,128]{1,0:T(8,128)(2,1)S(1)} %get-tuple-element.350), channel_id=1, source_target_pairs={{0,2},{1,0},{2,4},{3,1},{4,6},{5,3},{6,7},{7,5},{8,10},{9,8},{10,1... | collective-permute-start | bytes 393224 | tf_op jit(solution)/shard_map/ppermute | solution.py:95
  559.4 25.4 %collective-permute-start.79 = (bf16[144,1536]{1,0:T(8,128)(2,1)S(1)}, bf16[144,1536]{1,0:T(8,128)(2,1)S(1)}, u32[]{:S(2)}, u32[]{:S(2)}) collective-permute-start(bf16[144,1536]{1,0:T(8,128)(2,1)S(1)} %add_convert_fusion.27), channel_id=1, source_target_pairs={{0,1},{1,3},{2,0},{3,5},{4,2},{5,7},{6,4},{7,6},{8,9},{9,11},{10,8... | collective-permute-start | bytes 1327112 | tf_op jit(solution)/shard_map/ppermute | solution.py:95
  560.9 24.2 %collective-permute-start.82 = (bf16[128,2304]{1,0:T(8,128)(2,1)S(1)}, bf16[128,2304]{1,0:T(8,128)(2,1)S(1)}, u32[]{:S(2)}, u32[]{:S(2)}) collective-permute-start(bf16[128,2304]{1,0:T(8,128)(2,1)S(1)} %add_convert_fusion.3), channel_id=1, source_target_pairs={{0,16},{1,17},{2,18},{3,19},{4,20},{5,21},{6,22},{7,23},{8,24},{9,... | collective-permute-start | bytes 1769480 | tf_op jit(solution)/shard_map/ppermute | solution.py:95
  585.2 32.8 %collective-permute-start.95 = (bf16[2,128,2304]{2,1,0:T(8,128)(2,1)S(1)}, bf16[2,128,2304]{2,1,0:T(8,128)(2,1)S(1)}, u32[]{:S(2)}, u32[]{:S(2)}) collective-permute-start(bf16[2,128,2304]{2,1,0:T(8,128)(2,1)S(1)} %pad_maximum_fusion.8), channel_id=1, source_target_pairs={{0,8},{1,9},{2,10},{3,11},{4,12},{5,13},{6,14},{7,15},{8,0},{9,1},... | collective-permute-start | bytes 3538952 | tf_op jit(solution)/shard_map/ppermute | solution.py:95
  (214 other events, 2693.6 us)

commit v3 on v2

v3 whole, which is shorter than its diff:
```python
import functools

import jax
import jax.numpy as jnp
from jax import lax
from jax.experimental import pallas as pl
from jax.experimental.pallas import tpu as pltpu
from jax.sharding import PartitionSpec as P

SEQ = 512


EPSILON = 1e-05

AXES = ("rep", "shard")
PACK = 16


def plain_dot(left, right, kind=jnp.float32):
    return jnp.dot(left, right, preferred_element_type=jnp.float32).astype(kind)


def rows_dot(left, right):
    return lax.dot_general(
        left, right, (((1,), (1,)), ((), ())), preferred_element_type=jnp.float32
    )


def cols_dot(left, right):
    return lax.dot_general(
        left, right, (((0,), (0,)), ((), ())), preferred_element_type=jnp.float32
    ).astype(jnp.bfloat16)


def kernel_call(body, steps, ins, outs):
    return pl.pallas_call(
        body,
        grid=(steps,),
        in_specs=[pl.BlockSpec(block, where) for _, block, where in ins],
        out_specs=[pl.BlockSpec(block, where) for _, _, block, where in outs],
        out_shape=[jax.ShapeDtypeStruct(shape, kind) for shape, kind, _, _ in outs],
        compiler_params=pltpu.CompilerParams(vmem_limit_bytes=56 * 2**20),
    )(*[v for v, _, _ in ins])


def same(n):
    return (0, 0)


def columns(n):
    return (0, n)


def rows(n):
    return (n, 0)


def gathered(piece_refs, weight_ref):
    extent = piece_refs[0].shape[0]
    for n, piece_ref in enumerate(piece_refs):
        weight_ref[n * extent : (n + 1) * extent, :] = piece_ref[...]


def feed(normed, pieces, tiles):
    count, depth = normed.shape
    extent = depth // len(pieces)
    pair = pieces[0].shape[1] // tiles
    tile = pair // 2

    def body(normed_ref, *refs):
        *piece_refs, pre_ref, hidden_ref, weight_ref = refs
        gathered(piece_refs, weight_ref)
        pre = jnp.dot(normed_ref[...], weight_ref[...], preferred_element_type=jnp.float32)
        pre_ref[...] = pre.astype(jnp.bfloat16)
        gate = pre[:, :tile]
        hidden_ref[...] = (gate * jax.nn.sigmoid(gate) * pre[:, tile:]).astype(jnp.bfloat16)

    return kernel_call(
        body,
        tiles,
        [(normed, (count, depth), same)] + [(v, (extent, pair), columns) for v in pieces],
        [
            ((count, tiles * pair), jnp.bfloat16, (count, pair), columns),
            ((count, tiles * tile), jnp.bfloat16, (count, tile), columns),
            ((depth, tiles * pair), jnp.bfloat16, (depth, pair), columns),
        ],
    )


def feed_back(cot, down_rows, pre, normed, tiles, first):
    count, depth = cot.shape
    pair = pre.shape[1] // tiles
    tile = pair // 2

    def body(cot_ref, down_ref, pre_ref, normed_ref, back_ref, local_ref):
        grad = rows_dot(cot_ref[...], down_ref[...])
        gate = pre_ref[:, :tile].astype(jnp.float32)
        up = pre_ref[:, tile:].astype(jnp.float32)
        sigma = jax.nn.sigmoid(gate)
        back_ref[:, :tile] = (grad * up * sigma * (1.0 + gate * (1.0 - sigma))).astype(jnp.bfloat16)
        back_ref[:, tile:] = (grad * gate * sigma).astype(jnp.bfloat16)
        local_ref[...] = cols_dot(normed_ref[...], back_ref[...])

    return kernel_call(
        body,
        tiles,
        [
            (cot, (count, depth), same),
            (down_rows, (tile, depth), lambda n: (n + first, 0)),
            (pre, (count, pair), columns),
            (normed, (count, depth), same),
        ],
        [
            ((count, tiles * pair), jnp.bfloat16, (count, pair), columns),
            ((depth, tiles * pair), jnp.bfloat16, (depth, pair), columns),
        ],
    )


def shifted(values, steps):
    count = values.shape[0]
    at = lax.broadcasted_iota(jnp.int32, values.shape, 0) % SEQ
    inside = (at >= steps) & (at < SEQ + steps)
    return jnp.where(inside, pltpu.roll(values, steps % count, 0), 0.0)


def convolve(normed, pieces, taps, tiles):
    count, depth = normed.shape
    extent = depth // len(pieces)
    triple = pieces[0].shape[1] // tiles
    tile = triple // 3

    def body(normed_ref, taps_ref, *refs):
        *piece_refs, parts_ref, gated_ref, weight_ref = refs
        gathered(piece_refs, weight_ref)
        parts = jnp.dot(normed_ref[...], weight_ref[...], preferred_element_type=jnp.float32)
        parts_ref[...] = parts.astype(jnp.bfloat16)
        mixed = parts[:, :tile] * parts[:, 2 * tile :]
        conv = (
            taps_ref[0:1, :] * shifted(mixed, 2)
            + taps_ref[1:2, :] * shifted(mixed, 1)
            + taps_ref[2:3, :] * mixed
        )
        gated_ref[...] = (parts[:, tile : 2 * tile] * conv).astype(jnp.bfloat16)

    return kernel_call(
        body,
        tiles,
        [(normed, (count, depth), same), (taps, (3, tile), columns)]
        + [(v, (extent, triple), columns) for v in pieces],
        [
            ((count, tiles * triple), jnp.bfloat16, (count, triple), columns),
            ((count, tiles * tile), jnp.bfloat16, (count, tile), columns),
            ((depth, tiles * triple), jnp.bfloat16, (depth, triple), columns),
        ],
    )


def convolve_back(branch_back, out_rows, parts, gated, taps, normed, tiles):
    count, depth = branch_back.shape
    triple = parts.shape[1] // tiles
    tile = triple // 3

    def body(
        branch_ref, out_ref, parts_ref, gated_ref, taps_ref, normed_ref,
        back_ref, local_ref, taps_local_ref,
    ):
        gated_grad = rows_dot(branch_ref[...], out_ref[...])
        b_part = parts_ref[:, :tile].astype(jnp.float32)
        c_part = parts_ref[:, tile : 2 * tile].astype(jnp.float32)
        x_part = parts_ref[:, 2 * tile :].astype(jnp.float32)
        mixed = b_part * x_part
        before_1, before_2 = shifted(mixed, 1), shifted(mixed, 2)
        conv = (
            taps_ref[0:1, :] * before_2 + taps_ref[1:2, :] * before_1 + taps_ref[2:3, :] * mixed
        )
        conv_grad = gated_grad * c_part
        taps_local_ref[...] = jnp.concatenate(
            [
                jnp.sum(conv_grad * before_2, 0, keepdims=True),
                jnp.sum(conv_grad * before_1, 0, keepdims=True),
                jnp.sum(conv_grad * mixed, 0, keepdims=True),
            ],
            0,
        )
        mixed_grad = (
            taps_ref[2:3, :] * conv_grad
            + taps_ref[1:2, :] * shifted(conv_grad, -1)
            + taps_ref[0:1, :] * shifted(conv_grad, -2)
        )
        back_ref[:, :tile] = (mixed_grad * x_part).astype(jnp.bfloat16)
        back_ref[:, tile : 2 * tile] = (gated_grad * conv).astype(jnp.bfloat16)
        back_ref[:, 2 * tile :] = (mixed_grad * b_part).astype(jnp.bfloat16)
        local_ref[:, :triple] = cols_dot(normed_ref[...], back_ref[...])
        local_ref[:, triple:] = cols_dot(branch_ref[...], gated_ref[...])

    return kernel_call(
        body,
        tiles,
        [
            (branch_back, (count, depth), same),
            (out_rows, (tile, depth), rows),
            (parts, (count, triple), columns),
            (gated, (count, tile), columns),
            (taps, (3, tile), columns),
            (normed, (count, depth), same),
        ],
        [
            ((count, tiles * triple), jnp.bfloat16, (count, triple), columns),
            ((depth, tiles * 4 * tile), jnp.bfloat16, (depth, 4 * tile), columns),
            ((3, tiles * tile), jnp.float32, (3, tile), columns),
        ],
    )


def norm_back(extra, backs, weights, values, inv_rms, gain, base, width):
    count, depth = values.shape
    total = len(backs)
    per = backs[0].shape[1] // width
    rows_at_once = min(128, count)
    operands = [] if extra is None else [extra]

    def at(q):
        return lambda n: (0, jnp.clip(n - q * per, 0, per - 1))

    def body(*refs):
        back_refs, weight_refs = refs[:total], refs[total : 2 * total]
        values_ref, inv_ref, gain_ref, base_ref = refs[2 * total : 2 * total + 4]
        extra_refs = refs[2 * total + 4 : -3]
        out_ref, gain_grad_ref, sum_ref = refs[-3:]
        n = pl.program_id(0)

        @pl.when(n == 0)
        def _():
            first = rows_dot(back_refs[0][...], weight_refs[0][...])
            sum_ref[...] = first + extra_refs[0][...] if extra_refs else first

        for q in range(total):

            @pl.when((n // per == q) & (n != 0))
            def _(q=q):
                sum_ref[...] += rows_dot(back_refs[q][...], weight_refs[q][...])

        @pl.when(n == total * per - 1)
        def _():
            def some_rows(at_chunk, gain_grad):
                here = pl.ds(pl.multiple_of(at_chunk * rows_at_once, rows_at_once), rows_at_once)
                grad = sum_ref[here, :]
                scaled = grad * gain_ref[...]
                held = values_ref[here, :].astype(jnp.float32)
                inv = inv_ref[here, :]
                mean = jnp.mean(scaled * held, -1, keepdims=True)
                made = inv * (scaled - held * (inv * inv * mean))
                out_ref[here, :] = (base_ref[here, :].astype(jnp.float32) + made).astype(
                    jnp.bfloat16
                )
                return gain_grad + jnp.sum(grad * held * inv, 0, keepdims=True)

            gain_grad_ref[...] = lax.fori_loop(
                0, count // rows_at_once, some_rows, jnp.zeros((1, depth), jnp.float32)
            )

    return pl.pallas_call(
        body,
        grid=(total * per,),
        in_specs=[pl.BlockSpec((count, width), at(q)) for q in range(total)]
        + [pl.BlockSpec((depth, width), at(q)) for q in range(total)]
        + [
            pl.BlockSpec((count, depth), same),
            pl.BlockSpec((count, 1), same),
            pl.BlockSpec((1, depth), same),
            pl.BlockSpec((count, depth), same),
        ]
        + [pl.BlockSpec((count, depth), same) for _ in operands],
        out_specs=[pl.BlockSpec((count, depth), same), pl.BlockSpec((1, depth), same)],
        out_shape=[
            jax.ShapeDtypeStruct((count, depth), jnp.bfloat16),
            jax.ShapeDtypeStruct((1, depth), jnp.float32),
        ],
        scratch_shapes=[pltpu.VMEM((count, depth), jnp.float32)],
        compiler_params=pltpu.CompilerParams(vmem_limit_bytes=56 * 2**20),
    )(*backs, *weights, values, inv_rms, gain[None, :], base, *operands)


def in_order(core, mine, other, quarter):
    block = mine.shape[0]

    def body(core_ref, mine_ref, other_ref, in_ref, out_ref):
        first = core_ref[0, 0] == 0
        halves = [
            jnp.where(first, mine_ref[...], other_ref[...]).astype(jnp.float32),
            jnp.where(first, other_ref[...], mine_ref[...]).astype(jnp.float32),
        ]
        for at in range(4):
            start = (at % 2) * 4 * quarter
            parts = halves[at // 2][:, start : start + 4 * quarter]
            for n in range(3):
                to = (4 * n + at) * quarter
                in_ref[:, to : to + quarter] = parts[:, n * quarter : (n + 1) * quarter]
            out_ref[at * quarter : (at + 1) * quarter, :] = parts[:, 3 * quarter :].T

    return pl.pallas_call(
        body,
        in_specs=[
            pl.BlockSpec(memory_space=pltpu.SMEM),
            pl.BlockSpec(memory_space=pltpu.VMEM),
            pl.BlockSpec(memory_space=pltpu.VMEM),
        ],
        out_specs=[pl.BlockSpec(memory_space=pltpu.VMEM)] * 2,
        out_shape=[
            jax.ShapeDtypeStruct((block, 12 * quarter), jnp.float32),
            jax.ShapeDtypeStruct((4 * quarter, block), jnp.float32),
        ],
        compiler_params=pltpu.CompilerParams(vmem_limit_bytes=56 * 2**20),
    )(core.astype(jnp.int32).reshape(1, 1), mine, other)


def cycle_of(size):
    wide = size // 4
    walk = [(0, 0)]
    for row in range(4):
        cols = range(1, wide)
        walk += [(row, col) for col in (cols if row % 2 == 0 else reversed(cols))]
    walk += [(row, 0) for row in (3, 2, 1)]
    return [row * wide + col for row, col in walk]


def shards(
    reps,
    size,
    tokens,
    norm_gain_one,
    in_weight,
    conv_weight,
    out_weight,
    norm_gain_two,
    gate_weight,
    up_weight,
    down_weight,
    cotangent,
):
    bf16, f32 = jnp.bfloat16, jnp.float32
    width = tokens.shape[1]
    hidden_width = gate_weight.shape[1]
    block = width // size
    fq, dq = hidden_width // 4, width // 4
    tiles = 3 if fq % 384 == 0 else 1
    tile = fq // tiles
    ring = cycle_of(size)
    place = [ring.index(s) for s in range(size)]

    def pairs(move):
        return [
            (r * size + s, move(r, s)[0] * size + move(r, s)[1])
            for r in range(reps)
            for s in range(size)
        ]

    cw = pairs(lambda r, s: (r, ring[(place[s] + 1) % size]))
    ccw = pairs(lambda r, s: (r, ring[(place[s] - 1) % size]))
    to_core = pairs(lambda r, s: (r ^ 1, s))
    to_y = pairs(lambda r, s: (r ^ 2, s))

    def send(value, perm):
        return lax.ppermute(value, AXES, perm)

    rep = lax.axis_index("rep")
    core, ybit = rep % 2, (rep // 2) % 2
    at = jnp.asarray(place)[lax.axis_index("shard")]

    order = [0]
    for step in range(1, size // 2):
        order += [step, size - step]
    order += [size // 2]
    natural_block = jnp.asarray(ring)[(at - jnp.asarray(order)) % size]
    natural = (natural_block[:, None] * block + jnp.arange(block)[None, :]).reshape(-1)
    to_rel = (jnp.arange(width)[:, None] == natural[None, :]).astype(bf16)

    def quarter(i, j):
        return (core ^ i) * 2 + (ybit ^ j)

    quarters = ((0, 0), (0, 1), (1, 0), (1, 1))
    natural_feature = (
        jnp.stack([quarter(i, j) for i, j in quarters])[:, None] * dq + jnp.arange(dq)[None, :]
    ).reshape(-1)

    last = []

    def ordered_round(sends, work=None, args=()):
        leaves, tree = jax.tree.flatten(([v for v, _ in sends], tuple(args)))
        held = lax.optimization_barrier(tuple(leaves) + tuple(last))
        values, args = jax.tree.unflatten(tree, held[: len(leaves)])
        got = [send(v, perm) for v, (_, perm) in zip(values, sends)]
        made = work(*args) if work is not None else None
        last[:] = got + jax.tree.leaves(made)
        return got, made

    class Gather:
        def __init__(self, piece, flip):
            self.got = {0: piece}
            self.n_cw = size // 2 - (1 if flip else 0)
            self.n_ccw = size - 1 - self.n_cw
            self.step = 0

        def sends(self):
            self.step += 1
            self.to = []
            out = []
            if self.step <= self.n_cw:
                out.append((self.got[self.step - 1], cw))
                self.to.append(self.step)
            if self.step <= self.n_ccw:
                out.append((self.got[(size - self.step + 1) % size], ccw))
                self.to.append(size - self.step)
            return out

        def take(self, got):
            for b in self.to:
                self.got[b] = got.pop(0)

        def done(self):
            return self.step == size // 2

        def rows(self):
            return jnp.concatenate([self.got[b] for b in order], 0)

        def cols(self):
            return jnp.concatenate([self.got[b] for b in order], 1)

    class Scatter:
        def __init__(self, own, flip):
            self.own = own
            self.n_cw = size // 2 - (1 if flip else 0)
            self.n_ccw = size - 1 - self.n_cw
            self.step = size // 2 + 1
            self.up = self.down = None

        def sends(self):
            self.step -= 1
            out = []
            if self.step <= self.n_cw:
                out.append((total(*self.own(size - self.step), self.up), cw))
            if self.step <= self.n_ccw:
                out.append((total(*self.own(self.step), self.down), ccw))
            return out

        def take(self, got):
            if self.step <= self.n_cw:
                self.up = got.pop(0)
            if self.step <= self.n_ccw:
                self.down = got.pop(0)

        def done(self):
            return self.step == 1

        def result(self):
            return total(*self.own(0), self.up, self.down)

    def total(*values):
        values = [v for v in values if v is not None]
        if len(values) == 1:
            return values[0]
        return sum(v.astype(f32) for v in values).astype(bf16)

    def add(left, right):
        return total(left, right)

    def both_rounds(rings, others=(), work=None, args=()):
        sends = []
        counts = []
        for r in rings:
            mine = r.sends()
            counts.append(len(mine))
            sends += mine
        got, made = ordered_round(sends + list(others), work, args)
        for r, n in zip(rings, counts):
            r.take(got[:n])
            got = got[n:]
        return got, made

    def finish(*rings):
        while rings := [r for r in rings if not r.done()]:
            both_rounds(rings)

    def high_reps(value):
        step = 4
        while step < reps:
            other = send(value, pairs(lambda r, s: (r ^ step, s)))
            value = (value.astype(f32) + other.astype(f32)).astype(value.dtype)
            step *= 2
        return value

    def part(value, axis, i, j, extent):
        return lax.dynamic_slice_in_dim(value, quarter(i, j) * extent, extent, axis)

    def in_part(i, j):
        return part(in_weight.reshape(block, 3, width), 2, i, j, dq).reshape(block, 3 * dq)

    def gu_part(gate_weight, up_weight, i, j):
        both = [part(gate_weight, 1, i, j, fq), part(up_weight, 1, i, j, fq)]
        return jnp.concatenate(
            [w[:, t * tile : (t + 1) * tile] for t in range(tiles) for w in both], 1
        )

    def half_part(value):
        extent = value.shape[0] // 4
        return jnp.concatenate([part(value, 0, 0, j, extent) for j in range(2)], 0)

    small = jnp.concatenate([norm_gain_one, norm_gain_two, conv_weight.reshape(-1)])
    pack = jnp.pad(small[None, :], ((0, PACK - 1), (0, 6 * dq - small.shape[0])))
    in_ring = Gather(
        jnp.concatenate([jnp.concatenate([in_part(0, 0), in_part(0, 1)], 1), pack], 0), False
    )
    far_order = [b for b in order if b != 0]

    def far_send():
        b = far_order[len(far_pieces) - 1]
        return (gu_ring.got[b], to_y)

    def far_take(value):
        far_pieces[far_order[len(far_pieces) - 1]] = value

    def prepare(tokens, gate_weight, up_weight):
        tokens_rel = plain_dot(tokens, to_rel, bf16)
        values = tokens_rel.astype(f32)
        inv_one = lax.rsqrt(jnp.mean(values * values, -1, keepdims=True) + EPSILON)
        return tokens_rel, inv_one

    _, out_own = both_rounds([in_ring], (), half_part, (out_weight,))
    out_ring = Gather(out_own, True)
    _, (tokens_rel, inv_one) = both_rounds(
        [in_ring, out_ring], (), prepare, (tokens, gate_weight, up_weight)
    )
    _, gu_own = both_rounds(
        [in_ring, out_ring], (), lambda g, u: gu_part(g, u, 0, 0), (gate_weight, up_weight)
    )
    gu_ring = Gather(gu_own, True)
    _, far_own = both_rounds(
        [in_ring, out_ring], (), lambda g, u: gu_part(g, u, 0, 1), (gate_weight, up_weight)
    )
    far_pieces = {0: far_own}
    finish(in_ring)
    in_pieces = [in_ring.got[b] for b in order]
    packs = jnp.stack([v[block, : 5 * block] for v in in_pieces], 0).reshape(size, 5, block)
    gain_one_f = packs[:, 0].reshape(-1).astype(f32)
    gain_two_f = packs[:, 1].reshape(-1).astype(f32)
    to_feature = (natural[:, None] == natural_feature[None, :]).astype(bf16)
    taps = plain_dot(packs[:, 2:].transpose(1, 0, 2).reshape(3, width), to_feature)
    taps_h = (taps[:, : 2 * dq], taps[:, 2 * dq :])

    def project_first(tokens_rel, inv_one, gain, taps, *pieces):
        normed_one = (tokens_rel.astype(f32) * inv_one * gain).astype(bf16)
        return normed_one, convolve(normed_one, pieces, taps, 2)

    _, (normed_one, (parts_0, gated_0, in_half)) = both_rounds(
        [gu_ring, out_ring],
        (),
        project_first,
        (tokens_rel, inv_one, gain_one_f, taps_h[0], *in_pieces),
    )

    def prepare_more(cotangent, down_weight):
        return plain_dot(cotangent, to_rel, bf16), half_part(down_weight)

    finish(out_ring)
    out_half = out_ring.cols()
    (far, in_far, out_far), (cot, down_own) = both_rounds(
        [gu_ring],
        [far_send(), (in_half, to_core), (out_half, to_core)],
        prepare_more,
        (cotangent, down_weight),
    )
    far_take(far)
    down_ring = Gather(down_own, False)
    in_h = (in_half, in_far)

    def project_second(normed_one, weight, taps):
        return convolve(normed_one, [weight], taps, 2)[:2]

    (far,), (parts_1, gated_1) = both_rounds(
        [gu_ring], [far_send()], project_second, (normed_one, in_far, taps_h[1])
    )
    far_take(far)
    parts_h, gated_h = (parts_0, parts_1), (gated_0, gated_1)

    def mid(tokens_rel, g0, w0, g1, w1):
        middle = tokens_rel.astype(f32) + plain_dot(g0, w0) + plain_dot(g1, w1)
        inv_two = lax.rsqrt(jnp.mean(middle * middle, -1, keepdims=True) + EPSILON)
        return middle, inv_two, (middle * inv_two * gain_two_f).astype(bf16)

    gu_q = [None] * 4
    fed = [None] * 4

    def feed_tiles(normed, *pieces):
        return feed(normed, pieces, tiles)

    out_h = (out_half, out_far)
    (far,), (middle, inv_two, normed_two) = both_rounds(
        [gu_ring], [far_send()], mid, (tokens_rel, gated_0, out_half, gated_1, out_far)
    )
    far_take(far)
    finish(gu_ring)
    (far,), fed[0] = both_rounds(
        [down_ring], [far_send()], feed_tiles, (normed_two, *[gu_ring.got[b] for b in order])
    )
    far_take(far)
    gu_q[0] = fed[0][2]

    def down_parts(cot, *hidden):
        return [cols_dot(h, cot) for h in hidden]

    (far, gu_q[2]), (down_00,) = both_rounds(
        [down_ring], [far_send(), (gu_q[0], to_core)], down_parts, (cot, fed[0][1])
    )
    far_take(far)
    (far,), fed[2] = both_rounds([down_ring], [far_send()], feed_tiles, (normed_two, gu_q[2]))
    far_take(far)
    (far,), (down_10,) = both_rounds(
        [down_ring], [far_send()], down_parts, (cot, fed[2][1])
    )
    far_take(far)

    def column(value, b):
        n = order.index(b)
        return value[:, n * block : (n + 1) * block]

    def row(value, b):
        n = order.index(b)
        return value[n * block : (n + 1) * block]

    def col_scatter(mine, other, flip):
        return Scatter(lambda b: (column(mine, b), column(other, b)), flip)

    finish(down_ring)
    while len(far_pieces) < size:
        (far,), _ = ordered_round([far_send()])
        far_take(far)
    down_half = down_ring.cols()
    (down_other, down_far), fed[1] = ordered_round(
        [(down_half, to_core), (down_10, to_core)],
        feed_tiles,
        (normed_two, *[far_pieces[b] for b in order]),
    )
    gu_q[1] = fed[1][2]
    down_s0 = col_scatter(down_00, down_far, True)
    down_h = (down_half, down_other)
    (gu_q[3],), (down_01,) = both_rounds(
        [down_s0], [(gu_q[1], to_core)], down_parts, (cot, fed[1][1])
    )
    _, fed[3] = both_rounds([down_s0], (), feed_tiles, (normed_two, gu_q[3]))

    def feed_back_first(cot, down_rows, pre, normed):
        return feed_back(cot, down_rows, pre, normed, tiles, 0)

    def feed_back_second(cot, down_rows, pre, normed):
        return feed_back(cot, down_rows, pre, normed, tiles, tiles)

    def back_args(n):
        return (cot, down_h[n // 2], fed[n][0], normed_two)

    _, (back_3, local_3) = both_rounds([down_s0], (), feed_back_second, back_args(3))
    (gu_far_1,), (back_1, local_1) = both_rounds(
        [down_s0], [(local_3, to_core)], feed_back_second, back_args(1)
    )
    y_order = [size // 2]
    for step in range(size // 2 - 1, 0, -1):
        y_order += [size - step, step]
    y_order += [0]
    y_got = {}

    def y_send():
        b = y_order[len(y_got)]
        return (total(row(local_1, b), row(gu_far_1, b)), to_y)

    def y_take(value):
        y_got[y_order[len(y_got)]] = value


    def down_part_and_sum(cot, h3, middle, h0, h1, weight):
        half = middle + plain_dot(jnp.concatenate([h0, h1], 1), weight)
        return cols_dot(h3, cot), half

    (away,), (down_11, half_out) = ordered_round(
        [y_send()], down_part_and_sum, (cot, fed[3][1], middle, fed[0][1], fed[1][1], down_half)
    )
    y_take(away)
    (away, down_far_1), (back_2, local_2) = ordered_round(
        [y_send(), (down_11, to_core)], feed_back_first, back_args(2)
    )
    y_take(away)
    down_s1 = col_scatter(down_01, down_far_1, False)
    (away, gu_far_0), (back_0, local_0) = both_rounds(
        [down_s1], [y_send(), (local_2, to_core)], feed_back_first, back_args(0)
    )
    y_take(away)
    gu_s = Scatter(lambda b: (row(local_0, b), row(gu_far_0, b), y_got[b]), False)

    def through(b0, w0, b1, w1):
        return rows_dot(b0, w0) + rows_dot(b1, w1)

    (away,), grad_a = both_rounds(
        [down_s1, gu_s], [y_send()], through, (back_1, gu_q[1], back_3, gu_q[3])
    )
    y_take(away)

    def mid_back(grad_a, b0, w0, b1, w1, middle, inv_two, gain, cot):
        return norm_back(grad_a, [b0, b1], [w0, w1], middle, inv_two, gain, cot, 2 * tile)

    (away,), (branch_back, gain_two_local) = both_rounds(
        [down_s1],
        [y_send()],
        mid_back,
        (grad_a, back_0, gu_q[0], back_2, gu_q[2], middle, inv_two, gain_two_f, cot),
    )
    y_take(away)

    def conv_back_half(branch_back, out_rows, parts, gated, taps, normed_one):
        return convolve_back(branch_back, out_rows, parts, gated, taps, normed_one, 2)

    def conv_args(i):
        return (branch_back, out_h[i], parts_h[i], gated_h[i], taps_h[i], normed_one)

    (away,), (in_back_1, in_local_1, taps_local_1) = both_rounds(
        [down_s1, gu_s], [y_send()], conv_back_half, conv_args(1)
    )
    y_take(away)
    (away, in_got), (in_back_0, in_local_0, taps_local_0) = both_rounds(
        [gu_s], [y_send(), (in_local_1, to_core)], conv_back_half, conv_args(0)
    )
    y_take(away)
    in_s = Scatter(lambda b: (row(in_local_0, b), row(in_got, b)), False)

    def swap(flag, first, second, axis):
        return jnp.where(
            flag == 0,
            jnp.concatenate([first, second], axis),
            jnp.concatenate([second, first], axis),
        )

    def y_ordered(value, axis):
        n = value.shape[axis] // 2
        return swap(
            ybit,
            lax.slice_in_dim(value, 0, n, axis=axis),
            lax.slice_in_dim(value, n, 2 * n, axis=axis),
            axis,
        )

    finish(down_s0, down_s1)
    down_slice = y_ordered(jnp.concatenate([down_s0.result(), down_s1.result()], 0), 0)

    def first_back(b0, w0, b1, w1, tokens_rel, inv_one, gain, branch_back):
        return norm_back(
            None, [b0, b1], [w0, w1], tokens_rel, inv_one, gain, branch_back, 3 * dq
        )

    (away, down_got), (tokens_grad, gain_one_local) = both_rounds(
        [gu_s, in_s],
        [y_send(), (down_slice, to_y)],
        first_back,
        (in_back_0, in_h[0], in_back_1, in_h[1], tokens_rel, inv_one, gain_one_f, branch_back),
    )
    y_take(away)

    def to_natural(value):
        return rows_dot(value.astype(bf16), to_rel)

    def small_start(gain_one_local, gain_two_local, taps_0, taps_1):
        conv_natural = rows_dot(
            jnp.concatenate([taps_0, taps_1], 1).astype(bf16),
            (jnp.arange(width)[:, None] == natural_feature[None, :]).astype(bf16),
        )
        gains = to_natural(jnp.concatenate([gain_one_local, gain_two_local], 0))
        return jnp.concatenate([gains, conv_natural], 0)

    small_moves = []
    step = 1
    while step < size:
        small_moves.append(pairs(lambda r, s, step=step: (r, s ^ step)))
        step *= 2

    def small_send():
        return (small_sum, small_moves.pop(0))

    while len(y_got) < size:
        (away,), _ = ordered_round([y_send()])
        y_take(away)
    finish(gu_s)
    gu_slice = gu_s.result()

    def block_sum(half_out, h2, h3, weight):
        return (half_out + plain_dot(jnp.concatenate([h2, h3], 1), weight)).astype(bf16)

    gu_slice = high_reps(gu_slice)
    down_total = high_reps(add(down_slice, down_got))
    def block_sum_and_small(half_out, h2, h3, weight, *small):
        return block_sum(half_out, h2, h3, weight), small_start(*small)

    (down_away, gu_other), (block_out, small_sum) = both_rounds(
        [in_s],
        [(down_total, to_core), (gu_slice, to_y)],
        block_sum_and_small,
        (
            half_out, fed[2][1], fed[3][1], down_other,
            gain_one_local, gain_two_local, taps_local_0, taps_local_1,
        ),
    )
    gu_both = jnp.stack([gu_slice, gu_other], 0)
    (small_got, gu_far), natural_outs = both_rounds(
        [in_s],
        [small_send(), (gu_both, to_core)],
        lambda *vs: [to_natural(v).astype(bf16) for v in vs],
        (block_out, tokens_grad),
    )
    small_sum = small_sum + small_got

    def core_whole(mine, other, axis):
        return swap(core, mine, other, axis).astype(f32)

    def gu_out(start):
        def of(value):
            return jnp.concatenate(
                [value[:, (2 * t + start) * tile : (2 * t + start + 1) * tile] for t in range(tiles)], 1
            )

        own = swap(ybit, of(gu_both[0]), of(gu_both[1]), 1)
        far = swap(ybit, of(gu_far[0]), of(gu_far[1]), 1)
        return core_whole(own, far, 1)

    def down_gate_up(down_total, down_away):
        return core_whole(down_total, down_away, 0), gu_out(0), gu_out(1)

    (small_got,), (down_grad, gate_grad, up_grad) = both_rounds(
        [in_s], [small_send()], down_gate_up, (down_total, down_away)
    )
    small_sum = small_sum + small_got
    finish(in_s)
    in_slice = y_ordered(in_s.result(), 1)
    (small_got, in_got), _ = ordered_round([small_send(), (in_slice, to_y)])
    small_sum = small_sum + small_got
    in_total = high_reps(add(in_slice, in_got))
    while small_moves:
        (small_got,), _ = ordered_round([small_send()])
        small_sum = small_sum + small_got
    to_both = pairs(lambda r, s: (r ^ 3, s))
    (in_away, by_core, by_y, by_both), _ = ordered_round(
        [(in_total, to_core)] + [(small_sum, perm) for perm in (to_core, to_y, to_both)]
    )
    small_sum = high_reps((small_sum + by_y) + (by_core + by_both))
    in_grad, out_grad = in_order(core, in_total, in_away, dq)
    small_total = lax.dynamic_slice_in_dim(
        small_sum, lax.axis_index("shard") * block, block, 1
    )
    return (
        *natural_outs,
        small_total[0],
        in_grad,
        small_total[2:],
        out_grad,
        small_total[1],
        gate_grad,
        up_grad,
        down_grad,
    )


def solution(mesh):
    in_specs = (
        P(("rep", "shard"), None),
        P("shard"),
        P("shard", None),
        P(None, "shard"),
        P(None, "shard"),
        P("shard"),
        P("shard", None),
        P("shard", None),
        P(None, "shard"),
        P(("rep", "shard"), None),
    )
    out_specs = (
        P(("rep", "shard"), None),
        P(("rep", "shard"), None),
        P("shard"),
        P("shard", None),
        P(None, "shard"),
        P(None, "shard"),
        P("shard"),
        P("shard", None),
        P("shard", None),
        P(None, "shard"),
    )
    body = functools.partial(shards, mesh.shape["rep"], mesh.shape["shard"])
    return jax.shard_map(body, mesh=mesh, in_specs=in_specs, out_specs=out_specs, check_vma=False)
```

time: 654 us -> 531 us (0.81)
  Pallas kernels: 0 us -> 186 us
  matrix products: 197 us -> 65.6 us
  other arithmetic: 131 us -> 62 us
  local copies, waits for them, and re-layouts: 92.1 us -> 25.6 us
  waiting for transfers between devices: 133 us -> 92.1 us
    pallas_call x0 -> x15, Pallas kernels: none -> 186 us  [the longest x12 146 us: kernel_call(): pl.pallas_call(body, grid=(steps,), in_specs=[pl.BlockSpec(block, where)...]
    dot_general x11 -> x6, matrix products: 79.1 us -> 24 us  [rows_dot(): lax.dot_general(left, right, (((1,), (1,)), ((), ())), preferred_element_...]
    convert_element_type x18 -> x5, other arithmetic: 52.7 us -> 8.08 us  [the longest x3 5.09 us: core_whole(): return swap(core, mine, other, axis).astype(f32)]
    ppermute x98 -> x93, waiting for transfers between devices: 133 us -> 92.1 us  [send(): return lax.ppermute(value, AXES, perm)]
    dot_general x12 -> x7, matrix products: 64.3 us -> 23.6 us  [plain_dot(): return jnp.dot(left, right, preferred_element_type=jnp.float32).astype(kind)]
    dot_general x11 -> x4, matrix products: 52.5 us -> 18 us  [cols_dot(): lax.dot_general(left, right, (((0,), (0,)), ((), ())), preferred_element_...]
    slice x34 -> x9, local copies, waits for them, and re-layouts: 34 us -> 1.34 us  [the longest x1 0.61 us: shards(): taps_h = (taps[:, :2 * dq], taps[:, 2 * dq:])]
    unnamed x332 -> x208, local copies, waits for them, and re-layouts: 46.2 us -> 16.2 us
  transfers between devices with their start and end apart: 98 -> 93, of which waited for: 38 -> 36; matrix products, arithmetic and copies ran while one was open for 58% -> 26% of each run, Pallas kernels for 0% -> 35%
where the time goes in v3:
time: 531 us; the launch traced here: 521 us
  Pallas kernels  186 us (35%)
  waiting for transfers between devices  92.1 us (17%)
  starting transfers between devices  87.4 us (16%)
  matrix products  65.6 us (12%)
  other arithmetic  62 us (12%)
  local copies, waits for them, and re-layouts  25.6 us (5%)
    pallas_call x12, Pallas kernels, kernel_call(): pl.pallas_call(body, grid=(steps,), in_specs=[pl.BlockSpec(block, where)...  146 us
    ppermute x93, waiting for transfers between devices, send(): return lax.ppermute(value, AXES, perm)  92.1 us
    ppermute x93, starting transfers between devices, send(): return lax.ppermute(value, AXES, perm)  87.4 us
    convert_element_type x23, other arithmetic, total(): return sum((v.astype(f32) for v in values)).astype(bf16)  44.6 us
    pallas_call x2, Pallas kernels, norm_back(): pl.pallas_call(body, grid=(total * per,), in_specs=[pl.BlockSpec((count,...  37.3 us
    dot_general x6, matrix products, rows_dot(): lax.dot_general(left, right, (((1,), (1,)), ((), ())), preferred_element_...  24 us
    dot_general x7, matrix products, plain_dot(): return jnp.dot(left, right, preferred_element_type=jnp.float32).astype(kind)  23.6 us
    dot_general x4, matrix products, cols_dot(): lax.dot_general(left, right, (((0,), (0,)), ((), ())), preferred_element_...  18 us
  transfers between devices with their start and end apart: 93, of which 36 were waited for; matrix products, arithmetic and copies ran while one was open for 26% of the time, Pallas kernels for 35%

profile of v3, /device:TPU:0, one launch (start us, length us, event | category | flops | bytes accessed | tf_op | source)
XLA Modules:
  0.0 521.4 jit_solution(3828910599925907301)
XLA Ops:
  24.6 7.8 %collective-permute-done.2.refs_3_ = bf16[144,1536]{1,0:T(8,128)(2,1)S(1)} collective-permute-done((bf16[144,1536]{1,0:T(8,128)(2,1)S(1)}, bf16[144,1536]{1,0:T(8,128)(2,1)S(1)}, u32[]{:S(2)}, u32[]{:S(2)}) %collective-permute-start.2) | collective-permute-done | bytes 442400 | tf_op jit(solution)/shard_map/ppermute | solution.py:365
  52.1 7.1 %collective-permute-done.11.refs_7_ = bf16[144,1536]{1,0:T(8,128)(2,1)S(1)} collective-permute-done((bf16[144,1536]{1,0:T(8,128)(2,1)S(1)}, bf16[144,1536]{1,0:T(8,128)(2,1)S(1)}, u32[]{:S(2)}, u32[]{:S(2)}) %collective-permute-start.11) | collective-permute-done | bytes 442400 | tf_op jit(solution)/shard_map/ppermute | solution.py:365
  65.3 8.4 %shard_map.204 = (bf16[1024,1536]{1,0:T(8,128)(2,1)}, bf16[1024,512]{1,0:T(8,128)(2,1)}, bf16[1024,1536]{1,0:T(8,128)(2,1)}) custom-call(bf16[1024,1024]{1,0:T(8,128)(2,1)} %multiply_convert_fusion.1.normed_ref, f32[3,512]{1,0:T(4,128)} %get-tuple-element.457.taps_ref, bf16[144,1536]{1,0:T(8,128)(2,1)} %copy-done.16, bf16[144,1536]{1,0:T(8,128)(2,1)} %copy-done.43, ...), custom_call_target="tpu_custom_call" | custom-call | tf_op jit(solution)/shard_map/pallas_call | solution.py:36
  83.2 7.6 %collective-permute-done.16.refs_4_ = bf16[128,2304]{1,0:T(8,128)(2,1)} collective-permute-done((bf16[128,2304]{1,0:T(8,128)(2,1)}, bf16[128,2304]{1,0:T(8,128)(2,1)}, u32[]{:S(2)}, u32[]{:S(2)}) %collective-permute-start.16) | collective-permute-done | bytes 589856 | tf_op jit(solution)/shard_map/ppermute | solution.py:365
  96.7 7.9 %shard_map.205 = (bf16[1024,1536]{1,0:T(8,128)(2,1)}, bf16[1024,512]{1,0:T(8,128)(2,1)}, bf16[1024,1536]{1,0:T(8,128)(2,1)}) custom-call(bf16[1024,1024]{1,0:T(8,128)(2,1)} %multiply_convert_fusion.1.normed_ref, f32[3,512]{1,0:T(4,128)} %get-tuple-element.445.taps_ref, bf16[1024,1536]{1,0:T(8,128)(2,1)} %copy-done.9), custom_call_target="tpu_custom_call" | custom-call | tf_op jit(solution)/shard_map/pallas_call | solution.py:36
  125.8 11.0 %shard_map.206 = (bf16[1024,2304]{1,0:T(8,128)(2,1)}, bf16[1024,1152]{1,0:T(8,128)(2,1)}, bf16[1024,2304]{1,0:T(8,128)(2,1)}) custom-call(bf16[1024,1024]{1,0:T(8,128)(2,1)} %multiply_convert_fusion.normed_ref, bf16[128,2304]{1,0:T(8,128)(2,1)} %copy-done.19, bf16[128,2304]{1,0:T(8,128)(2,1)} %collective-permute-done.13.refs_1_, ...), custom_call_target="tpu_custom_call" | custom-call | tf_op jit(solution)/shard_map/pallas_call | solution.py:36
  146.3 6.3 %collective-permute-done.29 = bf16[2304,128]{1,0:T(8,128)(2,1)S(1)} collective-permute-done((bf16[2304,128]{1,0:T(8,128)(2,1)S(1)}, bf16[2304,128]{1,0:T(8,128)(2,1)S(1)}, u32[]{:S(2)}, u32[]{:S(2)}) %collective-permute-start.29) | collective-permute-done | bytes 589856 | tf_op jit(solution)/shard_map/ppermute | solution.py:365
  158.7 10.4 %shard_map.207 = (bf16[1024,2304]{1,0:T(8,128)(2,1)}, bf16[1024,1152]{1,0:T(8,128)(2,1)}, bf16[1024,2304]{1,0:T(8,128)(2,1)}) custom-call(bf16[1024,1024]{1,0:T(8,128)(2,1)} %multiply_convert_fusion.normed_ref, bf16[1024,2304]{1,0:T(8,128)(2,1)} %collective-permute-done.31.refs_0_.refs_3_), custom_call_target="tpu_custom_call" | custom-call | tf_op jit(solution)/shard_map/pallas_call | solution.py:36
  185.8 11.0 %shard_map.208 = (bf16[1024,2304]{1,0:T(8,128)(2,1)}, bf16[1024,1152]{1,0:T(8,128)(2,1)}, bf16[1024,2304]{1,0:T(8,128)(2,1)}) custom-call(bf16[1024,1024]{1,0:T(8,128)(2,1)} %multiply_convert_fusion.normed_ref, bf16[128,2304]{1,0:T(8,128)(2,1)} %copy-done.20, bf16[128,2304]{1,0:T(8,128)(2,1)} %copy-done.28, ...), custom_call_target="tpu_custom_call" | custom-call | tf_op jit(solution)/shard_map/pallas_call | solution.py:36
  211.0 10.3 %shard_map.209 = (bf16[1024,2304]{1,0:T(8,128)(2,1)}, bf16[1024,1152]{1,0:T(8,128)(2,1)}, bf16[1024,2304]{1,0:T(8,128)(2,1)}) custom-call(bf16[1024,1024]{1,0:T(8,128)(2,1)} %multiply_convert_fusion.normed_ref, bf16[1024,2304]{1,0:T(8,128)(2,1)} %collective-permute-done.41.refs_0_), custom_call_target="tpu_custom_call" | custom-call | tf_op jit(solution)/shard_map/pallas_call | solution.py:36
  224.8 14.3 %shard_map.210 = (bf16[1024,2304]{1,0:T(8,128)(2,1)}, bf16[1024,2304]{1,0:T(8,128)(2,1)}) custom-call(bf16[1024,1024]{1,0:T(8,128)(2,1)} %copy-done.4, bf16[2304,1024]{1,0:T(8,128)(2,1)} %collective-permute-done.39.down_ref, bf16[1024,2304]{1,0:T(8,128)(2,1)} %get-tuple-element.380.pre_ref, bf16[1024,1024]{1,0:T(8,128)(2,1)} %multiply_convert_fusion.normed_ref), custom_call_target="tpu_custom_call" | custom-call | tf_op jit(solution)/shard_map/pallas_call | solution.py:36
  243.0 14.4 %shard_map.211 = (bf16[1024,2304]{1,0:T(8,128)(2,1)}, bf16[1024,2304]{1,0:T(8,128)(2,1)}) custom-call(bf16[1024,1024]{1,0:T(8,128)(2,1)} %copy-done.4, bf16[2304,1024]{1,0:T(8,128)(2,1)} %constant_dynamic-update-slice_fusion.28.down_ref, bf16[1024,2304]{1,0:T(8,128)(2,1)} %get-tuple-element.386.pre_ref, bf16[1024,1024]{1,0:T(8,128)(2,1)} %multiply_convert_fusion.normed_ref), custom_call_target="tpu_custom_call" | custom-call | tf_op jit(solution)/shard_map/pallas_call | solution.py:36
  257.4 5.8 %add_convert_fusion.3 = (bf16[128,2304]{1,0:T(8,128)(2,1)S(1)}, bf16[128,2304]{1,0:T(8,128)(2,1)S(1)}, bf16[128,2304]{1,0:T(8,128)(2,1)}, bf16[128,2304]{1,0:T(8...) fusion(bf16[1024,2304]{1,0:T(8,128)(2,1)} %collective-permute-d, ...), kind=kLoop, calls=%fused_computation.51 | loop fusion | flops 9437184 | bytes 14155776 | tf_op jit(solution)/shard_map/convert_element_type | solution.py:463
  264.1 6.9 %fusion = f32[1024,1024]{1,0:T(8,128)S(1)} fusion(bf16[2304,1024]{1,0:T(8,128)(2,1)} %constant_dynamic-update-slice_fusion.28.down_ref, bf16[1024,1152]{1,0:T(8,128)(2,1)S(1)} %copy-done.70, bf16[1024,1152]{1,0:T(8,128)(2,1)S(1)} %copy-done.69), kind=kOutput, calls=%fused_computation.1 | convolution fusion | flops 4841275392 | bytes 13631488 | tf_op jit(solution)/shard_map/dot_general | solution.py:20
  280.0 14.4 %shard_map.212 = (bf16[1024,2304]{1,0:T(8,128)(2,1)}, bf16[1024,2304]{1,0:T(8,128)(2,1)}) custom-call(bf16[1024,1024]{1,0:T(8,128)(2,1)} %copy-done.4, bf16[2304,1024]{1,0:T(8,128)(2,1)} %collective-permute-done.39.down_ref, bf16[1024,2304]{1,0:T(8,128)(2,1)} %get-tuple-element.403.pre_ref, bf16[1024,1024]{1,0:T(8,128)(2,1)} %multiply_convert_fusion.normed_ref), custom_call_target="tpu_custom_call" | custom-call | tf_op jit(solution)/shard_map/pallas_call | solution.py:36
  299.2 14.4 %shard_map.213 = (bf16[1024,2304]{1,0:T(8,128)(2,1)}, bf16[1024,2304]{1,0:T(8,128)(2,1)}) custom-call(bf16[1024,1024]{1,0:T(8,128)(2,1)} %copy-done.4, bf16[2304,1024]{1,0:T(8,128)(2,1)} %constant_dynamic-update-slice_fusion.28.down_ref, bf16[1024,2304]{1,0:T(8,128)(2,1)} %get-tuple-element.410.pre_ref, bf16[1024,1024]{1,0:T(8,128)(2,1)} %multiply_convert_fusion.normed_ref), custom_call_target="tpu_custom_call" | custom-call | tf_op jit(solution)/shard_map/pallas_call | solution.py:36
  321.2 8.3 %fusion.51 = f32[1024,1024]{1,0:T(8,128)S(1)} fusion(bf16[1024,2304]{1,0:T(8,128)(2,1)} %get-tuple-element.422, bf16[1024,2304]{1,0:T(8,128)(2,1)} %collective-permute-done.41.refs_0_), kind=kOutput, calls=%fused_computation.241 | convolution fusion | flops 4831838208 | bytes 13631488 | tf_op jit(solution)/shard_map/dot_general | solution.py:24
  329.6 6.7 %convolution_add_fusion.refs_8_ = f32[1024,1024]{1,0:T(8,128)} fusion(f32[1024,1024]{1,0:T(8,128)S(1)} %fusion.51, bf16[1024,2304]{1,0:T(8,128)(2,1)S(1)} %bitcast.93, bf16[1024,2304]{1,0:T(8,128)(2,1)S(1)} %bitcast.91), kind=kOutput, calls=%fused_computation.37 | convolution fusion | flops 4832886784 | bytes 17825792 | tf_op jit(solution)/shard_map/dot_general | solution.py:24
  346.0 21.4 %shard_map.214 = (bf16[1024,1024]{1,0:T(8,128)(2,1)}, f32[1,1024]{1,0:T(1,128)}) custom-call(bf16[1024,2304]{1,0:T(8,128)(2,1)} %get-tuple-element.427.refs_0_, bf16[1024,2304]{1,0:T(8,128)(2,1)} %get-tuple-element.428.refs_1_, bf16[1024,2304]{1,0:T(8,128)(2,1)} %get-tuple-element.429.refs_2_, bf16[1024,2304]{1,0:T(8,128)(2,1)} %collective-permute-done.31.refs_0_.refs_3_, ...), custom_call_target="tpu_custom_call" | custom-call | tf_op jit(solution)/shard_map/pallas_call | solution.py:263
  374.4 14.7 %shard_map.215 = (bf16[1024,1536]{1,0:T(8,128)(2,1)}, bf16[1024,2048]{1,0:T(8,128)(2,1)}, f32[3,512]{1,0:T(4,128)}) custom-call(bf16[1024,1024]{1,0:T(8,128)(2,1)} %get-tuple-element.478.branch_ref.refs_7_, bf16[512,1024]{1,0:T(8,128)(2,1)} %copy-done.12, bf16[1024,1536]{1,0:T(8,128)(2,1)} %get-tuple-element.443.parts_ref, ...), custom_call_target="tpu_custom_call" | custom-call | tf_op jit(solution)/shard_map/pallas_call | solution.py:36
  400.3 14.8 %shard_map.216 = (bf16[1024,1536]{1,0:T(8,128)(2,1)}, bf16[1024,2048]{1,0:T(8,128)(2,1)}, f32[3,512]{1,0:T(4,128)}) custom-call(bf16[1024,1024]{1,0:T(8,128)(2,1)} %get-tuple-element.478.branch_ref.refs_7_, bf16[512,1024]{1,0:T(8,128)(2,1)} %copy-done.18, bf16[1024,1536]{1,0:T(8,128)(2,1)} %get-tuple-element.455.parts_ref, ...), custom_call_target="tpu_custom_call" | custom-call | tf_op jit(solution)/shard_map/pallas_call | solution.py:36
  426.9 15.9 %shard_map.217 = (bf16[1024,1024]{1,0:T(8,128)(2,1)}, f32[1,1024]{1,0:T(1,128)}) custom-call(bf16[1024,1536]{1,0:T(8,128)(2,1)} %get-tuple-element.471.refs_0_, bf16[1024,1536]{1,0:T(8,128)(2,1)} %get-tuple-element.472.refs_1_, bf16[1024,1536]{1,0:T(8,128)(2,1)} %get-tuple-element.473.refs_2_, bf16[1024,1536]{1,0:T(8,128)(2,1)} %copy-done.9, ...), custom_call_target="tpu_custom_call" | custom-call | tf_op jit(solution)/shard_map/pallas_call | solution.py:263
  456.3 7.0 %fusion.4 = f32[1024,1024]{1,0:T(8,128)S(1)} fusion(bf16[2304,1024]{1,0:T(8,128)(2,1)} %collective-permute-done.39.down_ref, bf16[1024,1152]{1,0:T(8,128)(2,1)S(1)} %copy-done.67, bf16[1024,1152]{1,0:T(8,128)(2,1)S(1)} %copy-done.65), kind=kOutput, calls=%fused_computation.5 | convolution fusion | flops 4841275392 | bytes 13631488 | tf_op jit(solution)/shard_map/dot_general | solution.py:20
  505.6 6.0 %collective-permute-done.88 = bf16[128,2048]{1,0:T(8,128)(2,1)S(1)} collective-permute-done((bf16[128,2048]{1,0:T(8,128)(2,1)S(1)}, bf16[128,2048]{1,0:T(8,128)(2,1)S(1)}, u32[]{:S(2)}, u32[]{:S(2)}) %collective-permute-start.88) | collective-permute-done | bytes 524320 | tf_op jit(solution)/shard_map/ppermute | solution.py:365
  (496 shorter events, 265.9 us)
Async XLA Ops:
  240.8 22.5 %collective-permute-start.47 = (bf16[1152,128]{1,0:T(8,128)(2,1)S(1)}, bf16[1152,128]{1,0:T(8,128)(2,1)S(1)}, u32[]{:S(2)}, u32[]{:S(2)}) collective-permute-start(bf16[1152,128]{1,0:T(8,128)(2,1)S(1)} %get-tuple-element.390), channel_id=1, source_target_pairs={{0,1},{1,3},{2,0},{3,5},{4,2},{5,7},{6,4},{7,6},{8,9},{9,11},{10,8... | collective-permute-start | bytes 884744 | tf_op jit(solution)/shard_map/ppermute | solution.py:365
  242.5 20.8 %collective-permute-start.48 = (bf16[1152,128]{1,0:T(8,128)(2,1)S(1)}, bf16[1152,128]{1,0:T(8,128)(2,1)S(1)}, u32[]{:S(2)}, u32[]{:S(2)}) collective-permute-start(bf16[1152,128]{1,0:T(8,128)(2,1)S(1)} %get-tuple-element.391), channel_id=1, source_target_pairs={{0,2},{1,0},{2,4},{3,1},{4,6},{5,3},{6,7},{7,5},{8,10},{9,8},{10,1... | collective-permute-start | bytes 884744 | tf_op jit(solution)/shard_map/ppermute | solution.py:365
  295.8 19.5 %collective-permute-start.52 = (bf16[1024,2304]{1,0:T(8,128)(2,1)}, bf16[1024,2304]{1,0:T(8,128)(2,1)S(1)}, u32[]{:S(2)}, u32[]{:S(2)}) collective-permute-start(bf16[1024,2304]{1,0:T(8,128)(2,1)} %get-tuple-element.413), channel_id=1, source_target_pairs={{0,8},{1,9},{2,10},{3,11},{4,12},{5,13},{6,14},{7,15},{8,0},{9,1},... | collective-permute-start | bytes 14155784 | tf_op jit(solution)/shard_map/ppermute | solution.py:365
  297.9 19.2 %collective-permute-start.54 = (bf16[128,2304]{1,0:T(8,128)(2,1)S(1)}, bf16[128,2304]{1,0:T(8,128)(2,1)S(1)}, u32[]{:S(2)}, u32[]{:S(2)}) collective-permute-start(bf16[128,2304]{1,0:T(8,128)(2,1)S(1)} %copy-done.26), channel_id=1, source_target_pairs={{0,16},{1,17},{2,18},{3,19},{4,20},{5,21},{6,22},{7,23},{8,24},{9,... | collective-permute-start | bytes 1769480 | tf_op jit(solution)/shard_map/ppermute | solution.py:365
  317.1 19.2 %collective-permute-start.56 = (bf16[1152,128]{1,0:T(8,128)(2,1)S(1)}, bf16[1152,128]{1,0:T(8,128)(2,1)S(1)}, u32[]{:S(2)}, u32[]{:S(2)}) collective-permute-start(bf16[1152,128]{1,0:T(8,128)(2,1)S(1)} %get-tuple-element.418), channel_id=1, source_target_pairs={{0,1},{1,3},{2,0},{3,5},{4,2},{5,7},{6,4},{7,6},{8,9},{9,11},{10,8... | collective-permute-start | bytes 884744 | tf_op jit(solution)/shard_map/ppermute | solution.py:365
  318.2 18.1 %collective-permute-start.57 = (bf16[1152,128]{1,0:T(8,128)(2,1)S(1)}, bf16[1152,128]{1,0:T(8,128)(2,1)S(1)}, u32[]{:S(2)}, u32[]{:S(2)}) collective-permute-start(bf16[1152,128]{1,0:T(8,128)(2,1)S(1)} %get-tuple-element.419), channel_id=1, source_target_pairs={{0,2},{1,0},{2,4},{3,1},{4,6},{5,3},{6,7},{7,5},{8,10},{9,8},{10,1... | collective-permute-start | bytes 884744 | tf_op jit(solution)/shard_map/ppermute | solution.py:365
  319.2 19.5 %collective-permute-start.55 = (bf16[128,2304]{1,0:T(8,128)(2,1)S(1)}, bf16[128,2304]{1,0:T(8,128)(2,1)S(1)}, u32[]{:S(2)}, u32[]{:S(2)}) collective-permute-start(bf16[128,2304]{1,0:T(8,128)(2,1)S(1)} %copy-done.23), channel_id=1, source_target_pairs={{0,16},{1,17},{2,18},{3,19},{4,20},{5,21},{6,22},{7,23},{8,24},{9,... | collective-permute-start | bytes 1769480 | tf_op jit(solution)/shard_map/ppermute | solution.py:365
  319.9 18.8 %collective-permute-start.58 = (bf16[128,2304]{1,0:T(8,128)(2,1)S(1)}, bf16[128,2304]{1,0:T(8,128)(2,1)S(1)}, u32[]{:S(2)}, u32[]{:S(2)}) collective-permute-start(bf16[128,2304]{1,0:T(8,128)(2,1)S(1)} %add_convert_fusion.14), channel_id=1, source_target_pairs={{0,1},{1,3},{2,0},{3,5},{4,2},{5,7},{6,4},{7,6},{8,9},{9,11},{10,8... | collective-permute-start | bytes 1769480 | tf_op jit(solution)/shard_map/ppermute | solution.py:365
  338.7 28.8 %collective-permute-start.59 = (bf16[1152,128]{1,0:T(8,128)(2,1)}, bf16[1152,128]{1,0:T(8,128)(2,1)}, u32[]{:S(2)}, u32[]{:S(2)}) collective-permute-start(bf16[1152,128]{1,0:T(8,128)(2,1)} %get-tuple-element.425), channel_id=1, source_target_pairs={{0,1},{1,3},{2,0},{3,5},{4,2},{5,7},{6,4},{7,6},{8,9},{9,11},{10,8... | collective-permute-start | bytes 884744 | tf_op jit(solution)/shard_map/ppermute | solution.py:365
  339.7 27.7 %collective-permute-start.60 = (bf16[1152,128]{1,0:T(8,128)(2,1)S(1)}, bf16[1152,128]{1,0:T(8,128)(2,1)}, u32[]{:S(2)}, u32[]{:S(2)}) collective-permute-start(bf16[1152,128]{1,0:T(8,128)(2,1)S(1)} %get-tuple-element.426), channel_id=1, source_target_pairs={{0,2},{1,0},{2,4},{3,1},{4,6},{5,3},{6,7},{7,5},{8,10},{9,8},{10,1... | collective-permute-start | bytes 884744 | tf_op jit(solution)/shard_map/ppermute | solution.py:365
  341.1 28.1 %collective-permute-start.61 = (bf16[128,2304]{1,0:T(8,128)(2,1)S(1)}, bf16[128,2304]{1,0:T(8,128)(2,1)}, u32[]{:S(2)}, u32[]{:S(2)}) collective-permute-start(bf16[128,2304]{1,0:T(8,128)(2,1)S(1)} %copy-done.22), channel_id=1, source_target_pairs={{0,16},{1,17},{2,18},{3,19},{4,20},{5,21},{6,22},{7,23},{8,24},{9,... | collective-permute-start | bytes 1769480 | tf_op jit(solution)/shard_map/ppermute | solution.py:365
  369.3 19.8 %collective-permute-start.62 = (bf16[128,2304]{1,0:T(8,128)(2,1)S(1)}, bf16[128,2304]{1,0:T(8,128)(2,1)S(1)}, u32[]{:S(2)}, u32[]{:S(2)}) collective-permute-start(bf16[128,2304]{1,0:T(8,128)(2,1)S(1)} %copy-done.37), channel_id=1, source_target_pairs={{0,1},{1,3},{2,0},{3,5},{4,2},{5,7},{6,4},{7,6},{8,9},{9,11},{10,8... | collective-permute-start | bytes 1769480 | tf_op jit(solution)/shard_map/ppermute | solution.py:365
  370.3 18.8 %collective-permute-start.63 = (bf16[128,2304]{1,0:T(8,128)(2,1)S(1)}, bf16[128,2304]{1,0:T(8,128)(2,1)S(1)}, u32[]{:S(2)}, u32[]{:S(2)}) collective-permute-start(bf16[128,2304]{1,0:T(8,128)(2,1)S(1)} %copy-done.36), channel_id=1, source_target_pairs={{0,2},{1,0},{2,4},{3,1},{4,6},{5,3},{6,7},{7,5},{8,10},{9,8},{10,1... | collective-permute-start | bytes 1769480 | tf_op jit(solution)/shard_map/ppermute | solution.py:365
  371.4 21.1 %collective-permute-start.64 = (bf16[1152,128]{1,0:T(8,128)(2,1)S(1)}, bf16[1152,128]{1,0:T(8,128)(2,1)S(1)}, u32[]{:S(2)}, u32[]{:S(2)}) collective-permute-start(bf16[1152,128]{1,0:T(8,128)(2,1)S(1)} %get-tuple-element.448), channel_id=1, source_target_pairs={{0,1},{1,3},{2,0},{3,5},{4,2},{5,7},{6,4},{7,6},{8,9},{9,11},{10,8... | collective-permute-start | bytes 884744 | tf_op jit(solution)/shard_map/ppermute | solution.py:365
  372.4 20.1 %collective-permute-start.65 = (bf16[1152,128]{1,0:T(8,128)(2,1)S(1)}, bf16[1152,128]{1,0:T(8,128)(2,1)S(1)}, u32[]{:S(2)}, u32[]{:S(2)}) collective-permute-start(bf16[1152,128]{1,0:T(8,128)(2,1)S(1)} %get-tuple-element.449), channel_id=1, source_target_pairs={{0,2},{1,0},{2,4},{3,1},{4,6},{5,3},{6,7},{7,5},{8,10},{9,8},{10,1... | collective-permute-start | bytes 884744 | tf_op jit(solution)/shard_map/ppermute | solution.py:365
  373.4 19.1 %collective-permute-start.66 = (bf16[128,2304]{1,0:T(8,128)(2,1)S(1)}, bf16[128,2304]{1,0:T(8,128)(2,1)S(1)}, u32[]{:S(2)}, u32[]{:S(2)}) collective-permute-start(bf16[128,2304]{1,0:T(8,128)(2,1)S(1)} %copy-done.21), channel_id=1, source_target_pairs={{0,16},{1,17},{2,18},{3,19},{4,20},{5,21},{6,22},{7,23},{8,24},{9,... | collective-permute-start | bytes 1769480 | tf_op jit(solution)/shard_map/ppermute | solution.py:365
  393.3 24.8 %collective-permute-start.67 = (bf16[1024,2048]{1,0:T(8,128)(2,1)}, bf16[1024,2048]{1,0:T(8,128)(2,1)}, u32[]{:S(2)}, u32[]{:S(2)}) collective-permute-start(bf16[1024,2048]{1,0:T(8,128)(2,1)} %get-tuple-element.460), channel_id=1, source_target_pairs={{0,8},{1,9},{2,10},{3,11},{4,12},{5,13},{6,14},{7,15},{8,0},{9,1},... | collective-permute-start | bytes 12582920 | tf_op jit(solution)/shard_map/ppermute | solution.py:365
  395.4 19.7 %collective-permute-start.68 = (bf16[128,2304]{1,0:T(8,128)(2,1)}, bf16[128,2304]{1,0:T(8,128)(2,1)S(1)}, u32[]{:S(2)}, u32[]{:S(2)}) collective-permute-start(bf16[128,2304]{1,0:T(8,128)(2,1)} %get-tuple-element.461), channel_id=1, source_target_pairs={{0,1},{1,3},{2,0},{3,5},{4,2},{5,7},{6,4},{7,6},{8,9},{9,11},{10,8... | collective-permute-start | bytes 1769480 | tf_op jit(solution)/shard_map/ppermute | solution.py:365
  396.4 18.7 %collective-permute-start.69 = (bf16[128,2304]{1,0:T(8,128)(2,1)S(1)}, bf16[128,2304]{1,0:T(8,128)(2,1)S(1)}, u32[]{:S(2)}, u32[]{:S(2)}) collective-permute-start(bf16[128,2304]{1,0:T(8,128)(2,1)S(1)} %get-tuple-element.462), channel_id=1, source_target_pairs={{0,16},{1,17},{2,18},{3,19},{4,20},{5,21},{6,22},{7,23},{8,24},{9,... | collective-permute-start | bytes 1769480 | tf_op jit(solution)/shard_map/ppermute | solution.py:365
  420.8 22.0 %collective-permute-start.71 = (bf16[128,2048]{1,0:T(8,128)(2,1)S(1)}, bf16[128,2048]{1,0:T(8,128)(2,1)}, u32[]{:S(2)}, u32[]{:S(2)}) collective-permute-start(bf16[128,2048]{1,0:T(8,128)(2,1)S(1)} %get-tuple-element.466), channel_id=1, source_target_pairs={{0,1},{1,3},{2,0},{3,5},{4,2},{5,7},{6,4},{7,6},{8,9},{9,11},{10,8... | collective-permute-start | bytes 1572872 | tf_op jit(solution)/shard_map/ppermute | solution.py:365
  421.8 22.5 %collective-permute-start.72 = (bf16[2304,128]{1,0:T(8,128)(2,1)S(1)}, bf16[2304,128]{1,0:T(8,128)(2,1)}, u32[]{:S(2)}, u32[]{:S(2)}) collective-permute-start(bf16[2304,128]{1,0:T(8,128)(2,1)S(1)} %maximum_select_fusion.3), channel_id=1, source_target_pairs={{0,16},{1,17},{2,18},{3,19},{4,20},{5,21},{6,22},{7,23},{8,24},{9,... | collective-permute-start | bytes 1769480 | tf_op jit(solution)/shard_map/ppermute | solution.py:365
  423.8 24.6 %collective-permute-start.73 = (bf16[128,2304]{1,0:T(8,128)(2,1)S(1)}, bf16[128,2304]{1,0:T(8,128)(2,1)S(1)}, u32[]{:S(2)}, u32[]{:S(2)}) collective-permute-start(bf16[128,2304]{1,0:T(8,128)(2,1)S(1)} %get-tuple-element.468), channel_id=1, source_target_pairs={{0,16},{1,17},{2,18},{3,19},{4,20},{5,21},{6,22},{7,23},{8,24},{9,... | collective-permute-start | bytes 1769480 | tf_op jit(solution)/shard_map/ppermute | solution.py:365
  424.9 23.5 %collective-permute-start.74 = (bf16[128,2304]{1,0:T(8,128)(2,1)}, bf16[128,2304]{1,0:T(8,128)(2,1)}, u32[]{:S(2)}, u32[]{:S(2)}) collective-permute-start(bf16[128,2304]{1,0:T(8,128)(2,1)} %get-tuple-element.469), channel_id=1, source_target_pairs={{0,1},{1,3},{2,0},{3,5},{4,2},{5,7},{6,4},{7,6},{8,9},{9,11},{10,8... | collective-permute-start | bytes 1769480 | tf_op jit(solution)/shard_map/ppermute | solution.py:365
  425.7 23.5 %collective-permute-start.75 = (bf16[128,2304]{1,0:T(8,128)(2,1)S(1)}, bf16[128,2304]{1,0:T(8,128)(2,1)}, u32[]{:S(2)}, u32[]{:S(2)}) collective-permute-start(bf16[128,2304]{1,0:T(8,128)(2,1)S(1)} %get-tuple-element.470), channel_id=1, source_target_pairs={{0,2},{1,0},{2,4},{3,1},{4,6},{5,3},{6,7},{7,5},{8,10},{9,8},{10,1... | collective-permute-start | bytes 1769480 | tf_op jit(solution)/shard_map/ppermute | solution.py:365
  (148 other events, 1900.0 us)

commit v4 on v3

--- a/solution.py
+++ b/solution.py
@@ -30,6 +30,10 @@
     return lax.dot_general(
         left, right, (((0,), (0,)), ((), ())), preferred_element_type=jnp.float32
     ).astype(jnp.bfloat16)
+
+
+def sigmoid(values):
+    return 0.5 * jnp.tanh(0.5 * values) + 0.5
 
 
 def kernel_call(body, steps, ins, outs):
@@ -73,7 +77,7 @@
         pre = jnp.dot(normed_ref[...], weight_ref[...], preferred_element_type=jnp.float32)
         pre_ref[...] = pre.astype(jnp.bfloat16)
         gate = pre[:, :tile]
-        hidden_ref[...] = (gate * jax.nn.sigmoid(gate) * pre[:, tile:]).astype(jnp.bfloat16)
+        hidden_ref[...] = (gate * sigmoid(gate) * pre[:, tile:]).astype(jnp.bfloat16)
 
     return kernel_call(
         body,
@@ -87,6 +91,47 @@
     )
 
 
+def feed_and_down(normed, pieces, cot, half, at, tiles):
+    count, depth = normed.shape
+    extent = depth // len(pieces)
+    pair = pieces[0].shape[1] // tiles
+    tile = pair // 2
+    n_pieces = len(pieces)
+    operands = [] if half is None else [half]
+
+    def body(normed_ref, cot_ref, *refs):
+        piece_refs = refs[:n_pieces]
+        pre_ref, hidden_ref, weight_ref, down_ref = refs[-4:]
+        gathered(piece_refs, weight_ref)
+        pre = jnp.dot(normed_ref[...], weight_ref[...], preferred_element_type=jnp.float32)
+        pre_ref[...] = pre.astype(jnp.bfloat16)
+        gate = pre[:, :tile]
+        hidden_ref[...] = (gate * sigmoid(gate) * pre[:, tile:]).astype(jnp.bfloat16)
+        down_ref[...] = cols_dot(cot_ref[...], hidden_ref[...])
+
+    return pl.pallas_call(
+        body,
+        grid=(tiles,),
+        in_specs=[pl.BlockSpec((count, depth), same)] * 2
+        + [pl.BlockSpec((extent, pair), columns) for _ in pieces]
+        + [pl.BlockSpec(memory_space=pl.ANY) for _ in operands],
+        out_specs=[
+            pl.BlockSpec((count, pair), columns),
+            pl.BlockSpec((count, tile), columns),
+            pl.BlockSpec((depth, pair), columns),
+            pl.BlockSpec((depth, tile), lambda n: (0, n + at * tiles)),
+        ],
+        out_shape=[
+            jax.ShapeDtypeStruct((count, tiles * pair), jnp.bfloat16),
+            jax.ShapeDtypeStruct((count, tiles * tile), jnp.bfloat16),
+            jax.ShapeDtypeStruct((depth, tiles * pair), jnp.bfloat16),
+            jax.ShapeDtypeStruct((depth, 2 * tiles * tile), jnp.bfloat16),
+        ],
+        input_output_aliases={2 + n_pieces: 3} if operands else {},
+        compiler_params=pltpu.CompilerParams(vmem_limit_bytes=56 * 2**20),
+    )(normed, cot, *pieces, *operands)
+
+
 def feed_back(cot, down_rows, pre, normed, tiles, first):
     count, depth = cot.shape
     pair = pre.shape[1] // tiles
@@ -96,9 +141,10 @@
         grad = rows_dot(cot_ref[...], down_ref[...])
         gate = pre_ref[:, :tile].astype(jnp.float32)
         up = pre_ref[:, tile:].astype(jnp.float32)
-        sigma = jax.nn.sigmoid(gate)
-        back_ref[:, :tile] = (grad * up * sigma * (1.0 + gate * (1.0 - sigma))).astype(jnp.bfloat16)
-        back_ref[:, tile:] = (grad * gate * sigma).astype(jnp.bfloat16)
+        sigma = sigmoid(gate)
+        passed = grad * sigma
+        back_ref[:, :tile] = (passed * up * (1.0 + gate * (1.0 - sigma))).astype(jnp.bfloat16)
+        back_ref[:, tile:] = (passed * gate).astype(jnp.bfloat16)
         local_ref[...] = cols_dot(normed_ref[...], back_ref[...])
 
     return kernel_call(
@@ -117,11 +163,36 @@
     )
 
 
-def shifted(values, steps):
-    count = values.shape[0]
-    at = lax.broadcasted_iota(jnp.int32, values.shape, 0) % SEQ
-    inside = (at >= steps) & (at < SEQ + steps)
-    return jnp.where(inside, pltpu.roll(values, steps % count, 0), 0.0)
+def down_local(cot, hidden, half, at):
+    count, depth = cot.shape
+    extent = hidden.shape[1]
+
+    def body(cot_ref, hidden_ref, *refs):
+        refs[-1][...] = cols_dot(cot_ref[...], hidden_ref[...])
+
+    operands = [] if half is None else [half]
+    return pl.pallas_call(
+        body,
+        grid=(1,),
+        in_specs=[
+            pl.BlockSpec((count, depth), same),
+            pl.BlockSpec((count, extent), same),
+        ]
+        + [pl.BlockSpec(memory_space=pl.ANY) for _ in operands],
+        out_specs=pl.BlockSpec((depth, extent), lambda n: (0, at)),
+        out_shape=jax.ShapeDtypeStruct((depth, 2 * extent), jnp.bfloat16),
+        input_output_aliases={2: 0} if operands else {},
+        compiler_params=pltpu.CompilerParams(vmem_limit_bytes=56 * 2**20),
+    )(cot, hidden, *operands)
+
+
+def place_in_sequence(shape):
+    return lax.rem(lax.broadcasted_iota(jnp.int32, shape, 0), SEQ)
+
+
+def shifted(values, steps, at):
+    inside = at >= steps if steps > 0 else at < SEQ + steps
+    return jnp.where(inside, pltpu.roll(values, steps % values.shape[0], 0), 0.0)
 
 
 def convolve(normed, pieces, taps, tiles):
@@ -136,9 +207,10 @@
         parts = jnp.dot(normed_ref[...], weight_ref[...], preferred_element_type=jnp.float32)
         parts_ref[...] = parts.astype(jnp.bfloat16)
         mixed = parts[:, :tile] * parts[:, 2 * tile :]
+        at = place_in_sequence(mixed.shape)
         conv = (
-            taps_ref[0:1, :] * shifted(mixed, 2)
-            + taps_ref[1:2, :] * shifted(mixed, 1)
+            taps_ref[0:1, :] * shifted(mixed, 2, at)
+            + taps_ref[1:2, :] * shifted(mixed, 1, at)
             + taps_ref[2:3, :] * mixed
         )
         gated_ref[...] = (parts[:, tile : 2 * tile] * conv).astype(jnp.bfloat16)
@@ -170,7 +242,8 @@
         c_part = parts_ref[:, tile : 2 * tile].astype(jnp.float32)
         x_part = parts_ref[:, 2 * tile :].astype(jnp.float32)
         mixed = b_part * x_part
-        before_1, before_2 = shifted(mixed, 1), shifted(mixed, 2)
+        at = place_in_sequence(mixed.shape)
+        before_1, before_2 = shifted(mixed, 1, at), shifted(mixed, 2, at)
         conv = (
             taps_ref[0:1, :] * before_2 + taps_ref[1:2, :] * before_1 + taps_ref[2:3, :] * mixed
         )
@@ -185,8 +258,8 @@
         )
         mixed_grad = (
             taps_ref[2:3, :] * conv_grad
-            + taps_ref[1:2, :] * shifted(conv_grad, -1)
-            + taps_ref[0:1, :] * shifted(conv_grad, -2)
+            + taps_ref[1:2, :] * shifted(conv_grad, -1, at)
+            + taps_ref[0:1, :] * shifted(conv_grad, -2, at)
         )
         back_ref[:, :tile] = (mixed_grad * x_part).astype(jnp.bfloat16)
         back_ref[:, tile : 2 * tile] = (gated_grad * conv).astype(jnp.bfloat16)
@@ -213,12 +286,11 @@
     )
 
 
-def norm_back(extra, backs, weights, values, inv_rms, gain, base, width):
+def norm_back(backs, weights, values, inv_rms, gain, base, width):
     count, depth = values.shape
     total = len(backs)
     per = backs[0].shape[1] // width
     rows_at_once = min(128, count)
-    operands = [] if extra is None else [extra]
 
     def at(q):
         return lambda n: (0, jnp.clip(n - q * per, 0, per - 1))
@@ -226,14 +298,12 @@
     def body(*refs):
         back_refs, weight_refs = refs[:total], refs[total : 2 * total]
         values_ref, inv_ref, gain_ref, base_ref = refs[2 * total : 2 * total + 4]
-        extra_refs = refs[2 * total + 4 : -3]
         out_ref, gain_grad_ref, sum_ref = refs[-3:]
         n = pl.program_id(0)
 
         @pl.when(n == 0)
         def _():
-            first = rows_dot(back_refs[0][...], weight_refs[0][...])
-            sum_ref[...] = first + extra_refs[0][...] if extra_refs else first
+            sum_ref[...] = rows_dot(back_refs[0][...], weight_refs[0][...])
 
         for q in range(total):
 
@@ -270,8 +340,7 @@
             pl.BlockSpec((count, 1), same),
             pl.BlockSpec((1, depth), same),
             pl.BlockSpec((count, depth), same),
-        ]
-        + [pl.BlockSpec((count, depth), same) for _ in operands],
+        ],
         out_specs=[pl.BlockSpec((count, depth), same), pl.BlockSpec((1, depth), same)],
         out_shape=[
             jax.ShapeDtypeStruct((count, depth), jnp.bfloat16),
@@ -279,7 +348,7 @@
         ],
         scratch_shapes=[pltpu.VMEM((count, depth), jnp.float32)],
         compiler_params=pltpu.CompilerParams(vmem_limit_bytes=56 * 2**20),
-    )(*backs, *weights, values, inv_rms, gain[None, :], base, *operands)
+    )(*backs, *weights, values, inv_rms, gain[None, :], base)
 
 
 def in_order(core, mine, other, quarter):
@@ -311,6 +380,28 @@
             jax.ShapeDtypeStruct((block, 12 * quarter), jnp.float32),
             jax.ShapeDtypeStruct((4 * quarter, block), jnp.float32),
         ],
+        compiler_params=pltpu.CompilerParams(vmem_limit_bytes=56 * 2**20),
+    )(core.astype(jnp.int32).reshape(1, 1), mine, other)
+
+
+def down_in_order(core, mine, other):
+    block, half = mine.shape
+
+    def body(core_ref, mine_ref, other_ref, out_ref):
+        first = core_ref[0, 0] == 0
+        mine, other = mine_ref[...].astype(jnp.float32), other_ref[...].astype(jnp.float32)
+        out_ref[:half, :] = jnp.where(first, mine, other).T
+        out_ref[half:, :] = jnp.where(first, other, mine).T
+
+    return pl.pallas_call(
+        body,
+        in_specs=[
+            pl.BlockSpec(memory_space=pltpu.SMEM),
+            pl.BlockSpec(memory_space=pltpu.VMEM),
+            pl.BlockSpec(memory_space=pltpu.VMEM),
+        ],
+        out_specs=pl.BlockSpec(memory_space=pltpu.VMEM),
+        out_shape=jax.ShapeDtypeStruct((2 * half, block), jnp.float32),
         compiler_params=pltpu.CompilerParams(vmem_limit_bytes=56 * 2**20),
     )(core.astype(jnp.int32).reshape(1, 1), mine, other)
 
@@ -395,17 +486,25 @@
         last[:] = got + jax.tree.leaves(made)
         return got, made
 
+    def cut_of(rows_of_piece):
+        return rows_of_piece // 32 * 16
+
     class Gather:
         def __init__(self, piece, flip):
             self.got = {0: piece}
-            self.n_cw = size // 2 - (1 if flip else 0)
-            self.n_ccw = size - 1 - self.n_cw
+            self.halves = flip is None
+            self.n_cw = size // 2 - (0 if flip is False else 1)
+            self.n_ccw = size - 1 - self.n_cw - (1 if self.halves else 0)
             self.step = 0
 
         def sends(self):
             self.step += 1
             self.to = []
             out = []
+            if self.halves and self.step == size // 2:
+                before, after = self.got[self.step - 1], self.got[self.step + 1]
+                cut = cut_of(before.shape[0])
+                return [(before[:cut], cw), (after[cut:], ccw)]
             if self.step <= self.n_cw:
                 out.append((self.got[self.step - 1], cw))
                 self.to.append(self.step)
@@ -415,6 +514,9 @@
             return out
 
         def take(self, got):
+            if self.halves and self.step == size // 2:
+                self.got[self.step] = jnp.concatenate(got, 0)
+                return
             for b in self.to:
                 self.got[b] = got.pop(0)
 
@@ -430,14 +532,26 @@
     class Scatter:
         def __init__(self, own, flip):
             self.own = own
-            self.n_cw = size // 2 - (1 if flip else 0)
-            self.n_ccw = size - 1 - self.n_cw
+            self.halves = flip is None
+            self.n_cw = size // 2 - (0 if flip is False else 1)
+            self.n_ccw = size - 1 - self.n_cw - (1 if self.halves else 0)
             self.step = size // 2 + 1
             self.up = self.down = None
 
         def sends(self):
             self.step -= 1
             out = []
+            if self.halves and self.step == size // 2:
+                far = total(*self.own(self.step))
+                cut = cut_of(far.shape[0])
+                return [(far[:cut], cw), (far[cut:], ccw)]
+            if self.halves and self.step == size // 2 - 1:
+                up, down = total(*self.own(size - self.step)), total(*self.own(self.step))
+                cut = cut_of(up.shape[0])
+                return [
+                    (jnp.concatenate([total(up[:cut], self.up), up[cut:]], 0), cw),
+                    (jnp.concatenate([down[:cut], total(down[cut:], self.down)], 0), ccw),
+                ]
             if self.step <= self.n_cw:
                 out.append((total(*self.own(size - self.step), self.up), cw))
             if self.step <= self.n_ccw:
@@ -445,6 +559,9 @@
             return out
 
         def take(self, got):
+            if self.halves and self.step == size // 2:
+                self.up, self.down = got
+                return
             if self.step <= self.n_cw:
                 self.up = got.pop(0)
             if self.step <= self.n_ccw:
@@ -509,7 +626,7 @@
     small = jnp.concatenate([norm_gain_one, norm_gain_two, conv_weight.reshape(-1)])
     pack = jnp.pad(small[None, :], ((0, PACK - 1), (0, 6 * dq - small.shape[0])))
     in_ring = Gather(
-        jnp.concatenate([jnp.concatenate([in_part(0, 0), in_part(0, 1)], 1), pack], 0), False
+        jnp.concatenate([jnp.concatenate([in_part(0, 0), in_part(0, 1)], 1), pack], 0), None
     )
     far_order = [b for b in order if b != 0]
 
@@ -606,48 +723,52 @@
     far_take(far)
     gu_q[0] = fed[0][2]
 
-    def down_parts(cot, *hidden):
-        return [cols_dot(h, cot) for h in hidden]
-
-    (far, gu_q[2]), (down_00,) = both_rounds(
-        [down_ring], [far_send(), (gu_q[0], to_core)], down_parts, (cot, fed[0][1])
+    def down_first(cot, hidden):
+        return down_local(cot, hidden, None, 0)
+
+    def down_second(cot, hidden, half):
+        return down_local(cot, hidden, half, 1)
+
+    (far, gu_q[2]), down_0 = both_rounds(
+        [down_ring], [far_send(), (gu_q[0], to_core)], down_first, (cot, fed[0][1])
     )
     far_take(far)
-    (far,), fed[2] = both_rounds([down_ring], [far_send()], feed_tiles, (normed_two, gu_q[2]))
+
+    def feed_both(normed, weight, cot, half, at):
+        return feed_and_down(normed, [weight], cot, half, at, tiles)
+
+    (far,), fed[2] = both_rounds(
+        [down_ring],
+        [far_send()],
+        lambda *args: feed_both(*args, None, 0),
+        (normed_two, gu_q[2], cot),
+    )
     far_take(far)
-    (far,), (down_10,) = both_rounds(
-        [down_ring], [far_send()], down_parts, (cot, fed[2][1])
-    )
+    (far,), _ = both_rounds([down_ring], [far_send()])
     far_take(far)
-
-    def column(value, b):
-        n = order.index(b)
-        return value[:, n * block : (n + 1) * block]
 
     def row(value, b):
         n = order.index(b)
         return value[n * block : (n + 1) * block]
-
-    def col_scatter(mine, other, flip):
-        return Scatter(lambda b: (column(mine, b), column(other, b)), flip)
 
     finish(down_ring)
     while len(far_pieces) < size:
         (far,), _ = ordered_round([far_send()])
         far_take(far)
     down_half = down_ring.cols()
-    (down_other, down_far), fed[1] = ordered_round(
-        [(down_half, to_core), (down_10, to_core)],
-        feed_tiles,
-        (normed_two, *[far_pieces[b] for b in order]),
+    (down_other,), fed[1] = ordered_round(
+        [(down_half, to_core)], feed_tiles, (normed_two, *[far_pieces[b] for b in order])
     )
     gu_q[1] = fed[1][2]
-    down_s0 = col_scatter(down_00, down_far, True)
     down_h = (down_half, down_other)
-    (gu_q[3],), (down_01,) = both_rounds(
-        [down_s0], [(gu_q[1], to_core)], down_parts, (cot, fed[1][1])
-    )
-    _, fed[3] = both_rounds([down_s0], (), feed_tiles, (normed_two, gu_q[3]))
+    (gu_q[3],), down_0 = ordered_round(
+        [(gu_q[1], to_core)], down_second, (cot, fed[1][1], down_0)
+    )
+
+    _, fed[3] = ordered_round(
+        [], lambda *args: feed_both(*args, 1), (normed_two, gu_q[3], cot, fed[2][3])
+    )
+    down_1 = fed[3][3]
 
     def feed_back_first(cot, down_rows, pre, normed):
         return feed_back(cot, down_rows, pre, normed, tiles, 0)
@@ -658,10 +779,13 @@
     def back_args(n):
         return (cot, down_h[n // 2], fed[n][0], normed_two)
 
-    _, (back_3, local_3) = both_rounds([down_s0], (), feed_back_second, back_args(3))
-    (gu_far_1,), (back_1, local_1) = both_rounds(
-        [down_s0], [(local_3, to_core)], feed_back_second, back_args(1)
-    )
+    (down_far,), (back_3, local_3) = ordered_round(
+        [(down_1, to_core)], feed_back_second, back_args(3)
+    )
+    (gu_far_1,), (back_1, local_1) = ordered_round(
+        [(local_3, to_core)], feed_back_second, back_args(1)
+    )
+    down_s = Scatter(lambda b: (row(down_0, b), row(down_far, b)), False)
     y_order = [size // 2]
     for step in range(size // 2 - 1, 0, -1):
         y_order += [size - step, step]
@@ -676,43 +800,53 @@
         y_got[y_order[len(y_got)]] = value
 
 
-    def down_part_and_sum(cot, h3, middle, h0, h1, weight):
-        half = middle + plain_dot(jnp.concatenate([h0, h1], 1), weight)
-        return cols_dot(h3, cot), half
-
-    (away,), (down_11, half_out) = ordered_round(
-        [y_send()], down_part_and_sum, (cot, fed[3][1], middle, fed[0][1], fed[1][1], down_half)
+    def sum_out(middle, h0, h1, w0, h2, h3, w1):
+        return (
+            middle
+            + plain_dot(jnp.concatenate([h0, h1], 1), w0)
+            + plain_dot(jnp.concatenate([h2, h3], 1), w1)
+        ).astype(bf16)
+
+    (away,), block_out = both_rounds(
+        [down_s],
+        [y_send()],
+        sum_out,
+        (middle, fed[0][1], fed[1][1], down_half, fed[2][1], fed[3][1], down_other),
     )
     y_take(away)
-    (away, down_far_1), (back_2, local_2) = ordered_round(
-        [y_send(), (down_11, to_core)], feed_back_first, back_args(2)
+    (away,), (back_2, local_2) = both_rounds(
+        [down_s], [y_send()], feed_back_first, back_args(2)
     )
     y_take(away)
-    down_s1 = col_scatter(down_01, down_far_1, False)
     (away, gu_far_0), (back_0, local_0) = both_rounds(
-        [down_s1], [y_send(), (local_2, to_core)], feed_back_first, back_args(0)
+        [down_s], [y_send(), (local_2, to_core)], feed_back_first, back_args(0)
     )
     y_take(away)
     gu_s = Scatter(lambda b: (row(local_0, b), row(gu_far_0, b), y_got[b]), False)
 
-    def through(b0, w0, b1, w1):
-        return rows_dot(b0, w0) + rows_dot(b1, w1)
-
-    (away,), grad_a = both_rounds(
-        [down_s1, gu_s], [y_send()], through, (back_1, gu_q[1], back_3, gu_q[3])
-    )
-    y_take(away)
-
-    def mid_back(grad_a, b0, w0, b1, w1, middle, inv_two, gain, cot):
-        return norm_back(grad_a, [b0, b1], [w0, w1], middle, inv_two, gain, cot, 2 * tile)
-
+    def y_send_pair():
+        at = min(order.index(y_order[len(y_got) + n]) for n in range(2))
+        both = [v[at * block : (at + 2) * block] for v in (local_1, gu_far_1)]
+        return (total(*both), to_y)
+
+    def y_take_pair(value):
+        at = min(order.index(y_order[len(y_got) + n]) for n in range(2))
+        for n in range(2):
+            y_got[order[at + n]] = value[n * block : (n + 1) * block]
+
+    def mid_back(b0, w0, b1, w1, b2, w2, b3, w3, middle, inv_two, gain, cot):
+        return norm_back(
+            [b0, b1, b2, b3], [w0, w1, w2, w3], middle, inv_two, gain, cot, 2 * tile
+        )
+
+    mid_args = [v for n, back in enumerate((back_0, back_1, back_2, back_3)) for v in (back, gu_q[n])]
     (away,), (branch_back, gain_two_local) = both_rounds(
-        [down_s1],
-        [y_send()],
+        [down_s, gu_s],
+        [y_send_pair()],
         mid_back,
-        (grad_a, back_0, gu_q[0], back_2, gu_q[2], middle, inv_two, gain_two_f, cot),
-    )
-    y_take(away)
+        (*mid_args, middle, inv_two, gain_two_f, cot),
+    )
+    y_take_pair(away)
 
     def conv_back_half(branch_back, out_rows, parts, gated, taps, normed_one):
         return convolve_back(branch_back, out_rows, parts, gated, taps, normed_one, 2)
@@ -721,14 +855,14 @@
         return (branch_back, out_h[i], parts_h[i], gated_h[i], taps_h[i], normed_one)
 
     (away,), (in_back_1, in_local_1, taps_local_1) = both_rounds(
-        [down_s1, gu_s], [y_send()], conv_back_half, conv_args(1)
+        [gu_s], [y_send()], conv_back_half, conv_args(1)
     )
     y_take(away)
     (away, in_got), (in_back_0, in_local_0, taps_local_0) = both_rounds(
         [gu_s], [y_send(), (in_local_1, to_core)], conv_back_half, conv_args(0)
     )
     y_take(away)
-    in_s = Scatter(lambda b: (row(in_local_0, b), row(in_got, b)), False)
+    in_s = Scatter(lambda b: (row(in_local_0, b), row(in_got, b)), None)
 
     def swap(flag, first, second, axis):
         return jnp.where(
@@ -746,17 +880,17 @@
             axis,
         )
 
-    finish(down_s0, down_s1)
-    down_slice = y_ordered(jnp.concatenate([down_s0.result(), down_s1.result()], 0), 0)
+    finish(down_s)
+    down_slice = y_ordered(down_s.result(), 1)
 
     def first_back(b0, w0, b1, w1, tokens_rel, inv_one, gain, branch_back):
         return norm_back(
-            None, [b0, b1], [w0, w1], tokens_rel, inv_one, gain, branch_back, 3 * dq
+            [b0, b1], [w0, w1], tokens_rel, inv_one, gain, branch_back, 3 * dq
         )
 
-    (away, down_got), (tokens_grad, gain_one_local) = both_rounds(
+    (away,), (tokens_grad, gain_one_local) = both_rounds(
         [gu_s, in_s],
-        [y_send(), (down_slice, to_y)],
+        [y_send()],
         first_back,
         (in_back_0, in_h[0], in_back_1, in_h[1], tokens_rel, inv_one, gain_one_f, branch_back),
     )
@@ -788,36 +922,26 @@
     finish(gu_s)
     gu_slice = gu_s.result()
 
-    def block_sum(half_out, h2, h3, weight):
-        return (half_out + plain_dot(jnp.concatenate([h2, h3], 1), weight)).astype(bf16)
-
     gu_slice = high_reps(gu_slice)
-    down_total = high_reps(add(down_slice, down_got))
-    def block_sum_and_small(half_out, h2, h3, weight, *small):
-        return block_sum(half_out, h2, h3, weight), small_start(*small)
-
-    (down_away, gu_other), (block_out, small_sum) = both_rounds(
+    (gu_other,), (small_sum, tokens_natural) = both_rounds(
         [in_s],
-        [(down_total, to_core), (gu_slice, to_y)],
-        block_sum_and_small,
-        (
-            half_out, fed[2][1], fed[3][1], down_other,
-            gain_one_local, gain_two_local, taps_local_0, taps_local_1,
-        ),
+        [(gu_slice, to_y)],
+        lambda values, *small: (small_start(*small), to_natural(values).astype(bf16)),
+        (tokens_grad, gain_one_local, gain_two_local, taps_local_0, taps_local_1),
     )
     gu_both = jnp.stack([gu_slice, gu_other], 0)
-    (small_got, gu_far), natural_outs = both_rounds(
+    (small_got, gu_far, down_got), block_natural = both_rounds(
         [in_s],
-        [small_send(), (gu_both, to_core)],
-        lambda *vs: [to_natural(v).astype(bf16) for v in vs],
-        (block_out, tokens_grad),
+        [small_send(), (gu_both, to_core), (down_slice, to_y)],
+        lambda v: to_natural(v).astype(bf16),
+        (block_out,),
     )
     small_sum = small_sum + small_got
 
     def core_whole(mine, other, axis):
         return swap(core, mine, other, axis).astype(f32)
 
-    def gu_out(start):
+    def gu_out(gu_both, gu_far, start):
         def of(value):
             return jnp.concatenate(
                 [value[:, (2 * t + start) * tile : (2 * t + start + 1) * tile] for t in range(tiles)], 1
@@ -827,16 +951,21 @@
         far = swap(ybit, of(gu_far[0]), of(gu_far[1]), 1)
         return core_whole(own, far, 1)
 
-    def down_gate_up(down_total, down_away):
-        return core_whole(down_total, down_away, 0), gu_out(0), gu_out(1)
-
-    (small_got,), (down_grad, gate_grad, up_grad) = both_rounds(
-        [in_s], [small_send()], down_gate_up, (down_total, down_away)
+    down_total = high_reps(add(down_slice, down_got))
+    (small_got, down_away), (gate_grad, up_grad) = both_rounds(
+        [in_s],
+        [small_send(), (down_total, to_core)],
+        lambda gu_both, gu_far: (gu_out(gu_both, gu_far, 0), gu_out(gu_both, gu_far, 1)),
+        (gu_both, gu_far),
     )
     small_sum = small_sum + small_got
     finish(in_s)
     in_slice = y_ordered(in_s.result(), 1)
-    (small_got, in_got), _ = ordered_round([small_send(), (in_slice, to_y)])
+    (small_got, in_got), down_grad = ordered_round(
+        [small_send(), (in_slice, to_y)],
+        lambda mine, other: down_in_order(core, mine, other),
+        (down_total, down_away),
+    )
     small_sum = small_sum + small_got
     in_total = high_reps(add(in_slice, in_got))
     while small_moves:
@@ -852,7 +981,8 @@
         small_sum, lax.axis_index("shard") * block, block, 1
     )
     return (
-        *natural_outs,
+        block_natural,
+        tokens_natural,
         small_total[0],
         in_grad,
         small_total[2:],

time: 531 us -> 509 us (0.959)
  Pallas kernels: 186 us -> 222 us
  matrix products: 65.6 us -> 34.1 us
  other arithmetic: 62 us -> 48.8 us
  starting transfers between devices: 87.4 us -> 79.8 us
  waiting for transfers between devices: 92.1 us -> 84.6 us
    pallas_call x0 -> x5, Pallas kernels: none -> 42.1 us  [the longest x2 25.4 us: feed_and_down(): pl.pallas_call(body, grid=(tiles,), in_specs=[pl.BlockSpec((count, depth)...]
    pallas_call x12 -> x10, Pallas kernels: 146 us -> 127 us  [kernel_call(): pl.pallas_call(body, grid=(steps,), in_specs=[pl.BlockSpec(block, where)...]
    dot_general x4 -> x0, matrix products: 18 us -> none  [cols_dot(): lax.dot_general(left, right, (((0,), (0,)), ((), ())), preferred_element_...]
    dot_general x6 -> x4, matrix products: 24 us -> 9.01 us  [rows_dot(): lax.dot_general(left, right, (((1,), (1,)), ((), ())), preferred_element_...]
    pallas_call x2, Pallas kernels: 37.3 us -> 50.4 us  [norm_back(): pl.pallas_call(body, grid=(total * per,), in_specs=[pl.BlockSpec((count,...]
    convert_element_type x23 -> x20, other arithmetic: 44.6 us -> 36.6 us  [total(): return sum((v.astype(f32) for v in values)).astype(bf16)]
    ppermute x93 -> x86, waiting for transfers between devices: 92.1 us -> 84.6 us  [send(): return lax.ppermute(value, AXES, perm)]
    ppermute x93 -> x86, starting transfers between devices: 87.4 us -> 79.8 us  [send(): return lax.ppermute(value, AXES, perm)]
  transfers between devices with their start and end apart: 93 -> 86, of which waited for: 36 -> 28; matrix products, arithmetic and copies ran while one was open for 26% -> 17% of each run, Pallas kernels for 35% -> 41%
where the time goes in v4:
time: 509 us; the launch traced here: 501 us
  Pallas kernels  222 us (44%)
  waiting for transfers between devices  84.6 us (17%)
  starting transfers between devices  79.8 us (16%)
  other arithmetic  48.8 us (10%)
  matrix products  34.1 us (7%)
  local copies, waits for them, and re-layouts  28.6 us (6%)
    pallas_call x10, Pallas kernels, kernel_call(): pl.pallas_call(body, grid=(steps,), in_specs=[pl.BlockSpec(block, where)...  127 us
    ppermute x86, waiting for transfers between devices, send(): return lax.ppermute(value, AXES, perm)  84.6 us
    ppermute x86, starting transfers between devices, send(): return lax.ppermute(value, AXES, perm)  79.8 us
    pallas_call x2, Pallas kernels, norm_back(): pl.pallas_call(body, grid=(total * per,), in_specs=[pl.BlockSpec((count,...  50.4 us
    convert_element_type x20, other arithmetic, total(): return sum((v.astype(f32) for v in values)).astype(bf16)  36.6 us
    pallas_call x2, Pallas kernels, feed_and_down(): pl.pallas_call(body, grid=(tiles,), in_specs=[pl.BlockSpec((count, depth)...  25.4 us
    dot_general x7, matrix products, plain_dot(): return jnp.dot(left, right, preferred_element_type=jnp.float32).astype(kind)  25.1 us
    unnamed x182, local copies, waits for them, and re-layouts  19.2 us
  transfers between devices with their start and end apart: 86, of which 28 were waited for; matrix products, arithmetic and copies ran while one was open for 17% of the time, Pallas kernels for 41%

profile of v4, /device:TPU:0, one launch (start us, length us, event | category | flops | bytes accessed | tf_op | source)
XLA Modules:
  0.0 500.8 jit_solution(3713672766339471600)
XLA Ops:
  25.6 6.7 %collective-permute-done.2.refs_3_ = bf16[144,1536]{1,0:T(8,128)(2,1)S(1)} collective-permute-done((bf16[144,1536]{1,0:T(8,128)(2,1)S(1)}, bf16[144,1536]{1,0:T(8,128)(2,1)S(1)}, u32[]{:S(2)}, u32[]{:S(2)}) %collective-permute-start.2) | collective-permute-done | bytes 442400 | tf_op jit(solution)/shard_map/ppermute | solution.py:456
  51.6 5.0 %collective-permute-done.11 = bf16[80,1536]{1,0:T(8,128)(2,1)S(1)} collective-permute-done((bf16[80,1536]{1,0:T(8,128)(2,1)S(1)}, bf16[80,1536]{1,0:T(8,128)(2,1)S(1)}, u32[]{:S(2)}, u32[]{:S(2)}) %collective-permute-start.11) | collective-permute-done | bytes 245792 | tf_op jit(solution)/shard_map/ppermute | solution.py:456
  64.4 8.4 %shard_map.204 = (bf16[1024,1536]{1,0:T(8,128)(2,1)}, bf16[1024,512]{1,0:T(8,128)(2,1)}, bf16[1024,1536]{1,0:T(8,128)(2,1)}) custom-call(bf16[1024,1024]{1,0:T(8,128)(2,1)} %multiply_convert_fusion.1.normed_ref, f32[3,512]{1,0:T(4,128)} %get-tuple-element.448.taps_ref, bf16[144,1536]{1,0:T(8,128)(2,1)} %copy-done.17, bf16[144,1536]{1,0:T(8,128)(2,1)} %copy-done.37, ...), custom_call_target="tpu_custom_call" | custom-call | tf_op jit(solution)/shard_map/pallas_call | solution.py:40
  82.3 7.4 %collective-permute-done.17.refs_4_ = bf16[128,2304]{1,0:T(8,128)(2,1)} collective-permute-done((bf16[128,2304]{1,0:T(8,128)(2,1)}, bf16[128,2304]{1,0:T(8,128)(2,1)}, u32[]{:S(2)}, u32[]{:S(2)}) %collective-permute-start.17) | collective-permute-done | bytes 589856 | tf_op jit(solution)/shard_map/ppermute | solution.py:456
  95.4 7.9 %shard_map.205 = (bf16[1024,1536]{1,0:T(8,128)(2,1)}, bf16[1024,512]{1,0:T(8,128)(2,1)}, bf16[1024,1536]{1,0:T(8,128)(2,1)}) custom-call(bf16[1024,1024]{1,0:T(8,128)(2,1)} %multiply_convert_fusion.1.normed_ref, f32[3,512]{1,0:T(4,128)} %get-tuple-element.438.taps_ref, bf16[1024,1536]{1,0:T(8,128)(2,1)} %collective-permute-done.19.refs_0_.refs_3_), custom_call_target="tpu_custom_call" | custom-call | tf_op jit(solution)/shard_map/pallas_call | solution.py:40
  126.5 11.0 %shard_map.206 = (bf16[1024,2304]{1,0:T(8,128)(2,1)}, bf16[1024,1152]{1,0:T(8,128)(2,1)}, bf16[1024,2304]{1,0:T(8,128)(2,1)}) custom-call(bf16[1024,1024]{1,0:T(8,128)(2,1)} %multiply_convert_fusion.normed_ref, bf16[128,2304]{1,0:T(8,128)(2,1)} %copy-done.20, bf16[128,2304]{1,0:T(8,128)(2,1)} %collective-permute-done.14.refs_1_, ...), custom_call_target="tpu_custom_call" | custom-call | tf_op jit(solution)/shard_map/pallas_call | solution.py:40
  140.9 6.7 %shard_map.207.refs_0_ = bf16[1024,2304]{1,0:T(8,128)(2,1)} custom-call(bf16[1024,1024]{1,0:T(8,128)(2,1)} %fusion.25.cot_ref.refs_11_, bf16[1024,1152]{1,0:T(8,128)(2,1)} %get-tuple-element.389.hidden_ref), custom_call_target="tpu_custom_call" | custom-call | tf_op jit(solution)/shard_map/pallas_call | solution.py:174
  148.0 5.3 %collective-permute-done.30 = bf16[2304,128]{1,0:T(8,128)(2,1)S(1)} collective-permute-done((bf16[2304,128]{1,0:T(8,128)(2,1)S(1)}, bf16[2304,128]{1,0:T(8,128)(2,1)S(1)}, u32[]{:S(2)}, u32[]{:S(2)}) %collective-permute-start.30) | collective-permute-done | bytes 589856 | tf_op jit(solution)/shard_map/ppermute | solution.py:456
  158.1 12.7 %shard_map.208 = (bf16[1024,2304]{1,0:T(8,128)(2,1)}, bf16[1024,1152]{1,0:T(8,128)(2,1)}, bf16[1024,2304]{1,0:T(8,128)(2,1)}, bf16[1024,2304]{1,0:T(8,128)(2,1)}) custom-call(bf16[1024,1024]{1,0:T(8,128)(2,1)} %multiply_convert_fusion.normed_ref, bf16[1024,1024]{1,0:T(8,128)(2,1)} %fusion.25.cot_ref.refs_11_, ...), custom_call_target="tpu_custom_call" | custom-call | tf_op jit(solution)/shard_map/pallas_call | solution.py:112
  173.3 10.2 %collective-permute-done.37 = bf16[2304,128]{1,0:T(8,128)(2,1)S(1)} collective-permute-done((bf16[2304,128]{1,0:T(8,128)(2,1)S(1)}, bf16[2304,128]{1,0:T(8,128)(2,1)S(1)}, u32[]{:S(2)}, u32[]{:S(2)}) %collective-permute-start.37) | collective-permute-done | bytes 589856 | tf_op jit(solution)/shard_map/ppermute | solution.py:456
  185.1 11.3 %shard_map.209 = (bf16[1024,2304]{1,0:T(8,128)(2,1)}, bf16[1024,1152]{1,0:T(8,128)(2,1)}, bf16[1024,2304]{1,0:T(8,128)(2,1)}) custom-call(bf16[1024,1024]{1,0:T(8,128)(2,1)} %multiply_convert_fusion.normed_ref, bf16[128,2304]{1,0:T(8,128)(2,1)} %copy-done.21, bf16[128,2304]{1,0:T(8,128)(2,1)} %copy-done.24, bf16[128,2304]{1,0:T(8,128)(2,1)} %copy-done.25, ...), custom_call_target="tpu_custom_call" | custom-call | tf_op jit(solution)/shard_map/pallas_call | solution.py:40
  196.5 6.8 %shard_map.210 = bf16[1024,2304]{1,0:T(8,128)(2,1)} custom-call(bf16[1024,1024]{1,0:T(8,128)(2,1)} %fusion.25.cot_ref.refs_11_, bf16[1024,1152]{1,0:T(8,128)(2,1)} %get-tuple-element.390.hidden_ref, bf16[1024,2304]{1,0:T(8,128)(2,1)} %shard_map.207.refs_0_), custom_call_target="tpu_custom_call", output_to_operand_aliasing={{}: (2, {})} | custom-call | tf_op jit(solution)/shard_map/pallas_call | solution.py:174
  206.7 12.7 %shard_map.211 = (bf16[1024,2304]{1,0:T(8,128)(2,1)}, bf16[1024,1152]{1,0:T(8,128)(2,1)}, bf16[1024,2304]{1,0:T(8,128)(2,1)}, bf16[1024,2304]{1,0:T(8,128)(2,1)}) custom-call(bf16[1024,1024]{1,0:T(8,128)(2,1)} %multiply_convert_fusion.normed_ref, bf16[1024,1024]{1,0:T(8,128)(2,1)} %fusion.25.cot_ref.refs_11_, ...), custom_call_target="tpu_custom_call", output_to_operand_aliasing={{3}: (3, {})} | custom-call | tf_op jit(solution)/shard_map/pallas_call | solution.py:112
  219.6 14.5 %shard_map.212 = (bf16[1024,2304]{1,0:T(8,128)(2,1)}, bf16[1024,2304]{1,0:T(8,128)(2,1)}) custom-call(bf16[1024,1024]{1,0:T(8,128)(2,1)} %fusion.25.cot_ref.refs_11_, bf16[2304,1024]{1,0:T(8,128)(2,1)} %collective-permute-done.39.down_ref, bf16[1024,2304]{1,0:T(8,128)(2,1)} %get-tuple-element.375.pre_ref, bf16[1024,1024]{1,0:T(8,128)(2,1)} %multiply_convert_fusion.normed_ref), custom_call_target="tpu_custom_call" | custom-call | tf_op jit(solution)/shard_map/pallas_call | solution.py:40
  236.7 14.9 %shard_map.213 = (bf16[1024,2304]{1,0:T(8,128)(2,1)}, bf16[1024,2304]{1,0:T(8,128)(2,1)}) custom-call(bf16[1024,1024]{1,0:T(8,128)(2,1)} %fusion.25.cot_ref.refs_11_, bf16[2304,1024]{1,0:T(8,128)(2,1)} %copy-done.5, bf16[1024,2304]{1,0:T(8,128)(2,1)} %get-tuple-element.381.pre_ref, bf16[1024,1024]{1,0:T(8,128)(2,1)} %multiply_convert_fusion.normed_ref), custom_call_target="tpu_custom_call" | custom-call | tf_op jit(solution)/shard_map/pallas_call | solution.py:40
  253.3 5.2 %add_convert_fusion.5 = (bf16[128,2304]{1,0:T(8,128)(2,1)}, bf16[128,2304]{1,0:T(8,128)(2,1)}, bf16[128,2304]{1,0:T(8,128)(2,1)}, bf16[128,2304]{1,0:T(8,128)(2,...) fusion(bf16[1024,2304]{1,0:T(8,128)(2,1)} %collective-permute-done.42, bf16[1024,2304]{1,0:T(8,128)(2,1)} %get-tuple-element.383), kind=kLoop, calls=%fused_computation.46 | loop fusion | flops 7077888 | bytes 10616832 | tf_op jit(solution)/shard_map/convert_element_type | solution.py:580
  260.8 5.1 %fusion = f32[1024,1024]{1,0:T(8,128)S(1)} fusion(bf16[2304,1024]{1,0:T(8,128)(2,1)S(1)} %bitcast.70, bf16[1024,1152]{1,0:T(8,128)(2,1)S(1)} %copy-done.14, bf16[1024,1152]{1,0:T(8,128)(2,1)S(1)} %copy-done.13), kind=kOutput, calls=%fused_computation.1 | convolution fusion | flops 4841275392 | bytes 13631488 | tf_op jit(solution)/shard_map/dot_general | solution.py:20
  265.9 8.7 %add_convert_fusion = bf16[1024,1024]{1,0:T(8,128)(2,1)} fusion(f32[1024,1024]{1,0:T(8,128)S(1)} %copy-done.4, f32[1024,1024]{1,0:T(8,128)S(1)} %fusion, bf16[2304,1024]{1,0:T(8,128)(2,1)} %collective-permute-done.39.down_ref, bf16[1024,1152]{1,0:T(8,128)(2,1)S(1)} %copy-done.54, bf16[1024,1152]{1,0:T(8,128)(2,1)S(1)} %copy-done.53), kind=kOutput, calls=%fused_computation.10 | convolution fusion | flops 4844421120 | bytes 19922944 | tf_op jit(solution)/shard_map/dot_general | solution.py:20
  279.6 14.5 %shard_map.214 = (bf16[1024,2304]{1,0:T(8,128)(2,1)}, bf16[1024,2304]{1,0:T(8,128)(2,1)}) custom-call(bf16[1024,1024]{1,0:T(8,128)(2,1)} %fusion.25.cot_ref.refs_11_, bf16[2304,1024]{1,0:T(8,128)(2,1)} %collective-permute-done.39.down_ref, bf16[1024,2304]{1,0:T(8,128)(2,1)} %get-tuple-element.399.pre_ref, bf16[1024,1024]{1,0:T(8,128)(2,1)} %multiply_convert_fusion.normed_ref), custom_call_target="tpu_custom_call" | custom-call | tf_op jit(solution)/shard_map/pallas_call | solution.py:40
  301.9 15.0 %shard_map.215 = (bf16[1024,2304]{1,0:T(8,128)(2,1)}, bf16[1024,2304]{1,0:T(8,128)(2,1)}) custom-call(bf16[1024,1024]{1,0:T(8,128)(2,1)} %fusion.25.cot_ref.refs_11_, bf16[2304,1024]{1,0:T(8,128)(2,1)} %copy-done.5, bf16[1024,2304]{1,0:T(8,128)(2,1)} %get-tuple-element.406.pre_ref, bf16[1024,1024]{1,0:T(8,128)(2,1)} %multiply_convert_fusion.normed_ref), custom_call_target="tpu_custom_call" | custom-call | tf_op jit(solution)/shard_map/pallas_call | solution.py:40
  326.7 34.4 %shard_map.216 = (bf16[1024,1024]{1,0:T(8,128)(2,1)}, f32[1,1024]{1,0:T(1,128)}) custom-call(bf16[1024,2304]{1,0:T(8,128)(2,1)} %get-tuple-element.416.refs_0_, bf16[1024,2304]{1,0:T(8,128)(2,1)} %get-tuple-element.417.refs_1_, bf16[1024,2304]{1,0:T(8,128)(2,1)} %get-tuple-element.418.refs_2_, bf16[1024,2304]{1,0:T(8,128)(2,1)} %get-tuple-element.419.refs_3_, ...), custom_call_target="tpu_custom_call" | custom-call | tf_op jit(solution)/shard_map/pallas_call | solution.py:333
  368.1 14.9 %shard_map.217 = (bf16[1024,1536]{1,0:T(8,128)(2,1)}, bf16[1024,2048]{1,0:T(8,128)(2,1)}, f32[3,512]{1,0:T(4,128)}) custom-call(bf16[1024,1024]{1,0:T(8,128)(2,1)} %get-tuple-element.469.branch_ref.refs_7_, bf16[512,1024]{1,0:T(8,128)(2,1)} %copy-done.11, bf16[1024,1536]{1,0:T(8,128)(2,1)} %get-tuple-element.436.parts_ref, ...), custom_call_target="tpu_custom_call" | custom-call | tf_op jit(solution)/shard_map/pallas_call | solution.py:40
  390.5 14.7 %shard_map.218 = (bf16[1024,1536]{1,0:T(8,128)(2,1)}, bf16[1024,2048]{1,0:T(8,128)(2,1)}, f32[3,512]{1,0:T(4,128)}) custom-call(bf16[1024,1024]{1,0:T(8,128)(2,1)} %get-tuple-element.469.branch_ref.refs_7_, bf16[512,1024]{1,0:T(8,128)(2,1)} %constant_dynamic-update-slice_fusion.20.out_ref, bf16[1024,1536]{1,0:T(8,128)(2,1)} %get-tuple-element.446.parts_ref, ...), custom_call_target="tpu_custom_call" | custom-call | tf_op jit(solution)/shard_map/pallas_call | solution.py:40
  418.4 16.0 %shard_map.219 = (bf16[1024,1024]{1,0:T(8,128)(2,1)}, f32[1,1024]{1,0:T(1,128)}) custom-call(bf16[1024,1536]{1,0:T(8,128)(2,1)} %get-tuple-element.462.refs_0_, bf16[1024,1536]{1,0:T(8,128)(2,1)} %get-tuple-element.463.refs_1_, bf16[1024,1536]{1,0:T(8,128)(2,1)} %get-tuple-element.464.refs_2_, bf16[1024,1536]{1,0:T(8,128)(2,1)} %collective-permute-done.19.refs_0_.refs_3_, ...), custom_call_target="tpu_custom_call" | custom-call | tf_op jit(solution)/shard_map/pallas_call | solution.py:333
  (457 shorter events, 228.1 us)
Async XLA Ops:
  73.5 17.8 %collective-permute-start.19 = (bf16[1024,1536]{1,0:T(8,128)(2,1)}, bf16[1024,1536]{1,0:T(8,128)(2,1)}, u32[]{:S(2)}, u32[]{:S(2)}) collective-permute-start(bf16[1024,1536]{1,0:T(8,128)(2,1)} %get-tuple-element.464.refs_2_), channel_id=1, source_target_pairs={{0,8},{1,9},{2,10},{3,11},{4,12},{5,13},{6,14},{7,15},{8,0},{9,1},... | collective-permute-start | bytes 9437192 | tf_op jit(solution)/shard_map/ppermute | solution.py:456
  73.6 17.8 %collective-permute-start.21 = (bf16[512,1024]{1,0:T(8,128)(2,1)}, bf16[512,1024]{1,0:T(8,128)(2,1)S(1)}, u32[]{:S(2)}, u32[]{:S(2)}) collective-permute-start(bf16[512,1024]{1,0:T(8,128)(2,1)} %constant_dynamic-update-slice_fusion.20.out_ref), channel_id=1, source_target_pairs={{0,8},{1,9},{2,10},{3,11},{4,12},{5,13},{6,14},{7,15},{8,0},{9,1},... | collective-permute-start | bytes 3145736 | tf_op jit(solution)/shard_map/ppermute | solution.py:456
  137.5 17.6 %collective-permute-start.32 = (bf16[1024,2304]{1,0:T(8,128)(2,1)}, bf16[1024,2304]{1,0:T(8,128)(2,1)}, u32[]{:S(2)}, u32[]{:S(2)}) collective-permute-start(bf16[1024,2304]{1,0:T(8,128)(2,1)} %get-tuple-element.420.refs_4_), channel_id=1, source_target_pairs={{0,8},{1,9},{2,10},{3,11},{4,12},{5,13},{6,14},{7,15},{8,0},{9,1},... | collective-permute-start | bytes 14155784 | tf_op jit(solution)/shard_map/ppermute | solution.py:456
  276.8 17.3 %collective-permute-start.45 = (bf16[128,2304]{1,0:T(8,128)(2,1)S(1)}, bf16[128,2304]{1,0:T(8,128)(2,1)S(1)}, u32[]{:S(2)}, u32[]{:S(2)}) collective-permute-start(bf16[128,2304]{1,0:T(8,128)(2,1)S(1)} %add_convert_fusion.22), channel_id=1, source_target_pairs={{0,1},{1,3},{2,0},{3,5},{4,2},{5,7},{6,4},{7,6},{8,9},{9,11},{10,8... | collective-permute-start | bytes 1769480 | tf_op jit(solution)/shard_map/ppermute | solution.py:456
  296.6 23.1 %collective-permute-start.48 = (bf16[1024,2304]{1,0:T(8,128)(2,1)}, bf16[1024,2304]{1,0:T(8,128)(2,1)}, u32[]{:S(2)}, u32[]{:S(2)}) collective-permute-start(bf16[1024,2304]{1,0:T(8,128)(2,1)} %get-tuple-element.409), channel_id=1, source_target_pairs={{0,8},{1,9},{2,10},{3,11},{4,12},{5,13},{6,14},{7,15},{8,0},{9,1},... | collective-permute-start | bytes 14155784 | tf_op jit(solution)/shard_map/ppermute | solution.py:456
  296.7 20.2 %collective-permute-start.49 = (bf16[128,2304]{1,0:T(8,128)(2,1)S(1)}, bf16[128,2304]{1,0:T(8,128)(2,1)S(1)}, u32[]{:S(2)}, u32[]{:S(2)}) collective-permute-start(bf16[128,2304]{1,0:T(8,128)(2,1)S(1)} %get-tuple-element.410), channel_id=1, source_target_pairs={{0,1},{1,3},{2,0},{3,5},{4,2},{5,7},{6,4},{7,6},{8,9},{9,11},{10,8... | collective-permute-start | bytes 1769480 | tf_op jit(solution)/shard_map/ppermute | solution.py:456
  297.5 20.2 %collective-permute-start.50 = (bf16[128,2304]{1,0:T(8,128)(2,1)S(1)}, bf16[128,2304]{1,0:T(8,128)(2,1)}, u32[]{:S(2)}, u32[]{:S(2)}) collective-permute-start(bf16[128,2304]{1,0:T(8,128)(2,1)S(1)} %get-tuple-element.411), channel_id=1, source_target_pairs={{0,2},{1,0},{2,4},{3,1},{4,6},{5,3},{6,7},{7,5},{8,10},{9,8},{10,1... | collective-permute-start | bytes 1769480 | tf_op jit(solution)/shard_map/ppermute | solution.py:456
  300.6 21.5 %collective-permute-start.51 = (bf16[128,2304]{1,0:T(8,128)(2,1)}, bf16[128,2304]{1,0:T(8,128)(2,1)}, u32[]{:S(2)}, u32[]{:S(2)}) collective-permute-start(bf16[128,2304]{1,0:T(8,128)(2,1)} %get-tuple-element.413), channel_id=1, source_target_pairs={{0,16},{1,17},{2,18},{3,19},{4,20},{5,21},{6,22},{7,23},{8,24},{9,... | collective-permute-start | bytes 1769480 | tf_op jit(solution)/shard_map/ppermute | solution.py:456
  322.0 39.1 %collective-permute-start.53 = (bf16[128,2304]{1,0:T(8,128)(2,1)}, bf16[128,2304]{1,0:T(8,128)(2,1)}, u32[]{:S(2)}, u32[]{:S(2)}) collective-permute-start(bf16[128,2304]{1,0:T(8,128)(2,1)} %add_convert_fusion.14), channel_id=1, source_target_pairs={{0,1},{1,3},{2,0},{3,5},{4,2},{5,7},{6,4},{7,6},{8,9},{9,11},{10,8... | collective-permute-start | bytes 1769480 | tf_op jit(solution)/shard_map/ppermute | solution.py:456
  323.2 41.3 %collective-permute-start.52 = (bf16[256,2304]{1,0:T(8,128)(2,1)S(1)}, bf16[256,2304]{1,0:T(8,128)(2,1)}, u32[]{:S(2)}, u32[]{:S(2)}) collective-permute-start(bf16[256,2304]{1,0:T(8,128)(2,1)S(1)} %add_convert_fusion.1), channel_id=1, source_target_pairs={{0,16},{1,17},{2,18},{3,19},{4,20},{5,21},{6,22},{7,23},{8,24},{9,... | collective-permute-start | bytes 3538952 | tf_op jit(solution)/shard_map/ppermute | solution.py:456
  323.6 40.8 %collective-permute-start.54 = (bf16[128,2304]{1,0:T(8,128)(2,1)S(1)}, bf16[128,2304]{1,0:T(8,128)(2,1)}, u32[]{:S(2)}, u32[]{:S(2)}) collective-permute-start(bf16[128,2304]{1,0:T(8,128)(2,1)S(1)} %get-tuple-element.429), channel_id=1, source_target_pairs={{0,1},{1,3},{2,0},{3,5},{4,2},{5,7},{6,4},{7,6},{8,9},{9,11},{10,8... | collective-permute-start | bytes 1769480 | tf_op jit(solution)/shard_map/ppermute | solution.py:456
  325.0 39.5 %collective-permute-start.55 = (bf16[128,2304]{1,0:T(8,128)(2,1)S(1)}, bf16[128,2304]{1,0:T(8,128)(2,1)}, u32[]{:S(2)}, u32[]{:S(2)}) collective-permute-start(bf16[128,2304]{1,0:T(8,128)(2,1)S(1)} %get-tuple-element.430), channel_id=1, source_target_pairs={{0,2},{1,0},{2,4},{3,1},{4,6},{5,3},{6,7},{7,5},{8,10},{9,8},{10,1... | collective-permute-start | bytes 1769480 | tf_op jit(solution)/shard_map/ppermute | solution.py:456
  364.5 18.5 %collective-permute-start.56 = (bf16[128,2304]{1,0:T(8,128)(2,1)}, bf16[128,2304]{1,0:T(8,128)(2,1)S(1)}, u32[]{:S(2)}, u32[]{:S(2)}) collective-permute-start(bf16[128,2304]{1,0:T(8,128)(2,1)} %get-tuple-element.432), channel_id=1, source_target_pairs={{0,1},{1,3},{2,0},{3,5},{4,2},{5,7},{6,4},{7,6},{8,9},{9,11},{10,8... | collective-permute-start | bytes 1769480 | tf_op jit(solution)/shard_map/ppermute | solution.py:456
  365.8 17.2 %collective-permute-start.57 = (bf16[128,2304]{1,0:T(8,128)(2,1)}, bf16[128,2304]{1,0:T(8,128)(2,1)S(1)}, u32[]{:S(2)}, u32[]{:S(2)}) collective-permute-start(bf16[128,2304]{1,0:T(8,128)(2,1)} %get-tuple-element.433), channel_id=1, source_target_pairs={{0,2},{1,0},{2,4},{3,1},{4,6},{5,3},{6,7},{7,5},{8,10},{9,8},{10,1... | collective-permute-start | bytes 1769480 | tf_op jit(solution)/shard_map/ppermute | solution.py:456
  366.5 19.5 %collective-permute-start.58 = (bf16[128,2304]{1,0:T(8,128)(2,1)}, bf16[128,2304]{1,0:T(8,128)(2,1)S(1)}, u32[]{:S(2)}, u32[]{:S(2)}) collective-permute-start(bf16[128,2304]{1,0:T(8,128)(2,1)} %get-tuple-element.441), channel_id=1, source_target_pairs={{0,16},{1,17},{2,18},{3,19},{4,20},{5,21},{6,22},{7,23},{8,24},{9,... | collective-permute-start | bytes 1769480 | tf_op jit(solution)/shard_map/ppermute | solution.py:456
  386.0 22.3 %collective-permute-start.59 = (bf16[1024,2048]{1,0:T(8,128)(2,1)}, bf16[1024,2048]{1,0:T(8,128)(2,1)}, u32[]{:S(2)}, u32[]{:S(2)}) collective-permute-start(bf16[1024,2048]{1,0:T(8,128)(2,1)} %get-tuple-element.451), channel_id=1, source_target_pairs={{0,8},{1,9},{2,10},{3,11},{4,12},{5,13},{6,14},{7,15},{8,0},{9,1},... | collective-permute-start | bytes 12582920 | tf_op jit(solution)/shard_map/ppermute | solution.py:456
  386.0 19.2 %collective-permute-start.60 = (bf16[128,2304]{1,0:T(8,128)(2,1)}, bf16[128,2304]{1,0:T(8,128)(2,1)S(1)}, u32[]{:S(2)}, u32[]{:S(2)}) collective-permute-start(bf16[128,2304]{1,0:T(8,128)(2,1)} %get-tuple-element.452), channel_id=1, source_target_pairs={{0,1},{1,3},{2,0},{3,5},{4,2},{5,7},{6,4},{7,6},{8,9},{9,11},{10,8... | collective-permute-start | bytes 1769480 | tf_op jit(solution)/shard_map/ppermute | solution.py:456
  387.4 17.9 %collective-permute-start.61 = (bf16[128,2304]{1,0:T(8,128)(2,1)}, bf16[128,2304]{1,0:T(8,128)(2,1)S(1)}, u32[]{:S(2)}, u32[]{:S(2)}) collective-permute-start(bf16[128,2304]{1,0:T(8,128)(2,1)} %get-tuple-element.453), channel_id=1, source_target_pairs={{0,16},{1,17},{2,18},{3,19},{4,20},{5,21},{6,22},{7,23},{8,24},{9,... | collective-permute-start | bytes 1769480 | tf_op jit(solution)/shard_map/ppermute | solution.py:456
  387.8 17.4 %collective-permute-start.62 = (bf16[128,2304]{1,0:T(8,128)(2,1)S(1)}, bf16[128,2304]{1,0:T(8,128)(2,1)S(1)}, u32[]{:S(2)}, u32[]{:S(2)}) collective-permute-start(bf16[128,2304]{1,0:T(8,128)(2,1)S(1)} %get-tuple-element.454), channel_id=1, source_target_pairs={{0,2},{1,0},{2,4},{3,1},{4,6},{5,3},{6,7},{7,5},{8,10},{9,8},{10,1... | collective-permute-start | bytes 1769480 | tf_op jit(solution)/shard_map/ppermute | solution.py:456
  411.6 22.9 %collective-permute-start.64 = (bf16[64,2048]{1,0:T(8,128)(2,1)}, bf16[64,2048]{1,0:T(8,128)(2,1)S(1)}, u32[]{:S(2)}, u32[]{:S(2)}) collective-permute-start(bf16[64,2048]{1,0:T(8,128)(2,1)} %get-tuple-element.458), channel_id=1, source_target_pairs={{0,2},{1,0},{2,4},{3,1},{4,6},{5,3},{6,7},{7,5},{8,10},{9,8},{10,1... | collective-permute-start | bytes 786440 | tf_op jit(solution)/shard_map/ppermute | solution.py:456
  413.9 21.6 %collective-permute-start.65 = (bf16[128,2304]{1,0:T(8,128)(2,1)}, bf16[128,2304]{1,0:T(8,128)(2,1)S(1)}, u32[]{:S(2)}, u32[]{:S(2)}) collective-permute-start(bf16[128,2304]{1,0:T(8,128)(2,1)} %get-tuple-element.459), channel_id=1, source_target_pairs={{0,16},{1,17},{2,18},{3,19},{4,20},{5,21},{6,22},{7,23},{8,24},{9,... | collective-permute-start | bytes 1769480 | tf_op jit(solution)/shard_map/ppermute | solution.py:456
  415.2 20.3 %collective-permute-start.66 = (bf16[128,2304]{1,0:T(8,128)(2,1)}, bf16[128,2304]{1,0:T(8,128)(2,1)S(1)}, u32[]{:S(2)}, u32[]{:S(2)}) collective-permute-start(bf16[128,2304]{1,0:T(8,128)(2,1)} %get-tuple-element.460), channel_id=1, source_target_pairs={{0,1},{1,3},{2,0},{3,5},{4,2},{5,7},{6,4},{7,6},{8,9},{9,11},{10,8... | collective-permute-start | bytes 1769480 | tf_op jit(solution)/shard_map/ppermute | solution.py:456
  416.3 19.2 %collective-permute-start.67 = (bf16[128,2304]{1,0:T(8,128)(2,1)S(1)}, bf16[128,2304]{1,0:T(8,128)(2,1)S(1)}, u32[]{:S(2)}, u32[]{:S(2)}) collective-permute-start(bf16[128,2304]{1,0:T(8,128)(2,1)S(1)} %get-tuple-element.461), channel_id=1, source_target_pairs={{0,2},{1,0},{2,4},{3,1},{4,6},{5,3},{6,7},{7,5},{8,10},{9,8},{10,1... | collective-permute-start | bytes 1769480 | tf_op jit(solution)/shard_map/ppermute | solution.py:456
  417.2 18.1 %collective-permute-start.63 = (bf16[64,2048]{1,0:T(8,128)(2,1)}, bf16[64,2048]{1,0:T(8,128)(2,1)S(1)}, u32[]{:S(2)}, u32[]{:S(2)}) collective-permute-start(bf16[64,2048]{1,0:T(8,128)(2,1)} %get-tuple-element.457), channel_id=1, source_target_pairs={{0,1},{1,3},{2,0},{3,5},{4,2},{5,7},{6,4},{7,6},{8,9},{9,11},{10,8... | collective-permute-start | bytes 786440 | tf_op jit(solution)/shard_map/ppermute | solution.py:456
  (128 other events, 1397.0 us)

commit v5 on v4

--- a/solution.py
+++ b/solution.py
@@ -907,14 +907,23 @@
         gains = to_natural(jnp.concatenate([gain_one_local, gain_two_local], 0))
         return jnp.concatenate([gains, conv_natural], 0)
 
-    small_moves = []
-    step = 1
+    def over_shard(*bits):
+        return [pairs(lambda r, s, bit=bit: (r, s ^ bit)) for bit in bits]
+
+    small_moves = [over_shard(1), over_shard(2, 4, 6)]
+    step = 8
     while step < size:
-        small_moves.append(pairs(lambda r, s, step=step: (r, s ^ step)))
+        small_moves.append(over_shard(step))
         step *= 2
-
-    def small_send():
-        return (small_sum, small_moves.pop(0))
+    small_moves.append([to_core, to_y, pairs(lambda r, s: (r ^ 3, s))])
+
+    def small_sends():
+        return [(small_sum, perm) for perm in small_moves.pop(0)]
+
+    def small_added(got):
+        if len(got) == 1:
+            return small_sum + got[0]
+        return (small_sum + got[0]) + (got[1] + got[2])
 
     while len(y_got) < size:
         (away,), _ = ordered_round([y_send()])
@@ -932,7 +941,7 @@
     gu_both = jnp.stack([gu_slice, gu_other], 0)
     (small_got, gu_far, down_got), block_natural = both_rounds(
         [in_s],
-        [small_send(), (gu_both, to_core), (down_slice, to_y)],
+        [*small_sends(), (gu_both, to_core), (down_slice, to_y)],
         lambda v: to_natural(v).astype(bf16),
         (block_out,),
     )
@@ -952,30 +961,28 @@
         return core_whole(own, far, 1)
 
     down_total = high_reps(add(down_slice, down_got))
-    (small_got, down_away), (gate_grad, up_grad) = both_rounds(
+    small_got, (gate_grad, up_grad) = both_rounds(
         [in_s],
-        [small_send(), (down_total, to_core)],
+        small_sends(),
         lambda gu_both, gu_far: (gu_out(gu_both, gu_far, 0), gu_out(gu_both, gu_far, 1)),
         (gu_both, gu_far),
     )
-    small_sum = small_sum + small_got
+    small_sum = small_added(small_got)
     finish(in_s)
+    while len(small_moves) > 1:
+        small_got, _ = ordered_round(small_sends())
+        small_sum = small_added(small_got)
     in_slice = y_ordered(in_s.result(), 1)
-    (small_got, in_got), down_grad = ordered_round(
-        [small_send(), (in_slice, to_y)],
+    (down_away, in_got, *small_got), _ = ordered_round(
+        [(down_total, to_core), (in_slice, to_y), *small_sends()]
+    )
+    small_sum = high_reps(small_added(small_got))
+    in_total = high_reps(add(in_slice, in_got))
+    (in_away,), down_grad = ordered_round(
+        [(in_total, to_core)],
         lambda mine, other: down_in_order(core, mine, other),
         (down_total, down_away),
     )
-    small_sum = small_sum + small_got
-    in_total = high_reps(add(in_slice, in_got))
-    while small_moves:
-        (small_got,), _ = ordered_round([small_send()])
-        small_sum = small_sum + small_got
-    to_both = pairs(lambda r, s: (r ^ 3, s))
-    (in_away, by_core, by_y, by_both), _ = ordered_round(
-        [(in_total, to_core)] + [(small_sum, perm) for perm in (to_core, to_y, to_both)]
-    )
-    small_sum = high_reps((small_sum + by_y) + (by_core + by_both))
     in_grad, out_grad = in_order(core, in_total, in_away, dq)
     small_total = lax.dynamic_slice_in_dim(
         small_sum, lax.axis_index("shard") * block, block, 1

time: 509 us -> 528 us (1.037)
  waiting for transfers between devices: 84.6 us -> 99.6 us
    ppermute x86 -> x87, waiting for transfers between devices: 84.6 us -> 99.6 us  [send(): return lax.ppermute(value, AXES, perm)]
    ppermute x86 -> x87, starting transfers between devices: 79.8 us -> 82.4 us  [send(): return lax.ppermute(value, AXES, perm)]
  transfers between devices with their start and end apart: 86 -> 87, of which waited for: 28 -> 29; matrix products, arithmetic and copies ran while one was open for 17% -> 16% of each run, Pallas kernels for 41% -> 40%
where the time goes in v5:
time: 528 us; the launch traced here: 519 us
  Pallas kernels  222 us (42%)
  waiting for transfers between devices  99.6 us (19%)
  starting transfers between devices  82.4 us (16%)
  other arithmetic  48.8 us (9%)
  matrix products  34.1 us (6%)
  local copies, waits for them, and re-layouts  29.4 us (6%)
    pallas_call x10, Pallas kernels, kernel_call(): pl.pallas_call(body, grid=(steps,), in_specs=[pl.BlockSpec(block, where)...  127 us
    ppermute x87, waiting for transfers between devices, send(): return lax.ppermute(value, AXES, perm)  99.6 us
    ppermute x87, starting transfers between devices, send(): return lax.ppermute(value, AXES, perm)  82.4 us
    pallas_call x2, Pallas kernels, norm_back(): pl.pallas_call(body, grid=(total * per,), in_specs=[pl.BlockSpec((count,...  50.3 us
    convert_element_type x20, other arithmetic, total(): return sum((v.astype(f32) for v in values)).astype(bf16)  36.6 us
    pallas_call x2, Pallas kernels, feed_and_down(): pl.pallas_call(body, grid=(tiles,), in_specs=[pl.BlockSpec((count, depth)...  25.4 us
    dot_general x7, matrix products, plain_dot(): return jnp.dot(left, right, preferred_element_type=jnp.float32).astype(kind)  25.1 us
    unnamed x182, local copies, waits for them, and re-layouts  20.1 us
  transfers between devices with their start and end apart: 87, of which 29 were waited for; matrix products, arithmetic and copies ran while one was open for 16% of the time, Pallas kernels for 40%

profile of v5, /device:TPU:0, one launch (start us, length us, event | category | flops | bytes accessed | tf_op | source)
XLA Modules:
  0.0 519.2 jit_solution(11684136062014407038)
XLA Ops:
  25.6 6.7 %collective-permute-done.2.refs_3_ = bf16[144,1536]{1,0:T(8,128)(2,1)S(1)} collective-permute-done((bf16[144,1536]{1,0:T(8,128)(2,1)S(1)}, bf16[144,1536]{1,0:T(8,128)(2,1)S(1)}, u32[]{:S(2)}, u32[]{:S(2)}) %collective-permute-start.2) | collective-permute-done | bytes 442400 | tf_op jit(solution)/shard_map/ppermute | solution.py:456
  64.4 8.4 %shard_map.204 = (bf16[1024,1536]{1,0:T(8,128)(2,1)}, bf16[1024,512]{1,0:T(8,128)(2,1)}, bf16[1024,1536]{1,0:T(8,128)(2,1)}) custom-call(bf16[1024,1024]{1,0:T(8,128)(2,1)} %multiply_convert_fusion.1.normed_ref, f32[3,512]{1,0:T(4,128)} %get-tuple-element.449.taps_ref, bf16[144,1536]{1,0:T(8,128)(2,1)} %copy-done.17, bf16[144,1536]{1,0:T(8,128)(2,1)} %copy-done.37, ...), custom_call_target="tpu_custom_call" | custom-call | tf_op jit(solution)/shard_map/pallas_call | solution.py:40
  82.4 7.4 %collective-permute-done.17.refs_4_ = bf16[128,2304]{1,0:T(8,128)(2,1)} collective-permute-done((bf16[128,2304]{1,0:T(8,128)(2,1)}, bf16[128,2304]{1,0:T(8,128)(2,1)}, u32[]{:S(2)}, u32[]{:S(2)}) %collective-permute-start.17) | collective-permute-done | bytes 589856 | tf_op jit(solution)/shard_map/ppermute | solution.py:456
  95.4 7.9 %shard_map.205 = (bf16[1024,1536]{1,0:T(8,128)(2,1)}, bf16[1024,512]{1,0:T(8,128)(2,1)}, bf16[1024,1536]{1,0:T(8,128)(2,1)}) custom-call(bf16[1024,1024]{1,0:T(8,128)(2,1)} %multiply_convert_fusion.1.normed_ref, f32[3,512]{1,0:T(4,128)} %get-tuple-element.439.taps_ref, bf16[1024,1536]{1,0:T(8,128)(2,1)} %collective-permute-done.19.refs_0_.refs_3_), custom_call_target="tpu_custom_call" | custom-call | tf_op jit(solution)/shard_map/pallas_call | solution.py:40
  126.6 11.0 %shard_map.206 = (bf16[1024,2304]{1,0:T(8,128)(2,1)}, bf16[1024,1152]{1,0:T(8,128)(2,1)}, bf16[1024,2304]{1,0:T(8,128)(2,1)}) custom-call(bf16[1024,1024]{1,0:T(8,128)(2,1)} %multiply_convert_fusion.normed_ref, bf16[128,2304]{1,0:T(8,128)(2,1)} %copy-done.20, bf16[128,2304]{1,0:T(8,128)(2,1)} %collective-permute-done.14.refs_1_, ...), custom_call_target="tpu_custom_call" | custom-call | tf_op jit(solution)/shard_map/pallas_call | solution.py:40
  141.0 6.8 %shard_map.207.refs_0_ = bf16[1024,2304]{1,0:T(8,128)(2,1)} custom-call(bf16[1024,1024]{1,0:T(8,128)(2,1)} %fusion.25.cot_ref.refs_11_, bf16[1024,1152]{1,0:T(8,128)(2,1)} %get-tuple-element.390.hidden_ref), custom_call_target="tpu_custom_call" | custom-call | tf_op jit(solution)/shard_map/pallas_call | solution.py:174
  148.2 5.3 %collective-permute-done.30 = bf16[2304,128]{1,0:T(8,128)(2,1)S(1)} collective-permute-done((bf16[2304,128]{1,0:T(8,128)(2,1)S(1)}, bf16[2304,128]{1,0:T(8,128)(2,1)S(1)}, u32[]{:S(2)}, u32[]{:S(2)}) %collective-permute-start.30) | collective-permute-done | bytes 589856 | tf_op jit(solution)/shard_map/ppermute | solution.py:456
  158.2 12.7 %shard_map.208 = (bf16[1024,2304]{1,0:T(8,128)(2,1)}, bf16[1024,1152]{1,0:T(8,128)(2,1)}, bf16[1024,2304]{1,0:T(8,128)(2,1)}, bf16[1024,2304]{1,0:T(8,128)(2,1)}) custom-call(bf16[1024,1024]{1,0:T(8,128)(2,1)} %multiply_convert_fusion.normed_ref, bf16[1024,1024]{1,0:T(8,128)(2,1)} %fusion.25.cot_ref.refs_11_, ...), custom_call_target="tpu_custom_call" | custom-call | tf_op jit(solution)/shard_map/pallas_call | solution.py:112
  173.5 10.1 %collective-permute-done.37 = bf16[2304,128]{1,0:T(8,128)(2,1)S(1)} collective-permute-done((bf16[2304,128]{1,0:T(8,128)(2,1)S(1)}, bf16[2304,128]{1,0:T(8,128)(2,1)S(1)}, u32[]{:S(2)}, u32[]{:S(2)}) %collective-permute-start.37) | collective-permute-done | bytes 589856 | tf_op jit(solution)/shard_map/ppermute | solution.py:456
  185.2 11.4 %shard_map.209 = (bf16[1024,2304]{1,0:T(8,128)(2,1)}, bf16[1024,1152]{1,0:T(8,128)(2,1)}, bf16[1024,2304]{1,0:T(8,128)(2,1)}) custom-call(bf16[1024,1024]{1,0:T(8,128)(2,1)} %multiply_convert_fusion.normed_ref, bf16[128,2304]{1,0:T(8,128)(2,1)} %copy-done.21, bf16[128,2304]{1,0:T(8,128)(2,1)} %copy-done.24, bf16[128,2304]{1,0:T(8,128)(2,1)} %copy-done.25, ...), custom_call_target="tpu_custom_call" | custom-call | tf_op jit(solution)/shard_map/pallas_call | solution.py:40
  196.7 6.7 %shard_map.210 = bf16[1024,2304]{1,0:T(8,128)(2,1)} custom-call(bf16[1024,1024]{1,0:T(8,128)(2,1)} %fusion.25.cot_ref.refs_11_, bf16[1024,1152]{1,0:T(8,128)(2,1)} %get-tuple-element.391.hidden_ref, bf16[1024,2304]{1,0:T(8,128)(2,1)} %shard_map.207.refs_0_), custom_call_target="tpu_custom_call", output_to_operand_aliasing={{}: (2, {})} | custom-call | tf_op jit(solution)/shard_map/pallas_call | solution.py:174
  206.9 12.7 %shard_map.211 = (bf16[1024,2304]{1,0:T(8,128)(2,1)}, bf16[1024,1152]{1,0:T(8,128)(2,1)}, bf16[1024,2304]{1,0:T(8,128)(2,1)}, bf16[1024,2304]{1,0:T(8,128)(2,1)}) custom-call(bf16[1024,1024]{1,0:T(8,128)(2,1)} %multiply_convert_fusion.normed_ref, bf16[1024,1024]{1,0:T(8,128)(2,1)} %fusion.25.cot_ref.refs_11_, ...), custom_call_target="tpu_custom_call", output_to_operand_aliasing={{3}: (3, {})} | custom-call | tf_op jit(solution)/shard_map/pallas_call | solution.py:112
  219.8 14.5 %shard_map.212 = (bf16[1024,2304]{1,0:T(8,128)(2,1)}, bf16[1024,2304]{1,0:T(8,128)(2,1)}) custom-call(bf16[1024,1024]{1,0:T(8,128)(2,1)} %fusion.25.cot_ref.refs_11_, bf16[2304,1024]{1,0:T(8,128)(2,1)} %collective-permute-done.39.down_ref, bf16[1024,2304]{1,0:T(8,128)(2,1)} %get-tuple-element.376.pre_ref, bf16[1024,1024]{1,0:T(8,128)(2,1)} %multiply_convert_fusion.normed_ref), custom_call_target="tpu_custom_call" | custom-call | tf_op jit(solution)/shard_map/pallas_call | solution.py:40
  236.9 14.9 %shard_map.213 = (bf16[1024,2304]{1,0:T(8,128)(2,1)}, bf16[1024,2304]{1,0:T(8,128)(2,1)}) custom-call(bf16[1024,1024]{1,0:T(8,128)(2,1)} %fusion.25.cot_ref.refs_11_, bf16[2304,1024]{1,0:T(8,128)(2,1)} %copy-done.5, bf16[1024,2304]{1,0:T(8,128)(2,1)} %get-tuple-element.382.pre_ref, bf16[1024,1024]{1,0:T(8,128)(2,1)} %multiply_convert_fusion.normed_ref), custom_call_target="tpu_custom_call" | custom-call | tf_op jit(solution)/shard_map/pallas_call | solution.py:40
  266.1 8.7 %add_convert_fusion = bf16[1024,1024]{1,0:T(8,128)(2,1)} fusion(f32[1024,1024]{1,0:T(8,128)S(1)} %copy-done.4, f32[1024,1024]{1,0:T(8,128)S(1)} %fusion, bf16[2304,1024]{1,0:T(8,128)(2,1)} %collective-permute-done.39.down_ref, bf16[1024,1152]{1,0:T(8,128)(2,1)S(1)} %copy-done.54, bf16[1024,1152]{1,0:T(8,128)(2,1)S(1)} %copy-done.53), kind=kOutput, calls=%fused_computation.10 | convolution fusion | flops 4844421120 | bytes 19922944 | tf_op jit(solution)/shard_map/dot_general | solution.py:20
  279.8 14.5 %shard_map.214 = (bf16[1024,2304]{1,0:T(8,128)(2,1)}, bf16[1024,2304]{1,0:T(8,128)(2,1)}) custom-call(bf16[1024,1024]{1,0:T(8,128)(2,1)} %fusion.25.cot_ref.refs_11_, bf16[2304,1024]{1,0:T(8,128)(2,1)} %collective-permute-done.39.down_ref, bf16[1024,2304]{1,0:T(8,128)(2,1)} %get-tuple-element.400.pre_ref, bf16[1024,1024]{1,0:T(8,128)(2,1)} %multiply_convert_fusion.normed_ref), custom_call_target="tpu_custom_call" | custom-call | tf_op jit(solution)/shard_map/pallas_call | solution.py:40
  302.1 15.0 %shard_map.215 = (bf16[1024,2304]{1,0:T(8,128)(2,1)}, bf16[1024,2304]{1,0:T(8,128)(2,1)}) custom-call(bf16[1024,1024]{1,0:T(8,128)(2,1)} %fusion.25.cot_ref.refs_11_, bf16[2304,1024]{1,0:T(8,128)(2,1)} %copy-done.5, bf16[1024,2304]{1,0:T(8,128)(2,1)} %get-tuple-element.407.pre_ref, bf16[1024,1024]{1,0:T(8,128)(2,1)} %multiply_convert_fusion.normed_ref), custom_call_target="tpu_custom_call" | custom-call | tf_op jit(solution)/shard_map/pallas_call | solution.py:40
  326.9 34.3 %shard_map.216 = (bf16[1024,1024]{1,0:T(8,128)(2,1)}, f32[1,1024]{1,0:T(1,128)}) custom-call(bf16[1024,2304]{1,0:T(8,128)(2,1)} %get-tuple-element.417.refs_0_, bf16[1024,2304]{1,0:T(8,128)(2,1)} %get-tuple-element.418.refs_1_, bf16[1024,2304]{1,0:T(8,128)(2,1)} %get-tuple-element.419.refs_2_, bf16[1024,2304]{1,0:T(8,128)(2,1)} %get-tuple-element.420.refs_3_, ...), custom_call_target="tpu_custom_call" | custom-call | tf_op jit(solution)/shard_map/pallas_call | solution.py:333
  368.1 14.9 %shard_map.217 = (bf16[1024,1536]{1,0:T(8,128)(2,1)}, bf16[1024,2048]{1,0:T(8,128)(2,1)}, f32[3,512]{1,0:T(4,128)}) custom-call(bf16[1024,1024]{1,0:T(8,128)(2,1)} %get-tuple-element.470.branch_ref.refs_7_, bf16[512,1024]{1,0:T(8,128)(2,1)} %copy-done.11, bf16[1024,1536]{1,0:T(8,128)(2,1)} %get-tuple-element.437.parts_ref, ...), custom_call_target="tpu_custom_call" | custom-call | tf_op jit(solution)/shard_map/pallas_call | solution.py:40
  390.6 14.7 %shard_map.218 = (bf16[1024,1536]{1,0:T(8,128)(2,1)}, bf16[1024,2048]{1,0:T(8,128)(2,1)}, f32[3,512]{1,0:T(4,128)}) custom-call(bf16[1024,1024]{1,0:T(8,128)(2,1)} %get-tuple-element.470.branch_ref.refs_7_, bf16[512,1024]{1,0:T(8,128)(2,1)} %constant_dynamic-update-slice_fusion.20.out_ref, bf16[1024,1536]{1,0:T(8,128)(2,1)} %get-tuple-element.447.parts_ref, ...), custom_call_target="tpu_custom_call" | custom-call | tf_op jit(solution)/shard_map/pallas_call | solution.py:40
  418.5 16.0 %shard_map.219 = (bf16[1024,1024]{1,0:T(8,128)(2,1)}, f32[1,1024]{1,0:T(1,128)}) custom-call(bf16[1024,1536]{1,0:T(8,128)(2,1)} %get-tuple-element.463.refs_0_, bf16[1024,1536]{1,0:T(8,128)(2,1)} %get-tuple-element.464.refs_1_, bf16[1024,1536]{1,0:T(8,128)(2,1)} %get-tuple-element.465.refs_2_, bf16[1024,1536]{1,0:T(8,128)(2,1)} %collective-permute-done.19.refs_0_.refs_3_, ...), custom_call_target="tpu_custom_call" | custom-call | tf_op jit(solution)/shard_map/pallas_call | solution.py:333
  466.8 8.8 %collective-permute-done.75 = bf16[128,2304]{1,0:T(8,128)(2,1)S(1)} collective-permute-done((bf16[128,2304]{1,0:T(8,128)(2,1)S(1)}, bf16[128,2304]{1,0:T(8,128)(2,1)S(1)}, u32[]{:S(2)}, u32[]{:S(2)}) %collective-permute-start.75) | collective-permute-done | bytes 589856 | tf_op jit(solution)/shard_map/ppermute | solution.py:456
  487.1 7.7 %collective-permute-done.79 = bf16[128,2048]{1,0:T(8,128)(2,1)S(1)} collective-permute-done((bf16[128,2048]{1,0:T(8,128)(2,1)S(1)}, bf16[128,2048]{1,0:T(8,128)(2,1)S(1)}, u32[]{:S(2)}, u32[]{:S(2)}) %collective-permute-start.79) | collective-permute-done | bytes 524320 | tf_op jit(solution)/shard_map/ppermute | solution.py:456
  499.8 9.8 %collective-permute-done.84 = bf16[128,2048]{1,0:T(8,128)(2,1)S(1)} collective-permute-done((bf16[128,2048]{1,0:T(8,128)(2,1)S(1)}, bf16[128,2048]{1,0:T(8,128)(2,1)S(1)}, u32[]{:S(2)}, u32[]{:S(2)}) %collective-permute-start.84) | collective-permute-done | bytes 524320 | tf_op jit(solution)/shard_map/ppermute | solution.py:456
  (458 shorter events, 235.8 us)
Async XLA Ops:
  73.6 17.8 %collective-permute-start.19 = (bf16[1024,1536]{1,0:T(8,128)(2,1)}, bf16[1024,1536]{1,0:T(8,128)(2,1)}, u32[]{:S(2)}, u32[]{:S(2)}) collective-permute-start(bf16[1024,1536]{1,0:T(8,128)(2,1)} %get-tuple-element.465.refs_2_), channel_id=1, source_target_pairs={{0,8},{1,9},{2,10},{3,11},{4,12},{5,13},{6,14},{7,15},{8,0},{9,1},... | collective-permute-start | bytes 9437192 | tf_op jit(solution)/shard_map/ppermute | solution.py:456
  73.6 17.8 %collective-permute-start.21 = (bf16[512,1024]{1,0:T(8,128)(2,1)}, bf16[512,1024]{1,0:T(8,128)(2,1)S(1)}, u32[]{:S(2)}, u32[]{:S(2)}) collective-permute-start(bf16[512,1024]{1,0:T(8,128)(2,1)} %constant_dynamic-update-slice_fusion.20.out_ref), channel_id=1, source_target_pairs={{0,8},{1,9},{2,10},{3,11},{4,12},{5,13},{6,14},{7,15},{8,0},{9,1},... | collective-permute-start | bytes 3145736 | tf_op jit(solution)/shard_map/ppermute | solution.py:456
  137.6 17.6 %collective-permute-start.32 = (bf16[1024,2304]{1,0:T(8,128)(2,1)}, bf16[1024,2304]{1,0:T(8,128)(2,1)}, u32[]{:S(2)}, u32[]{:S(2)}) collective-permute-start(bf16[1024,2304]{1,0:T(8,128)(2,1)} %get-tuple-element.421.refs_4_), channel_id=1, source_target_pairs={{0,8},{1,9},{2,10},{3,11},{4,12},{5,13},{6,14},{7,15},{8,0},{9,1},... | collective-permute-start | bytes 14155784 | tf_op jit(solution)/shard_map/ppermute | solution.py:456
  277.0 17.3 %collective-permute-start.45 = (bf16[128,2304]{1,0:T(8,128)(2,1)S(1)}, bf16[128,2304]{1,0:T(8,128)(2,1)S(1)}, u32[]{:S(2)}, u32[]{:S(2)}) collective-permute-start(bf16[128,2304]{1,0:T(8,128)(2,1)S(1)} %add_convert_fusion.22), channel_id=1, source_target_pairs={{0,1},{1,3},{2,0},{3,5},{4,2},{5,7},{6,4},{7,6},{8,9},{9,11},{10,8... | collective-permute-start | bytes 1769480 | tf_op jit(solution)/shard_map/ppermute | solution.py:456
  296.9 23.1 %collective-permute-start.48 = (bf16[1024,2304]{1,0:T(8,128)(2,1)}, bf16[1024,2304]{1,0:T(8,128)(2,1)}, u32[]{:S(2)}, u32[]{:S(2)}) collective-permute-start(bf16[1024,2304]{1,0:T(8,128)(2,1)} %get-tuple-element.410), channel_id=1, source_target_pairs={{0,8},{1,9},{2,10},{3,11},{4,12},{5,13},{6,14},{7,15},{8,0},{9,1},... | collective-permute-start | bytes 14155784 | tf_op jit(solution)/shard_map/ppermute | solution.py:456
  296.9 20.2 %collective-permute-start.49 = (bf16[128,2304]{1,0:T(8,128)(2,1)S(1)}, bf16[128,2304]{1,0:T(8,128)(2,1)S(1)}, u32[]{:S(2)}, u32[]{:S(2)}) collective-permute-start(bf16[128,2304]{1,0:T(8,128)(2,1)S(1)} %get-tuple-element.411), channel_id=1, source_target_pairs={{0,1},{1,3},{2,0},{3,5},{4,2},{5,7},{6,4},{7,6},{8,9},{9,11},{10,8... | collective-permute-start | bytes 1769480 | tf_op jit(solution)/shard_map/ppermute | solution.py:456
  297.7 20.2 %collective-permute-start.50 = (bf16[128,2304]{1,0:T(8,128)(2,1)S(1)}, bf16[128,2304]{1,0:T(8,128)(2,1)}, u32[]{:S(2)}, u32[]{:S(2)}) collective-permute-start(bf16[128,2304]{1,0:T(8,128)(2,1)S(1)} %get-tuple-element.412), channel_id=1, source_target_pairs={{0,2},{1,0},{2,4},{3,1},{4,6},{5,3},{6,7},{7,5},{8,10},{9,8},{10,1... | collective-permute-start | bytes 1769480 | tf_op jit(solution)/shard_map/ppermute | solution.py:456
  300.8 21.5 %collective-permute-start.51 = (bf16[128,2304]{1,0:T(8,128)(2,1)}, bf16[128,2304]{1,0:T(8,128)(2,1)}, u32[]{:S(2)}, u32[]{:S(2)}) collective-permute-start(bf16[128,2304]{1,0:T(8,128)(2,1)} %get-tuple-element.414), channel_id=1, source_target_pairs={{0,16},{1,17},{2,18},{3,19},{4,20},{5,21},{6,22},{7,23},{8,24},{9,... | collective-permute-start | bytes 1769480 | tf_op jit(solution)/shard_map/ppermute | solution.py:456
  322.3 38.9 %collective-permute-start.53 = (bf16[128,2304]{1,0:T(8,128)(2,1)}, bf16[128,2304]{1,0:T(8,128)(2,1)}, u32[]{:S(2)}, u32[]{:S(2)}) collective-permute-start(bf16[128,2304]{1,0:T(8,128)(2,1)} %add_convert_fusion.14), channel_id=1, source_target_pairs={{0,1},{1,3},{2,0},{3,5},{4,2},{5,7},{6,4},{7,6},{8,9},{9,11},{10,8... | collective-permute-start | bytes 1769480 | tf_op jit(solution)/shard_map/ppermute | solution.py:456
  323.3 41.2 %collective-permute-start.52 = (bf16[256,2304]{1,0:T(8,128)(2,1)S(1)}, bf16[256,2304]{1,0:T(8,128)(2,1)}, u32[]{:S(2)}, u32[]{:S(2)}) collective-permute-start(bf16[256,2304]{1,0:T(8,128)(2,1)S(1)} %add_convert_fusion.1), channel_id=1, source_target_pairs={{0,16},{1,17},{2,18},{3,19},{4,20},{5,21},{6,22},{7,23},{8,24},{9,... | collective-permute-start | bytes 3538952 | tf_op jit(solution)/shard_map/ppermute | solution.py:456
  323.8 40.7 %collective-permute-start.54 = (bf16[128,2304]{1,0:T(8,128)(2,1)S(1)}, bf16[128,2304]{1,0:T(8,128)(2,1)}, u32[]{:S(2)}, u32[]{:S(2)}) collective-permute-start(bf16[128,2304]{1,0:T(8,128)(2,1)S(1)} %get-tuple-element.430), channel_id=1, source_target_pairs={{0,1},{1,3},{2,0},{3,5},{4,2},{5,7},{6,4},{7,6},{8,9},{9,11},{10,8... | collective-permute-start | bytes 1769480 | tf_op jit(solution)/shard_map/ppermute | solution.py:456
  325.2 39.4 %collective-permute-start.55 = (bf16[128,2304]{1,0:T(8,128)(2,1)S(1)}, bf16[128,2304]{1,0:T(8,128)(2,1)}, u32[]{:S(2)}, u32[]{:S(2)}) collective-permute-start(bf16[128,2304]{1,0:T(8,128)(2,1)S(1)} %get-tuple-element.431), channel_id=1, source_target_pairs={{0,2},{1,0},{2,4},{3,1},{4,6},{5,3},{6,7},{7,5},{8,10},{9,8},{10,1... | collective-permute-start | bytes 1769480 | tf_op jit(solution)/shard_map/ppermute | solution.py:456
  364.5 18.5 %collective-permute-start.56 = (bf16[128,2304]{1,0:T(8,128)(2,1)}, bf16[128,2304]{1,0:T(8,128)(2,1)S(1)}, u32[]{:S(2)}, u32[]{:S(2)}) collective-permute-start(bf16[128,2304]{1,0:T(8,128)(2,1)} %get-tuple-element.433), channel_id=1, source_target_pairs={{0,1},{1,3},{2,0},{3,5},{4,2},{5,7},{6,4},{7,6},{8,9},{9,11},{10,8... | collective-permute-start | bytes 1769480 | tf_op jit(solution)/shard_map/ppermute | solution.py:456
  365.9 17.2 %collective-permute-start.57 = (bf16[128,2304]{1,0:T(8,128)(2,1)}, bf16[128,2304]{1,0:T(8,128)(2,1)S(1)}, u32[]{:S(2)}, u32[]{:S(2)}) collective-permute-start(bf16[128,2304]{1,0:T(8,128)(2,1)} %get-tuple-element.434), channel_id=1, source_target_pairs={{0,2},{1,0},{2,4},{3,1},{4,6},{5,3},{6,7},{7,5},{8,10},{9,8},{10,1... | collective-permute-start | bytes 1769480 | tf_op jit(solution)/shard_map/ppermute | solution.py:456
  366.6 19.5 %collective-permute-start.58 = (bf16[128,2304]{1,0:T(8,128)(2,1)}, bf16[128,2304]{1,0:T(8,128)(2,1)S(1)}, u32[]{:S(2)}, u32[]{:S(2)}) collective-permute-start(bf16[128,2304]{1,0:T(8,128)(2,1)} %get-tuple-element.442), channel_id=1, source_target_pairs={{0,16},{1,17},{2,18},{3,19},{4,20},{5,21},{6,22},{7,23},{8,24},{9,... | collective-permute-start | bytes 1769480 | tf_op jit(solution)/shard_map/ppermute | solution.py:456
  386.1 22.3 %collective-permute-start.59 = (bf16[1024,2048]{1,0:T(8,128)(2,1)}, bf16[1024,2048]{1,0:T(8,128)(2,1)}, u32[]{:S(2)}, u32[]{:S(2)}) collective-permute-start(bf16[1024,2048]{1,0:T(8,128)(2,1)} %get-tuple-element.452), channel_id=1, source_target_pairs={{0,8},{1,9},{2,10},{3,11},{4,12},{5,13},{6,14},{7,15},{8,0},{9,1},... | collective-permute-start | bytes 12582920 | tf_op jit(solution)/shard_map/ppermute | solution.py:456
  386.1 19.3 %collective-permute-start.60 = (bf16[128,2304]{1,0:T(8,128)(2,1)}, bf16[128,2304]{1,0:T(8,128)(2,1)S(1)}, u32[]{:S(2)}, u32[]{:S(2)}) collective-permute-start(bf16[128,2304]{1,0:T(8,128)(2,1)} %get-tuple-element.453), channel_id=1, source_target_pairs={{0,1},{1,3},{2,0},{3,5},{4,2},{5,7},{6,4},{7,6},{8,9},{9,11},{10,8... | collective-permute-start | bytes 1769480 | tf_op jit(solution)/shard_map/ppermute | solution.py:456
  387.4 17.9 %collective-permute-start.61 = (bf16[128,2304]{1,0:T(8,128)(2,1)}, bf16[128,2304]{1,0:T(8,128)(2,1)S(1)}, u32[]{:S(2)}, u32[]{:S(2)}) collective-permute-start(bf16[128,2304]{1,0:T(8,128)(2,1)} %get-tuple-element.454), channel_id=1, source_target_pairs={{0,16},{1,17},{2,18},{3,19},{4,20},{5,21},{6,22},{7,23},{8,24},{9,... | collective-permute-start | bytes 1769480 | tf_op jit(solution)/shard_map/ppermute | solution.py:456
  387.9 17.4 %collective-permute-start.62 = (bf16[128,2304]{1,0:T(8,128)(2,1)S(1)}, bf16[128,2304]{1,0:T(8,128)(2,1)S(1)}, u32[]{:S(2)}, u32[]{:S(2)}) collective-permute-start(bf16[128,2304]{1,0:T(8,128)(2,1)S(1)} %get-tuple-element.455), channel_id=1, source_target_pairs={{0,2},{1,0},{2,4},{3,1},{4,6},{5,3},{6,7},{7,5},{8,10},{9,8},{10,1... | collective-permute-start | bytes 1769480 | tf_op jit(solution)/shard_map/ppermute | solution.py:456
  411.6 22.8 %collective-permute-start.64 = (bf16[64,2048]{1,0:T(8,128)(2,1)}, bf16[64,2048]{1,0:T(8,128)(2,1)S(1)}, u32[]{:S(2)}, u32[]{:S(2)}) collective-permute-start(bf16[64,2048]{1,0:T(8,128)(2,1)} %get-tuple-element.459), channel_id=1, source_target_pairs={{0,2},{1,0},{2,4},{3,1},{4,6},{5,3},{6,7},{7,5},{8,10},{9,8},{10,1... | collective-permute-start | bytes 786440 | tf_op jit(solution)/shard_map/ppermute | solution.py:456
  414.0 21.6 %collective-permute-start.65 = (bf16[128,2304]{1,0:T(8,128)(2,1)}, bf16[128,2304]{1,0:T(8,128)(2,1)S(1)}, u32[]{:S(2)}, u32[]{:S(2)}) collective-permute-start(bf16[128,2304]{1,0:T(8,128)(2,1)} %get-tuple-element.460), channel_id=1, source_target_pairs={{0,16},{1,17},{2,18},{3,19},{4,20},{5,21},{6,22},{7,23},{8,24},{9,... | collective-permute-start | bytes 1769480 | tf_op jit(solution)/shard_map/ppermute | solution.py:456
  415.3 20.3 %collective-permute-start.66 = (bf16[128,2304]{1,0:T(8,128)(2,1)}, bf16[128,2304]{1,0:T(8,128)(2,1)S(1)}, u32[]{:S(2)}, u32[]{:S(2)}) collective-permute-start(bf16[128,2304]{1,0:T(8,128)(2,1)} %get-tuple-element.461), channel_id=1, source_target_pairs={{0,1},{1,3},{2,0},{3,5},{4,2},{5,7},{6,4},{7,6},{8,9},{9,11},{10,8... | collective-permute-start | bytes 1769480 | tf_op jit(solution)/shard_map/ppermute | solution.py:456
  416.3 19.3 %collective-permute-start.67 = (bf16[128,2304]{1,0:T(8,128)(2,1)S(1)}, bf16[128,2304]{1,0:T(8,128)(2,1)S(1)}, u32[]{:S(2)}, u32[]{:S(2)}) collective-permute-start(bf16[128,2304]{1,0:T(8,128)(2,1)S(1)} %get-tuple-element.462), channel_id=1, source_target_pairs={{0,2},{1,0},{2,4},{3,1},{4,6},{5,3},{6,7},{7,5},{8,10},{9,8},{10,1... | collective-permute-start | bytes 1769480 | tf_op jit(solution)/shard_map/ppermute | solution.py:456
  417.3 18.1 %collective-permute-start.63 = (bf16[64,2048]{1,0:T(8,128)(2,1)}, bf16[64,2048]{1,0:T(8,128)(2,1)S(1)}, u32[]{:S(2)}, u32[]{:S(2)}) collective-permute-start(bf16[64,2048]{1,0:T(8,128)(2,1)} %get-tuple-element.458), channel_id=1, source_target_pairs={{0,1},{1,3},{2,0},{3,5},{4,2},{5,7},{6,4},{7,6},{8,9},{9,11},{10,8... | collective-permute-start | bytes 786440 | tf_op jit(solution)/shard_map/ppermute | solution.py:456
  (129 other events, 1454.5 us)
